TPU v7x, 32 devices: a whole 2x2x4 slice. The times are simulated.
32 devices in a mesh: groups: 2 (over x), gx: 16 (over z, y, core).
Axes of the slice: x: 2, y: 2, z: 4, core: 2. Of those that a mesh axis runs over, the one named last changes fastest.
Arguments:
- charge: float32 [16, 1048576], P(None, ('groups', 'gx')), parts along dimension 1, may hold values from -6 to 6
- jitter: float32 [3, 1048576], P(None, ('groups', 'gx')), parts along dimension 1, may hold values from -1.5 to 1.5
- basis: float32 [32, 1048576], P(None, ('groups', 'gx')), parts along dimension 1, may hold values from -0.75 to 0.75
- near: int32 [16384, 16], P(('groups', 'gx')), parts along dimension 0, may hold values from 0 to 8191, as said below
- trans0: float32 [16384, 1024], P(('groups', 'gx')), parts along dimension 0, may hold values from -1 to 1
- trans1: float32 [4096, 1024], P(('groups', 'gx')), parts along dimension 0, may hold values from -1 to 1
- trans2: float32 [1024, 1024], P(('groups', 'gx')), parts along dimension 0, may hold values from -1 to 1
- trans3: float32 [256, 1024], P(('groups', 'gx')), parts along dimension 0, may hold values from -1 to 1
- prox1: float32 [4096, 96], P(('groups', 'gx')), parts along dimension 0, may hold values from -0.5 to 0.5
- prox2: float32 [1024, 96], P(('groups', 'gx')), parts along dimension 0, may hold values from -0.5 to 0.5
- prox3: float32 [256, 96], P(('groups', 'gx')), parts along dimension 0, may hold values from -0.5 to 0.5
- prox_top: float32 [64, 96], P('groups'), parts along dimension 0, may hold values from -0.5 to 0.5
- list1: int32 [4096, 3], P(('groups', 'gx')), parts along dimension 0, may hold values from 0 to 2047, as said below
- list2: int32 [1024, 3], P(('groups', 'gx')), parts along dimension 0, may hold values from 0 to 511, as said below
- list3: int32 [256, 3], P(('groups', 'gx')), parts along dimension 0, may hold values from 0 to 127, as said below
- top_of: int32 [256], P('groups'), parts along dimension 0, may hold values from 0 to 31, never falling along the last dimension, each value on 1 to 8 neighbouring positions
Outputs:
- potential: float32 [16, 1048576], P(None, ('groups', 'gx')), parts along dimension 1
There are 2 independent parts, one for each index of `groups`. A program takes and returns all parts, laid end to end along the dimension named above; each array names one. Nothing has to cross between parts.
Inputs may be any that keep to these rules, and one draw needn't show every extreme that they name: `near`: row g starts with g itself; its other entries are distinct leaves at distances 1 to 16 from g. `list1`: row c holds 3 distinct level-1 clusters at distances 2 to 4 from c. `list2`: row c holds 3 distinct level-2 clusters at distances 2 to 4 from c. `list3`: row c holds 3 distinct level-3 clusters at distances 2 to 4 from c. `top_of`: never falls; every top cluster owns 1 to 8 consecutive level-3 clusters, and some top cluster exactly 8.
All inputs are finite; a program needn't handle non-finite values.
Results may differ from a plain program's by a relative error of at most 0.0003.
Values sent between devices are 32-bit elements; how exact they have to be, the bound alone decides.
No kernel may reach another device: no remote copies, remote signals or barrier semaphores. Data moves between devices by JAX's collectives and lax.ppermute only.
A program may use at most 192 MiB of HBM per device.

v0:
```python
import jax
import jax.numpy as jnp
from jax import lax
from jax.sharding import PartitionSpec as P

LEAF = 64
K = 32
R = 16
NREACH = 16
REACH = 4


inv_four_pi = 0.07957747154594767
soft_square = 0.01
row_columns = 64
highest = lax.Precision.HIGHEST


def padded(block, sides, width):
    for axis, dim in sides:
        count = lax.axis_size(axis)
        forward = [(i, i + 1) for i in range(count - 1)]
        backward = [(target, source) for source, target in forward]
        low = lax.ppermute(
            lax.slice_in_dim(block, block.shape[dim] - width, None, axis=dim), axis, forward
        )
        high = lax.ppermute(lax.slice_in_dim(block, 0, width, axis=dim), axis, backward)
        block = jnp.concatenate([low, block, high], axis=dim)
    return block


def green(targets, sources):
    square = None
    for axis_id in range(3):
        spread = targets[..., axis_id, :, None] - sources[..., axis_id, None, :]
        square = spread * spread if square is None else square + spread * spread
    return inv_four_pi * lax.rsqrt(square + soft_square)


def cluster_centre(cluster_ids, level_width):
    first_column = cluster_ids * level_width
    row_number = first_column // row_columns
    row_offset = first_column % row_columns
    middle = row_offset.astype(jnp.float32) + 0.5 * (level_width - 1)
    flipped = row_columns - 1 - middle
    across = jnp.where(row_number % 2 == 0, middle, flipped)
    beside = 4.0 * row_number.astype(jnp.float32) + 1.5
    return (across, beside)


def panel_points(jitter, first_leaf):
    panel_count = jitter.shape[1]
    leaf_ids = first_leaf + jnp.arange(panel_count, dtype=jnp.int32) // LEAF
    across, beside = cluster_centre(leaf_ids // 4, 1)
    beside = beside - 1.5 + (leaf_ids % 4).astype(jnp.float32)
    return jnp.stack([across, beside, jnp.zeros_like(across)]) + jitter


def proxy_points(offsets, level, first_cluster):
    cluster_count = offsets.shape[0]
    level_width = 4 ** (level - 1)
    cluster_ids = first_cluster + jnp.arange(cluster_count, dtype=jnp.int32)
    across, beside = cluster_centre(cluster_ids, level_width)
    centre = jnp.stack([across, beside, jnp.zeros_like(across)], axis=1)
    extent = jnp.array([float(level_width), 4.0, 1.0], jnp.float32)
    return centre[:, :, None] + extent[None, :, None] * offsets.reshape(cluster_count, 3, -1)


def leaf_moments(basis, charge):
    leaf_count = basis.shape[1] // LEAF
    shaped_basis = basis.reshape(basis.shape[0], leaf_count, LEAF)
    shaped_charge = charge.reshape(charge.shape[0], leaf_count, LEAF)
    return jnp.einsum("klp,rlp->lkr", shaped_basis, shaped_charge, precision=highest)


def lift(trans, moments):
    return jnp.einsum("cab,cbr->car", trans.reshape(-1, K, K), moments, precision=highest)


def upward(trans, moments):
    return lift(trans, moments).reshape(-1, 4, K, R).sum(axis=1)


def descend(trans, parent_local):
    return jnp.einsum("cab,car->cbr", trans.reshape(-1, K, K), parent_local, precision=highest)


def couple(targets, sources, moments):
    return jnp.einsum(
        "cjab,cjbr->car", green(targets[:, None], sources), moments, precision=highest
    )


def near_potential(source_points, source_charge, near_ids, target_points, group):
    leaf_count = near_ids.shape[0]
    block_count = leaf_count // group
    shaped_points = source_points.reshape(3, -1, LEAF)
    shaped_charge = source_charge.reshape(source_charge.shape[0], -1, LEAF)
    target_blocks = target_points.reshape(3, block_count, group, LEAF).transpose(1, 0, 2, 3)
    id_blocks = near_ids.reshape(block_count, group, near_ids.shape[1])

    def block_term(inputs):
        target_block, id_block = inputs
        source_place = jnp.take(shaped_points, id_block, axis=1)
        source_values = jnp.take(shaped_charge, id_block, axis=1)
        square = None
        for axis_id in range(3):
            spread = target_block[axis_id][:, :, None, None] - source_place[axis_id][:, None, :, :]
            square = spread * spread if square is None else square + spread * spread
        kernel = inv_four_pi * lax.rsqrt(square + soft_square)
        return jnp.einsum("gpjq,rgjq->rgp", kernel, source_values, precision=highest)

    blocks = lax.map(block_term, (target_blocks, id_blocks))
    return blocks.transpose(1, 0, 2, 3).reshape(source_charge.shape[0], leaf_count * LEAF)


def far_potential(basis, local_leaf):
    leaf_count = local_leaf.shape[0]
    shaped = basis.reshape(K, leaf_count, LEAF)
    return jnp.einsum("klp,lkr->rlp", shaped, local_leaf, precision=highest).reshape(
        R, leaf_count * LEAF
    )


def make_payload(moments, places):
    cluster_count = moments.shape[0]
    return jnp.concatenate(
        [moments.reshape(cluster_count, K * R), places.reshape(cluster_count, 3 * K)], axis=1
    )


def couple_level(extended, payload, partners, first_cluster):
    cluster_count = payload.shape[0]
    row_ids = partners - (first_cluster - REACH)
    picked = extended[row_ids]
    moments = picked[..., : K * R].reshape(cluster_count, partners.shape[1], K, R)
    sources = picked[..., K * R :].reshape(cluster_count, partners.shape[1], 3, K)
    targets = payload[:, K * R :].reshape(cluster_count, 3, K)
    return couple(targets, sources, moments)


def body(
    charge,
    jitter,
    basis,
    near,
    trans0,
    trans1,
    trans2,
    trans3,
    prox1,
    prox2,
    prox3,
    prox_top,
    list1,
    list2,
    list3,
    top_of,
):
    here = lax.axis_index("gx")
    leaf_count = near.shape[0]
    count_one = prox1.shape[0]
    count_two = prox2.shape[0]
    count_three = prox3.shape[0]
    points = panel_points(jitter, here * leaf_count)
    bundle = jnp.concatenate([points, charge], axis=0)
    widened = padded(bundle, (("gx", 1),), NREACH * LEAF)
    coef0 = leaf_moments(basis, charge)
    coef1 = upward(trans0, coef0)
    coef2 = upward(trans1, coef1)
    coef3 = upward(trans2, coef2)
    lifted_flat = lift(trans3, coef3).reshape(count_three, K * R)
    payload_one = make_payload(coef1, proxy_points(prox1, 1, here * count_one))
    payload_two = make_payload(coef2, proxy_points(prox2, 2, here * count_two))
    payload_three = make_payload(coef3, proxy_points(prox3, 3, here * count_three))
    extended_one = padded(payload_one, (("gx", 0),), REACH)
    extended_two = padded(payload_two, (("gx", 0),), REACH)
    extended_three = padded(payload_three, (("gx", 0),), REACH)
    top_count = prox_top.shape[0]
    top_ids = jnp.arange(top_count, dtype=jnp.int32)
    my_tops = lax.dynamic_slice_in_dim(top_of, here * count_three, count_three)
    place_top = proxy_points(prox_top, 4, 0)
    member = (my_tops[:, None] == top_ids[None, :]).astype(jnp.float32)
    terms = jnp.einsum("ct,cq->tq", member, lifted_flat, precision=highest)
    coef_top = lax.psum(terms, "gx")
    separated = (jnp.abs(my_tops[:, None] - top_ids[None, :]) >= 2).astype(jnp.float32)
    kernel_top = (
        green(place_top[my_tops][:, None], place_top[None, :]) * separated[:, :, None, None]
    )
    local_top = jnp.einsum(
        "cuab,ubr->car", kernel_top, coef_top.reshape(top_count, K, R), precision=highest
    )
    local3 = couple_level(extended_three, payload_three, list3, here * count_three) + descend(
        trans3, local_top
    )
    local2 = couple_level(extended_two, payload_two, list2, here * count_two) + descend(
        trans2, jnp.repeat(local3, 4, axis=0)
    )
    local1 = couple_level(extended_one, payload_one, list1, here * count_one) + descend(
        trans1, jnp.repeat(local2, 4, axis=0)
    )
    local_leaf = descend(trans0, jnp.repeat(local1, 4, axis=0))
    far_field = far_potential(basis, local_leaf)
    near_ids = near - (here * leaf_count - NREACH)
    near_field = near_potential(widened[:3], widened[3:], near_ids, points, 64)
    return near_field + far_field


def solution(mesh):
    placed = (
        P(None, ("groups", "gx")),
        P(None, ("groups", "gx")),
        P(None, ("groups", "gx")),
        P(("groups", "gx"), None),
        P(("groups", "gx"), None),
        P(("groups", "gx"), None),
        P(("groups", "gx"), None),
        P(("groups", "gx"), None),
        P(("groups", "gx"), None),
        P(("groups", "gx"), None),
        P(("groups", "gx"), None),
        P("groups", None),
        P(("groups", "gx"), None),
        P(("groups", "gx"), None),
        P(("groups", "gx"), None),
        P("groups"),
    )
    return jax.shard_map(
        body, mesh=mesh, in_specs=placed, out_specs=P(None, ("groups", "gx")), check_vma=False
    )
```

profile of v0, /device:TPU:8, one launch (start us, length us, event | category | flops | bytes accessed | tf_op | source)
XLA Modules:
  0.0 784.9 jit_solution(18432889938067355060)
XLA Ops:
  8.6 7.5 reshape.1006
  16.2 3.0 reshape.1007
  19.2 2.9 copy.152
  22.1 8.4 %copy.153 = f32[512,32,32]{2,1,0:T(8,128)} copy(f32[512,32,32]{0,2,1:T(8,128)} %bitcast.195) | data formatting | bytes 4194304 | tf_op jit(solution)/shard_map/reshape | solution.py:85
  30.7 2.8 copy.168
  34.5 24.9 %fusion.39 = f32[512,32,16]{1,2,0:T(8,128)S(1)} fusion(f32[32,512,64]{2,1,0:T(8,128)} %reshape.1006, f32[16,512,64]{2,1,0:T(8,128)} %reshape.1007), kind=kOutput, calls=%fused_computation.46 | convolution fusion | flops 201326592 | bytes 7340032 | tf_op jit(solution)/shard_map/klp,rlp->lkr/dot_general | solution.py:73
  59.4 15.9 %bitcast_reduce_fusion = f32[128,32,16]{1,2,0:T(8,128)S(1)} fusion(f32[512,32,16]{1,2,0:T(8,128)S(1)} %fusion.39, f32[512,32,32]{2,1,0:T(8,128)} %copy.153), kind=kOutput, calls=%fused_computation.60 | convolution fusion | flops 100859904 | bytes 3407872 | tf_op jit(solution)/shard_map/cab,cbr->car/dot_general | solution.py:77
  75.4 3.4 bitcast_reduce_fusion.1
  82.7 1.9 collective-permute-start.6
  84.7 4.5 collective-permute-start.7
  90.7 1.8 convolution_bitcast_fusion.3
  92.6 1.6 copy.189
  97.5 1.8 copy.191
  104.4 1.9 collective-permute-start.4
  106.4 4.5 collective-permute-start.5
  113.9 2.3 collective-permute-start.2
  129.8 2.5 compare_select_fusion.4
  138.8 4.5 collective-permute-start.3
  143.3 1.9 collective-permute-start
  146.0 4.5 collective-permute-start.1
  154.3 2.4 gather_fusion.2
  156.8 2.5 reshape.1051
  159.3 2.4 slice.207
  168.2 2.5 copy.178
  173.4 2.4 copy.164
  175.9 3.2 copy.165
  179.1 3.8 fusion.102
  183.1 10.9 %fusion.97 = f32[128,32,16]{1,2,0:T(8,128)} fusion(f32[128,3,32,16]{2,3,1,0:T(8,128)S(1)} %copy-done.6, f32[128,3,32]{2,1,0:T(4,128)S(1)} %copy-done.15, f32[128,32]{1,0:T(8,128)S(1)} %copy-done.23, f32[128,3,32]{2,1,0:T(4,128)S(1)} %copy-done.14, f32[128,32]{1,0:T(8,128)S(1)} %copy-done.22, f32[128,3,32]{2,1,0:T(4,128)S(1)} %copy-done.13, ...), kind=kOutput, calls=%fused_computation.104 | convolution fusion | flops 79429632 | bytes 1245184 | tf_op jit(solution)/shard_map/cjab,cjbr->car/dot_general | solution.py:89
  195.1 10.6 %fusion.105 = f32[8,32,16]{1,2,0:T(8,128)S(1)} fusion(f32[8,32]{1,0:T(8,128)S(1)} %fusion.149, f32[32,32]{1,0:T(8,128)} %bitcast.217, f32[8,32]{1,0:T(8,128)} %bitcast.226, f32[32,32]{1,0:T(8,128)} %bitcast.218, f32[8,32]{1,0:T(8,128)} %bitcast.227, f32[32,32]{1,0:T(8,128)} %bitcast.216, f32[8,32]{1,0:T(8,128)S(1)} %bitcast.225, ...), kind=kOutput, calls=%fused_computation.110 | convolution fusion | flops 52953088 | bytes 98304 | tf_op jit(solution)/shard_map/cuab,ubr->car/dot_general | solution.py:190
  207.3 2.1 fusion.100
  209.7 8.9 %fusion.175 = f32[512,16,32]{2,1,0:T(8,128)S(1)} fusion(f32[512,32,16]{1,2,0:T(8,128)S(1)} %bitcast.191, f32[512,32,32]{2,1,0:T(8,128)S(1)} %bitcast.190), kind=kOutput, calls=%fused_computation.289 | convolution fusion | flops 100663296 | bytes 4194304 | tf_op jit(solution)/shard_map/cab,car->cbr/dot_general | solution.py:85
  218.6 13.1 %fusion.74 = f32[16,512,64]{2,0,1:T(8,128)S(1)} fusion(f32[512,16,32]{2,1,0:T(8,128)S(1)} %fusion.175, f32[32,512,64]{2,1,0:T(8,128)S(1)} %bitcast.188), kind=kOutput, calls=%fused_computation.83 | convolution fusion | flops 201326592 | bytes 7340032 | tf_op jit(solution)/shard_map/klp,lkr->rlp/dot_general | solution.py:120
  231.8 3.3 copy.195
  235.0 3.9 reshape.1033
  241.7 4.6 reshape.1001
  246.3 7.1 copy.145
  255.3 509.9 %while.10 = (s32[]{:T(128)}, f32[8,16,64,64]{3,1,2,0:T(8,128)}, s32[8,64,16]{2,1,0:T(8,128)}, f32[16,544,64]{2,0,1:T(8,128)}, f32[8,3,64,64]{3,2,0,1:T(8,128)}, /*index=5*/f32[3,544,64]{2,0,1:T(4,128)S(1)}, s32[]{:T(128)}) while((s32[]{:T(128)}, f32[8,16,64,64]{3,1,2,0:T(8,128)}, s32[8,64,16]{2,1,0:T(8,128)}, f32[16,544,64]{2,0,1:T(8,128)}, ...), condition=%wide.region_1.2_spmd, body=%wide.region_0.1_spmd.sunk | while | flops 848504832 | bytes 23092824 | solution.py:113
  256.1 3.6 gather_fusion
  263.0 12.0 %gather_fusion.1 = f32[1024,16,64]{2,1,0:T(8,128)} fusion(f32[16,544,64]{2,0,1:T(8,128)} %get-tuple-element.186, s32[1024]{0:T(1024)S(1)} %broadcast_clamp_fusion.2), kind=kCustom, calls=%fused_computation.clone.1 | custom fusion | bytes 8392704 | tf_op jit(solution)/shard_map/while/body/eval_jaxpr/jit(_take)/gather | solution.py:105
  276.0 43.1 %fusion.204 = f32[8,16,64,64]{3,1,2,0:T(8,128)} fusion(f32[8,16,64,64]{3,1,2,0:T(8,128)} %get-tuple-element.177, s32[]{:T(128)} %get-tuple-element.176, f32[64,16,64]{2,1,0:T(8,128)S(1)} %bitcast.193, f32[64,64]{1,0:T(8,128)S(1)} %get-tuple-element.164, f32[64,16,64]{2,1,0:T(8,128)S(1)} %bitcast.194, f32[64,64]{1,0:T(8,128)S(1)} %get-tuple-element.166, ...), kind=kOutput, calls=%fused_computation.32.clone.1 | convolution fusion | flops 848297984 | bytes 9750016 | tf_op jit(solution)/shard_map/while/body/eval_jaxpr/gpjq,rgjq->rgp/dot_general | solution.py:111
  319.9 3.6 gather_fusion
  326.7 12.0 %gather_fusion.1 = f32[1024,16,64]{2,1,0:T(8,128)} fusion(f32[16,544,64]{2,0,1:T(8,128)} %get-tuple-element.186, s32[1024]{0:T(1024)S(1)} %broadcast_clamp_fusion.2), kind=kCustom, calls=%fused_computation.clone.1 | custom fusion | bytes 8392704 | tf_op jit(solution)/shard_map/while/body/eval_jaxpr/jit(_take)/gather | solution.py:105
  339.7 43.1 %fusion.204 = f32[8,16,64,64]{3,1,2,0:T(8,128)} fusion(f32[8,16,64,64]{3,1,2,0:T(8,128)} %get-tuple-element.177, s32[]{:T(128)} %get-tuple-element.176, f32[64,16,64]{2,1,0:T(8,128)S(1)} %bitcast.193, f32[64,64]{1,0:T(8,128)S(1)} %get-tuple-element.164, f32[64,16,64]{2,1,0:T(8,128)S(1)} %bitcast.194, f32[64,64]{1,0:T(8,128)S(1)} %get-tuple-element.166, ...), kind=kOutput, calls=%fused_computation.32.clone.1 | convolution fusion | flops 848297984 | bytes 9750016 | tf_op jit(solution)/shard_map/while/body/eval_jaxpr/gpjq,rgjq->rgp/dot_general | solution.py:111
  383.6 3.6 gather_fusion
  390.5 12.0 %gather_fusion.1 = f32[1024,16,64]{2,1,0:T(8,128)} fusion(f32[16,544,64]{2,0,1:T(8,128)} %get-tuple-element.186, s32[1024]{0:T(1024)S(1)} %broadcast_clamp_fusion.2), kind=kCustom, calls=%fused_computation.clone.1 | custom fusion | bytes 8392704 | tf_op jit(solution)/shard_map/while/body/eval_jaxpr/jit(_take)/gather | solution.py:105
  403.4 43.1 %fusion.204 = f32[8,16,64,64]{3,1,2,0:T(8,128)} fusion(f32[8,16,64,64]{3,1,2,0:T(8,128)} %get-tuple-element.177, s32[]{:T(128)} %get-tuple-element.176, f32[64,16,64]{2,1,0:T(8,128)S(1)} %bitcast.193, f32[64,64]{1,0:T(8,128)S(1)} %get-tuple-element.164, f32[64,16,64]{2,1,0:T(8,128)S(1)} %bitcast.194, f32[64,64]{1,0:T(8,128)S(1)} %get-tuple-element.166, ...), kind=kOutput, calls=%fused_computation.32.clone.1 | convolution fusion | flops 848297984 | bytes 9750016 | tf_op jit(solution)/shard_map/while/body/eval_jaxpr/gpjq,rgjq->rgp/dot_general | solution.py:111
  447.4 3.6 gather_fusion
  454.2 12.0 %gather_fusion.1 = f32[1024,16,64]{2,1,0:T(8,128)} fusion(f32[16,544,64]{2,0,1:T(8,128)} %get-tuple-element.186, s32[1024]{0:T(1024)S(1)} %broadcast_clamp_fusion.2), kind=kCustom, calls=%fused_computation.clone.1 | custom fusion | bytes 8392704 | tf_op jit(solution)/shard_map/while/body/eval_jaxpr/jit(_take)/gather | solution.py:105
  467.2 43.1 %fusion.204 = f32[8,16,64,64]{3,1,2,0:T(8,128)} fusion(f32[8,16,64,64]{3,1,2,0:T(8,128)} %get-tuple-element.177, s32[]{:T(128)} %get-tuple-element.176, f32[64,16,64]{2,1,0:T(8,128)S(1)} %bitcast.193, f32[64,64]{1,0:T(8,128)S(1)} %get-tuple-element.164, f32[64,16,64]{2,1,0:T(8,128)S(1)} %bitcast.194, f32[64,64]{1,0:T(8,128)S(1)} %get-tuple-element.166, ...), kind=kOutput, calls=%fused_computation.32.clone.1 | convolution fusion | flops 848297984 | bytes 9750016 | tf_op jit(solution)/shard_map/while/body/eval_jaxpr/gpjq,rgjq->rgp/dot_general | solution.py:111
  511.1 3.6 gather_fusion
  518.0 12.0 %gather_fusion.1 = f32[1024,16,64]{2,1,0:T(8,128)} fusion(f32[16,544,64]{2,0,1:T(8,128)} %get-tuple-element.186, s32[1024]{0:T(1024)S(1)} %broadcast_clamp_fusion.2), kind=kCustom, calls=%fused_computation.clone.1 | custom fusion | bytes 8392704 | tf_op jit(solution)/shard_map/while/body/eval_jaxpr/jit(_take)/gather | solution.py:105
  530.9 43.1 %fusion.204 = f32[8,16,64,64]{3,1,2,0:T(8,128)} fusion(f32[8,16,64,64]{3,1,2,0:T(8,128)} %get-tuple-element.177, s32[]{:T(128)} %get-tuple-element.176, f32[64,16,64]{2,1,0:T(8,128)S(1)} %bitcast.193, f32[64,64]{1,0:T(8,128)S(1)} %get-tuple-element.164, f32[64,16,64]{2,1,0:T(8,128)S(1)} %bitcast.194, f32[64,64]{1,0:T(8,128)S(1)} %get-tuple-element.166, ...), kind=kOutput, calls=%fused_computation.32.clone.1 | convolution fusion | flops 848297984 | bytes 9750016 | tf_op jit(solution)/shard_map/while/body/eval_jaxpr/gpjq,rgjq->rgp/dot_general | solution.py:111
  574.8 3.6 gather_fusion
  581.7 12.0 %gather_fusion.1 = f32[1024,16,64]{2,1,0:T(8,128)} fusion(f32[16,544,64]{2,0,1:T(8,128)} %get-tuple-element.186, s32[1024]{0:T(1024)S(1)} %broadcast_clamp_fusion.2), kind=kCustom, calls=%fused_computation.clone.1 | custom fusion | bytes 8392704 | tf_op jit(solution)/shard_map/while/body/eval_jaxpr/jit(_take)/gather | solution.py:105
  594.6 43.1 %fusion.204 = f32[8,16,64,64]{3,1,2,0:T(8,128)} fusion(f32[8,16,64,64]{3,1,2,0:T(8,128)} %get-tuple-element.177, s32[]{:T(128)} %get-tuple-element.176, f32[64,16,64]{2,1,0:T(8,128)S(1)} %bitcast.193, f32[64,64]{1,0:T(8,128)S(1)} %get-tuple-element.164, f32[64,16,64]{2,1,0:T(8,128)S(1)} %bitcast.194, f32[64,64]{1,0:T(8,128)S(1)} %get-tuple-element.166, ...), kind=kOutput, calls=%fused_computation.32.clone.1 | convolution fusion | flops 848297984 | bytes 9750016 | tf_op jit(solution)/shard_map/while/body/eval_jaxpr/gpjq,rgjq->rgp/dot_general | solution.py:111
  638.6 3.6 gather_fusion
  645.4 12.0 %gather_fusion.1 = f32[1024,16,64]{2,1,0:T(8,128)} fusion(f32[16,544,64]{2,0,1:T(8,128)} %get-tuple-element.186, s32[1024]{0:T(1024)S(1)} %broadcast_clamp_fusion.2), kind=kCustom, calls=%fused_computation.clone.1 | custom fusion | bytes 8392704 | tf_op jit(solution)/shard_map/while/body/eval_jaxpr/jit(_take)/gather | solution.py:105
  658.4 43.1 %fusion.204 = f32[8,16,64,64]{3,1,2,0:T(8,128)} fusion(f32[8,16,64,64]{3,1,2,0:T(8,128)} %get-tuple-element.177, s32[]{:T(128)} %get-tuple-element.176, f32[64,16,64]{2,1,0:T(8,128)S(1)} %bitcast.193, f32[64,64]{1,0:T(8,128)S(1)} %get-tuple-element.164, f32[64,16,64]{2,1,0:T(8,128)S(1)} %bitcast.194, f32[64,64]{1,0:T(8,128)S(1)} %get-tuple-element.166, ...), kind=kOutput, calls=%fused_computation.32.clone.1 | convolution fusion | flops 848297984 | bytes 9750016 | tf_op jit(solution)/shard_map/while/body/eval_jaxpr/gpjq,rgjq->rgp/dot_general | solution.py:111
  702.3 3.6 gather_fusion
  709.1 12.0 %gather_fusion.1 = f32[1024,16,64]{2,1,0:T(8,128)} fusion(f32[16,544,64]{2,0,1:T(8,128)} %get-tuple-element.186, s32[1024]{0:T(1024)S(1)} %broadcast_clamp_fusion.2), kind=kCustom, calls=%fused_computation.clone.1 | custom fusion | bytes 8392704 | tf_op jit(solution)/shard_map/while/body/eval_jaxpr/jit(_take)/gather | solution.py:105
  722.1 43.1 %fusion.204 = f32[8,16,64,64]{3,1,2,0:T(8,128)} fusion(f32[8,16,64,64]{3,1,2,0:T(8,128)} %get-tuple-element.177, s32[]{:T(128)} %get-tuple-element.176, f32[64,16,64]{2,1,0:T(8,128)S(1)} %bitcast.193, f32[64,64]{1,0:T(8,128)S(1)} %get-tuple-element.164, f32[64,16,64]{2,1,0:T(8,128)S(1)} %bitcast.194, f32[64,64]{1,0:T(8,128)S(1)} %get-tuple-element.166, ...), kind=kOutput, calls=%fused_computation.32.clone.1 | convolution fusion | flops 848297984 | bytes 9750016 | tf_op jit(solution)/shard_map/while/body/eval_jaxpr/gpjq,rgjq->rgp/dot_general | solution.py:111
  765.2 5.5 copy.148
  770.7 4.0 reshape.1004
  774.7 3.1 add.662
  (278 shorter events, 101.6 us)
Async XLA Ops:
  6.5 188.5 %all-reduce.2.cloned.1.call-start = ((), (), s32[]{:S(2)}) async-start(), calls=%async_computation | async-start | bytes 524288 | tf_op jit(solution)/shard_map/psum | solution.py:185
  6.6 0.5 copy-start.31
  8.6 7.6 copy-start
  22.1 8.4 %copy-start.9 = (f32[128,1024]{1,0:T(8,128)S(1)}, f32[128,1024]{1,0:T(8,128)}, u32[]{:S(2)}) copy-start(f32[128,1024]{1,0:T(8,128)} %param.27) | copy-start | bytes 1572868
  22.1 11.4 %copy-start.20 = (f32[32,1024]{1,0:T(8,128)S(1)}, f32[32,1024]{1,0:T(8,128)}, u32[]{:S(2)}) copy-start(f32[32,1024]{1,0:T(8,128)} %param.28) | copy-start | bytes 393220
  59.4 16.0 %copy-start.1 = (f32[128,32,32]{2,1,0:T(8,128)S(1)}, f32[128,32,32]{2,1,0:T(8,128)}, u32[]{:S(2)}) copy-start(f32[128,32,32]{2,1,0:T(8,128)} %copy.168) | copy-start | bytes 1572868
  59.4 19.4 %copy-start.4 = (f32[32,32,32]{2,1,0:T(8,128)S(1)}, f32[32,32,32]{2,1,0:T(8,128)}, u32[]{:S(2)}) copy-start(f32[32,32,32]{2,1,0:T(8,128)} %reshape.1020) | copy-start | bytes 393220
  75.3 6.1 copy-start.25
  75.4 37.6 %copy-start.16 = (f32[128,96]{0,1:T(8,128)S(1)}, f32[128,96]{0,1:T(8,128)}, u32[]{:S(2)}) copy-start(f32[128,96]{0,1:T(8,128)} %param.30) | copy-start | bytes 147460
  81.5 20.6 %copy-start.17 = (f32[8,512]{1,0:T(8,128)}, f32[8,512]{1,0:T(8,128)S(1)}, u32[]{:S(2)}) copy-start(f32[8,512]{1,0:T(8,128)S(1)} %reshape.1022) | copy-start | bytes 49156
  82.7 63.3 %collective-permute-start.6 = (f32[4,608]{1,0:T(4,128)}, f32[4,608]{1,0:T(4,128)}, u32[]{:S(2)}, u32[]{:S(2)}) collective-permute-start(f32[4,608]{1,0:T(4,128)} %get-tuple-element.100), channel_id=1, source_target_pairs={{0,1},{1,2},{2,3},{3,4},{4,5},{5,6},{6,7},{7,8},{8,9},{9,10},{10,1... | collective-permute-start | bytes 29192 | tf_op jit(solution)/shard_map/ppermute | solution.py:24
  84.7 65.9 %collective-permute-start.7 = (f32[4,608]{1,0:T(4,128)}, f32[4,608]{1,0:T(4,128)}, u32[]{:S(2)}, u32[]{:S(2)}) collective-permute-start(f32[4,608]{1,0:T(4,128)} %get-tuple-element.101), channel_id=1, source_target_pairs={{1,0},{2,1},{3,2},{4,3},{5,4},{6,5},{7,6},{8,7},{9,8},{10,9},{11,1... | collective-permute-start | bytes 29192 | tf_op jit(solution)/shard_map/ppermute | solution.py:27
  96.4 5.6 copy-start.32
  101.0 9.9 %copy-start.19 = (f32[32,3]{1,0:T(8,128)}, f32[32,3]{1,0:T(8,128)S(1)}, u32[]{:S(2)}) copy-start(f32[32,3]{1,0:T(8,128)S(1)} %copy.166) | copy-start | bytes 1156
  104.4 34.4 %collective-permute-start.4 = (f32[4,608]{1,0:T(4,128)}, f32[4,608]{1,0:T(4,128)}, u32[]{:S(2)}, u32[]{:S(2)}) collective-permute-start(f32[4,608]{1,0:T(4,128)} %get-tuple-element.86), channel_id=1, source_target_pairs={{0,1},{1,2},{2,3},{3,4},{4,5},{5,6},{6,7},{7,8},{8,9},{9,10},{10,1... | collective-permute-start | bytes 29192 | tf_op jit(solution)/shard_map/ppermute | solution.py:24
  106.4 37.0 %collective-permute-start.5 = (f32[4,608]{1,0:T(4,128)}, f32[4,608]{1,0:T(4,128)}, u32[]{:S(2)}, u32[]{:S(2)}) collective-permute-start(f32[4,608]{1,0:T(4,128)} %get-tuple-element.87), channel_id=1, source_target_pairs={{1,0},{2,1},{3,2},{4,3},{5,4},{6,5},{7,6},{8,7},{9,8},{10,9},{11,1... | collective-permute-start | bytes 29192 | tf_op jit(solution)/shard_map/ppermute | solution.py:27
  111.4 23.0 %copy-start.24 = (s32[512,16]{0,1:T(8,128)S(1)}, s32[512,16]{0,1:T(8,128)}, u32[]{:S(2)}) copy-start(s32[512,16]{0,1:T(8,128)} %param.25) | copy-start | bytes 98308
  113.3 37.3 %copy-start.18 = (f32[8,512]{1,0:T(8,128)S(1)}, f32[8,512]{1,0:T(8,128)}, u32[]{:S(2)}) copy-start(f32[8,512]{1,0:T(8,128)} %copy-done.17) | copy-start | bytes 49156
  113.9 39.7 %collective-permute-start.2 = (f32[4,608]{1,0:T(4,128)}, f32[4,608]{1,0:T(4,128)}, u32[]{:S(2)}, u32[]{:S(2)}) collective-permute-start(f32[4,608]{1,0:T(4,128)} %get-tuple-element.78), channel_id=1, source_target_pairs={{0,1},{1,2},{2,3},{3,4},{4,5},{5,6},{6,7},{7,8},{8,9},{9,10},{10,1... | collective-permute-start | bytes 29192 | tf_op jit(solution)/shard_map/ppermute | solution.py:24
  138.8 14.8 %collective-permute-start.3 = (f32[4,608]{1,0:T(4,128)S(1)}, f32[4,608]{1,0:T(4,128)S(1)}, u32[]{:S(2)}, u32[]{:S(2)}) collective-permute-start(f32[4,608]{1,0:T(4,128)S(1)} %get-tuple-element.79), channel_id=1, source_target_pairs={{1,0},{2,1},{3,2},{4,3},{5,4},{6,5},{7,6},{8,7},{9,8},{10,9},{11,1... | collective-permute-start | bytes 29192 | tf_op jit(solution)/shard_map/ppermute | solution.py:27
  143.3 95.6 %collective-permute-start = (f32[19,1024]{1,0:T(8,128)}, f32[19,1024]{1,0:T(8,128)S(1)}, u32[]{:S(2)}, u32[]{:S(2)}) collective-permute-start(f32[19,1024]{1,0:T(8,128)} %get-tuple-element.76), channel_id=1, source_target_pairs={{0,1},{1,2},{2,3},{3,4},{4,5},{5,6},{6,7},{7,8},{8,9},{9,10},{10,1... | collective-permute-start | bytes 233480 | tf_op jit(solution)/shard_map/ppermute | solution.py:24
  146.0 92.9 %collective-permute-start.1 = (f32[19,1024]{1,0:T(8,128)}, f32[19,1024]{1,0:T(8,128)}, u32[]{:S(2)}, u32[]{:S(2)}) collective-permute-start(f32[19,1024]{1,0:T(8,128)} %get-tuple-element.77), channel_id=1, source_target_pairs={{1,0},{2,1},{3,2},{4,3},{5,4},{6,5},{7,6},{8,7},{9,8},{10,9},{11,1... | collective-permute-start | bytes 233480 | tf_op jit(solution)/shard_map/ppermute | solution.py:27
  156.8 7.2 slice-start.5
  156.8 10.2 %slice-start.6 = ((f32[32,3,608]{2,1,0:T(4,128)}), f32[32,3,512]{2,1,0:T(4,128)S(1)}, s32[]{:S(2)}) async-start(f32[32,3,608]{2,1,0:T(4,128)} %reshape.1059), calls=%async_computation.7 | async-start | bytes 524288 | tf_op jit(solution)/shard_map/slice | solution.py:136
  159.3 11.4 %slice-start.4 = ((f32[128,3,608]{2,1,0:T(4,128)}), f32[128,3,96]{2,1,0:T(4,128)S(1)}, s32[]{:S(2)}) async-start(f32[128,3,608]{2,1,0:T(4,128)} %reshape.1051), calls=%async_computation.5 | async-start | bytes 524288 | tf_op jit(solution)/shard_map/slice | solution.py:137
  168.2 10.9 %copy-start.28 = (f32[32,1,1,32]{3,2,0,1:T(1,128)S(1)}, f32[32,1,1,32]{3,2,0,1:T(1,128)}, u32[]{:S(2)}) copy-start(f32[32,1,1,32]{3,2,0,1:T(1,128)} %get-tuple-element.91) | copy-start | bytes 12292
  168.2 10.9 %copy-start.29 = (f32[32,1,1,32]{3,2,0,1:T(1,128)S(1)}, f32[32,1,1,32]{3,2,0,1:T(1,128)}, u32[]{:S(2)}) copy-start(f32[32,1,1,32]{3,2,0,1:T(1,128)} %get-tuple-element.92) | copy-start | bytes 12292
  168.2 10.9 %copy-start.30 = (f32[32,1,1,32]{3,2,0,1:T(1,128)S(1)}, f32[32,1,1,32]{3,2,0,1:T(1,128)}, u32[]{:S(2)}) copy-start(f32[32,1,1,32]{3,2,0,1:T(1,128)} %get-tuple-element.93) | copy-start | bytes 12292
  175.8 7.1 copy-start.21
  175.8 7.1 copy-start.22
  179.1 3.9 copy-start.6
  179.1 3.9 copy-start.13
  179.1 3.9 copy-start.14
  179.1 4.0 copy-start.15
  179.1 4.0 copy-start.23
  183.1 10.9 %copy-start.12 = (f32[8,3,32,16]{3,2,1,0:T(8,128)S(1)}, f32[8,3,32,16]{3,2,1,0:T(8,128)}, u32[]{:S(2)}) copy-start(f32[8,3,32,16]{3,2,1,0:T(8,128)} %reshape.1097) | copy-start | bytes 147460
  183.1 10.9 %copy-start.26 = (f32[8,3,32]{2,1,0:T(4,128)S(1)}, f32[8,3,32]{2,1,0:T(4,128)}, u32[]{:S(2)}) copy-start(f32[8,3,32]{2,1,0:T(4,128)} %copy.183) | copy-start | bytes 9220
  183.1 10.9 %copy-start.27 = (f32[8,3,32]{2,1,0:T(4,128)S(1)}, f32[8,3,32]{2,1,0:T(4,128)}, u32[]{:S(2)}) copy-start(f32[8,3,32]{2,1,0:T(4,128)} %copy.184) | copy-start | bytes 9220
  183.1 10.9 %copy-start.33 = (f32[8,1,1,32]{3,2,0,1:T(1,128)S(1)}, f32[8,1,1,32]{3,2,0,1:T(1,128)}, u32[]{:S(2)}) copy-start(f32[8,1,1,32]{3,2,0,1:T(1,128)} %get-tuple-element.106) | copy-start | bytes 3076
  183.1 10.9 %copy-start.34 = (f32[8,1,1,32]{3,2,0,1:T(1,128)S(1)}, f32[8,1,1,32]{3,2,0,1:T(1,128)}, u32[]{:S(2)}) copy-start(f32[8,1,1,32]{3,2,0,1:T(1,128)} %get-tuple-element.107) | copy-start | bytes 3076
  195.0 10.7 %copy-start.7 = (f32[8,32,32]{2,1,0:T(8,128)S(1)}, f32[8,32,32]{2,1,0:T(8,128)}, u32[]{:S(2)}) copy-start(f32[8,32,32]{2,1,0:T(8,128)} %reshape.1027) | copy-start | bytes 98308
  195.0 10.9 %copy-start.5 = (f32[32,32,32]{2,1,0:T(8,128)S(1)}, f32[32,32,32]{2,1,0:T(8,128)}, u32[]{:S(2)}) copy-start(f32[32,32,32]{2,1,0:T(8,128)} %reshape.1020) | copy-start | bytes 393220
  195.0 11.6 %copy-start.8 = (f32[128,32,16]{1,2,0:T(8,128)S(1)}, f32[128,32,16]{1,2,0:T(8,128)}, u32[]{:S(2)}) copy-start(f32[128,32,16]{1,2,0:T(8,128)} %fusion.97) | copy-start | bytes 786436
  195.0 14.6 %slice-start.2 = ((s8[8388608]{0:T(1024)(128)(4,1)}), s8[4194304]{0:T(1024)(128)(4,1)S(1)}, s32[]{:S(2)}) async-start(s8[8388608]{0:T(1024)(128)(4,1)} %bitcast.189), calls=%async_computation.3 | async-start | bytes 8388608
  205.7 1.6 copy-start.2
  205.9 3.8 slice-start.3
  209.3 9.3 %slice-start = ((s8[8388608]{0:T(1024)(128)(4,1)}), s8[4194304]{0:T(1024)(128)(4,1)S(1)}, s32[]{:S(2)}) async-start(s8[8388608]{0:T(1024)(128)(4,1)} %bitcast.187), calls=%async_computation.1 | async-start | bytes 8388608
  209.7 8.9 %slice-start.1 = ((s8[8388608]{0:T(1024)(128)(4,1)}), s8[4194304]{0:T(1024)(128)(4,1)S(1)}, s32[]{:S(2)}) async-start(s8[8388608]{0:T(1024)(128)(4,1)} %bitcast.187), calls=%async_computation.2 | async-start | bytes 8388608
  238.9 2.8 copy-start.10
  246.3 7.1 copy-start.11
  770.7 4.0 copy-start.3
Sparse Core Ops, SparseCore 0:
  99.5 90.5 all-reduce.1
where the time goes:
time: 792 us; the launch traced here: 785 us
  matrix products  444 us (56%)
  local copies, waits for them, and re-layouts  251 us (32%)
  other arithmetic  48.8 us (6%)
  starting transfers between devices  26.2 us (3%)
  between operations  14.5 us (2%)
    dot_general x8, matrix products, block_term(): jnp.einsum('gpjq,rgjq->rgp', kernel, source_values, precision=highest)  345 us
    gather x8, local copies, waits for them, and re-layouts, block_term(): source_values = jnp.take(shaped_charge, id_block, axis=1)  96.4 us
    gather x8, local copies, waits for them, and re-layouts, block_term(): source_place = jnp.take(shaped_points, id_block, axis=1)  28.5 us
    dot_general x1, matrix products, leaf_moments(): jnp.einsum('klp,rlp->lkr', shaped_basis, shaped_charge, precision=highest)  24.9 us
    dot_general x4, matrix products, lift(): jnp.einsum('cab,cbr->car', trans.reshape(-1, K, K), moments, precision=hi...  22.1 us
    ppermute x4, starting transfers between devices, padded(): lax.ppermute(lax.slice_in_dim(block, 0, width, axis=dim), axis, backward)  18.2 us
  transfers between devices with their start and end apart: 9, of which 0 were waited for; matrix products, arithmetic and copies ran while one was open for 16% of the time, Pallas kernels for 0%

commit v1 on v0

--- a/solution.py
+++ b/solution.py
@@ -1,6 +1,8 @@
 import jax
 import jax.numpy as jnp
 from jax import lax
+from jax.experimental import pallas as pl
+from jax.experimental.pallas import tpu as pltpu
 from jax.sharding import PartitionSpec as P
 
 LEAF = 64
@@ -29,6 +31,16 @@
     return block
 
 
+def leaf_halos(points, charge):
+    count = lax.axis_size("gx")
+    forward = [(i, i + 1) for i in range(count - 1)]
+    backward = [(target, source) for source, target in forward]
+    width = NREACH * LEAF
+    last = jnp.concatenate([points[:, -width:], charge[:, -width:]], axis=0)
+    first = jnp.concatenate([points[:, :width], charge[:, :width]], axis=0)
+    return lax.ppermute(last, "gx", forward), lax.ppermute(first, "gx", backward)
+
+
 def green(targets, sources):
     square = None
     for axis_id in range(3):
@@ -91,27 +103,170 @@
     )
 
 
-def near_potential(source_points, source_charge, near_ids, target_points, group):
-    leaf_count = near_ids.shape[0]
-    block_count = leaf_count // group
-    shaped_points = source_points.reshape(3, -1, LEAF)
-    shaped_charge = source_charge.reshape(source_charge.shape[0], -1, LEAF)
-    target_blocks = target_points.reshape(3, block_count, group, LEAF).transpose(1, 0, 2, 3)
-    id_blocks = near_ids.reshape(block_count, group, near_ids.shape[1])
-
-    def block_term(inputs):
-        target_block, id_block = inputs
-        source_place = jnp.take(shaped_points, id_block, axis=1)
-        source_values = jnp.take(shaped_charge, id_block, axis=1)
-        square = None
-        for axis_id in range(3):
-            spread = target_block[axis_id][:, :, None, None] - source_place[axis_id][:, None, :, :]
-            square = spread * spread if square is None else square + spread * spread
-        kernel = inv_four_pi * lax.rsqrt(square + soft_square)
-        return jnp.einsum("gpjq,rgjq->rgp", kernel, source_values, precision=highest)
-
-    blocks = lax.map(block_term, (target_blocks, id_blocks))
-    return blocks.transpose(1, 0, 2, 3).reshape(source_charge.shape[0], leaf_count * LEAF)
+GROUP = 16
+BATCH = 8
+bf16 = jnp.bfloat16
+f32 = jnp.float32
+
+
+def split_two(value):
+    high = value.astype(bf16)
+    return high, (value - high.astype(f32)).astype(bf16)
+
+
+def split_three(value):
+    first = value.astype(bf16).astype(f32)
+    rest = value - first
+    second = rest.astype(bf16).astype(f32)
+    return first, second, rest - second
+
+
+def lanes_of(tile):
+    return pl.ds(pl.multiple_of(tile * 128, 128), 128)
+
+
+def near_kernel(
+    ids, origin, own_points, own_charge, low_halo, high_halo, out, points, feats, charges, targets, kernels, weights
+):
+    halo_tiles = low_halo.shape[1] // 128
+    own_tiles = own_points.shape[1] // 128
+    left_half = lax.broadcasted_iota(jnp.int32, (32, 128), 1).astype(bf16) < 64
+    row = lax.broadcasted_iota(jnp.int32, (8, 128), 0)
+    is_three = row == 3
+    is_four = row == 4
+    below_five = row < 5
+    one_three = jnp.where(is_three, 1.0, 0.0)
+    one_four = jnp.where(is_four, 1.0, 0.0)
+
+    def stage(tile, place, charge):
+        points[:, lanes_of(tile)] = jnp.concatenate([place, jnp.zeros((5, 128), f32)], 0)
+        charge = charge * inv_four_pi
+        charges[2 * tile] = jnp.concatenate(split_two(charge), 0)
+        charges[2 * tile + 1] = jnp.concatenate(split_two(pltpu.roll(charge, 64, 1)), 0)
+
+    def stage_halo(halo, first):
+        def step(i, carry):
+            stage(first + i, halo[0:3, lanes_of(i)], halo[3:19, lanes_of(i)])
+            return carry
+
+        lax.fori_loop(0, halo_tiles, step, 0, unroll=2)
+
+    def stage_own(i, carry):
+        stage(halo_tiles + i, own_points[:, lanes_of(i)], own_charge[:, lanes_of(i)])
+        return carry
+
+    stage_halo(low_halo, 0)
+    stage_halo(high_halo, halo_tiles + own_tiles)
+    lax.fori_loop(0, own_tiles, stage_own, 0, unroll=4)
+
+    def back(slot):
+        total = lax.dot_general(
+            kernels[slot], weights[slot], (((1,), (1,)), ((), ())), preferred_element_type=f32
+        )
+        total = jnp.transpose(total[:LEAF] + total[LEAF:])
+        return total[:R] + total[R:]
+
+    def emit(first):
+        parts = [back(slot) for slot in range(BATCH)]
+        first = jnp.maximum(first, 0)
+        for half in range(BATCH // 2):
+            place = pl.ds(pl.multiple_of((first + 2 * half) * LEAF, 128), 128)
+            out[:, place] = jnp.concatenate([parts[2 * half], parts[2 * half + 1]], 1)
+
+    def do_group(group, carry):
+        base = group * GROUP
+        shift = jnp.where(row == 0, origin[2 * group], jnp.where(row == 1, origin[2 * group + 1], 0.0))
+
+        def local(tile):
+            place = points[:, lanes_of(tile)] - shift
+            square = place * place
+            return place, jnp.broadcast_to(square[0:1] + square[1:2] + square[2:3], (8, 128))
+
+        def source_rows(i, carry):
+            place, square = local(base // 2 + i)
+            rows = place * (-2.0) + jnp.where(is_three, square + soft_square, one_four)
+
+            def put(entry, value):
+                first, second, third = split_three(value)
+                one = jnp.where(below_five, first, pltpu.roll(second, 5, 0))
+                two = jnp.where(is_three, second, one)
+                three = jnp.where(below_five, third + one_four, pltpu.roll(first, 5, 0))
+                feats[entry] = jnp.concatenate([one, two, three, jnp.zeros_like(one)], 0).astype(bf16)
+
+            put(2 * i, rows)
+            put(2 * i + 1, pltpu.roll(rows, 64, 1))
+            return carry
+
+        def target_rows(i, carry):
+            place, square = local(base // 2 + NREACH // 2 + i)
+            first, second, third = split_three(place + jnp.where(is_four, square, one_three))
+            one = jnp.where(below_five, first, pltpu.roll(first, 5, 0))
+            two = jnp.where(below_five, second + one_three, pltpu.roll(second, 5, 0))
+            three = jnp.where(below_five, jnp.where(is_four, third, first), pltpu.roll(third, 5, 0))
+            rows = jnp.concatenate([one, two, three, jnp.zeros_like(one)], 0)
+            targets[lanes_of(i), :] = jnp.transpose(rows).astype(bf16)
+            return carry
+
+        lax.fori_loop(0, (GROUP + 2 * NREACH) // 2, source_rows, 0, unroll=True)
+        lax.fori_loop(0, GROUP // 2, target_rows, 0, unroll=True)
+
+        def front(leaf, slot):
+            target = targets[pl.ds(pl.multiple_of(leaf * LEAF, LEAF), LEAF), :]
+            entry = (base + leaf) * 16
+            for j in range(4):
+                sides = []
+                for h in range(2):
+                    one = ids[entry + 4 * j + 2 * h]
+                    two = ids[entry + 4 * j + 2 * h + 1] ^ 1
+                    sides.append(jnp.where(left_half, feats[one - base], feats[two - base]))
+                    weights[slot, :, (2 * j + h) * 128 : (2 * j + h + 1) * 128] = jnp.where(
+                        left_half, charges[one], charges[two]
+                    )
+                square = jnp.dot(target, jnp.concatenate(sides, 1), preferred_element_type=f32)
+                high, low = split_two(lax.rsqrt(square))
+                kernels[slot, 0:LEAF, j * 256 : (j + 1) * 256] = high
+                kernels[slot, LEAF : 2 * LEAF, j * 256 : (j + 1) * 256] = low
+
+        def step(i, carry):
+            emit(base + BATCH * i - BATCH)
+            for slot in range(BATCH):
+                front(BATCH * i + slot, slot)
+            return carry
+
+        lax.fori_loop(0, GROUP // BATCH, step, 0)
+        return carry
+
+    kernels[...] = jnp.zeros_like(kernels)
+    weights[...] = jnp.zeros_like(weights)
+    lax.fori_loop(0, own_tiles * 2 // GROUP, do_group, 0)
+    emit(own_tiles * 2 - BATCH)
+
+
+def near_potential(ids, origin, own_points, own_charge, low_halo, high_halo):
+    panels = own_points.shape[1]
+    leaves = (panels + 2 * low_halo.shape[1]) // LEAF
+    pairs = panels * 16 * LEAF
+    vmem = pl.BlockSpec(memory_space=pltpu.VMEM)
+    smem = pl.BlockSpec(memory_space=pltpu.SMEM)
+    return pl.pallas_call(
+        near_kernel,
+        out_shape=jax.ShapeDtypeStruct((R, panels), f32),
+        in_specs=[smem, smem, vmem, vmem, vmem, vmem],
+        out_specs=vmem,
+        scratch_shapes=[
+            pltpu.VMEM((8, leaves * LEAF), f32),
+            pltpu.VMEM((GROUP + 2 * NREACH, 32, 128), bf16),
+            pltpu.VMEM((leaves, 2 * R, 128), bf16),
+            pltpu.VMEM((GROUP * LEAF, 32), bf16),
+            pltpu.VMEM((BATCH, 2 * LEAF, 16 * LEAF), bf16),
+            pltpu.VMEM((BATCH, 2 * R, 16 * LEAF), bf16),
+        ],
+        compiler_params=pltpu.CompilerParams(vmem_limit_bytes=40 * 2**20),
+        cost_estimate=pl.CostEstimate(
+            flops=pairs * 192, bytes_accessed=panels * 160, transcendentals=pairs
+        ),
+        name="near_potential",
+    )(ids, origin, own_points, own_charge, low_halo, high_halo)
 
 
 def far_potential(basis, local_leaf):
@@ -163,8 +318,7 @@
     count_two = prox2.shape[0]
     count_three = prox3.shape[0]
     points = panel_points(jitter, here * leaf_count)
-    bundle = jnp.concatenate([points, charge], axis=0)
-    widened = padded(bundle, (("gx", 1),), NREACH * LEAF)
+    low_halo, high_halo = leaf_halos(points, charge)
     coef0 = leaf_moments(basis, charge)
     coef1 = upward(trans0, coef0)
     coef2 = upward(trans1, coef1)
@@ -201,8 +355,11 @@
     )
     local_leaf = descend(trans0, jnp.repeat(local1, 4, axis=0))
     far_field = far_potential(basis, local_leaf)
-    near_ids = near - (here * leaf_count - NREACH)
-    near_field = near_potential(widened[:3], widened[3:], near_ids, points, 64)
+    near_ids = (near - (here * leaf_count - NREACH)).reshape(-1)
+    group_count = leaf_count // GROUP
+    group_ids = here * group_count + jnp.arange(group_count, dtype=jnp.int32)
+    origin = jnp.stack(cluster_centre(group_ids, GROUP // 4), axis=1).reshape(-1)
+    near_field = near_potential(near_ids, origin, points, charge, low_halo, high_halo)
     return near_field + far_field
 
 

time: 792 us -> 348 us (0.44)
  matrix products: 444 us -> 99.3 us
  local copies, waits for them, and re-layouts: 251 us -> 89.6 us
  Pallas kernels: 0 us -> 86.4 us
  other arithmetic: 48.8 us -> 25.8 us
    dot_general x8 -> x0, matrix products: 345 us -> none  [block_term(): jnp.einsum('gpjq,rgjq->rgp', kernel, source_values, precision=highest)]
    gather x16 -> x0, local copies, waits for them, and re-layouts: 125 us -> none  [the longest x8 96.4 us: block_term(): source_values = jnp.take(shaped_charge, id_block, axis=1)]
    pallas_call x0 -> x1, Pallas kernels: none -> 86.4 us  [near_potential(): pl.pallas_call(near_kernel, out_shape=jax.ShapeDtypeStruct((R, panels), f...]
    select_n x16 -> x0, other arithmetic: 17.3 us -> none  [the longest x8 11.2 us: block_term(): source_place = jnp.take(shaped_points, id_block, axis=1)]
    slice x9 -> x2, local copies, waits for them, and re-layouts: 10.3 us -> 0.02 us  [leaf_halos(): first = jnp.concatenate([points[:, :width], charge[:, :width]], axis=0)]
    reshape x4 -> x2, local copies, waits for them, and re-layouts: 10.4 us -> 0.24 us  [the longest x1 0.13 us: body(): near_ids = (near - (here * leaf_count - NREACH)).reshape(-1)]
    ppermute x4 -> x3, starting transfers between devices: 18.2 us -> 13.6 us  [padded(): lax.ppermute(lax.slice_in_dim(block, 0, width, axis=dim), axis, backward)]
  transfers between devices with their start and end apart: 9 -> 9, of which waited for: 0 -> 0; matrix products, arithmetic and copies ran while one was open for 16% -> 40% of each run, Pallas kernels for 0% -> 0%
where the time goes in v1:
time: 348 us; the launch traced here: 342 us
  matrix products  99.3 us (29%)
  local copies, waits for them, and re-layouts  89.6 us (26%)
  Pallas kernels  86.4 us (25%)
  starting transfers between devices  26.2 us (8%)
  other arithmetic  25.8 us (7%)
  between operations  14.6 us (4%)
    pallas_call x1, Pallas kernels, near_potential(): pl.pallas_call(near_kernel, out_shape=jax.ShapeDtypeStruct((R, panels), f...  86.4 us
    dot_general x1, matrix products, leaf_moments(): jnp.einsum('klp,rlp->lkr', shaped_basis, shaped_charge, precision=highest)  24.9 us
    dot_general x4, matrix products, lift(): jnp.einsum('cab,cbr->car', trans.reshape(-1, K, K), moments, precision=hi...  22 us
    dot_general x3, matrix products, couple(): jnp.einsum('cjab,cjbr->car', green(targets[:, None], sources), moments, p...  15.8 us
    ppermute x3, starting transfers between devices, padded(): lax.ppermute(lax.slice_in_dim(block, 0, width, axis=dim), axis, backward)  13.6 us
    reshape x4, local copies, waits for them, and re-layouts, descend(): trans.reshape(-1, K, K)  13 us
    dot_general x1, matrix products, far_potential(): jnp.einsum('klp,lkr->rlp', shaped, local_leaf, precision=highest)  12.8 us
    dot_general x4, matrix products, descend(): jnp.einsum('cab,car->cbr', trans.reshape(-1, K, K), parent_local, precisi...  12 us
  transfers between devices with their start and end apart: 9, of which 0 were waited for; matrix products, arithmetic and copies ran while one was open for 40% of the time, Pallas kernels for 0%

profile of v1, /device:TPU:8, one launch (start us, length us, event | category | flops | bytes accessed | tf_op | source)
XLA Modules:
  0.0 341.9 jit_solution(13373787961840283175)
XLA Ops:
  8.2 7.6 %reshape.948 = f32[32,512,64]{2,1,0:T(8,128)} reshape(f32[32,32768]{1,0:T(8,128)} %param.22) | data formatting | bytes 8388608 | tf_op jit(solution)/shard_map/reshape | solution.py:83
  15.8 3.0 reshape.949
  18.8 2.9 copy.140
  21.7 8.4 %copy.141 = f32[512,32,32]{2,1,0:T(8,128)} copy(f32[512,32,32]{0,2,1:T(8,128)} %bitcast.122) | data formatting | bytes 4194304 | tf_op jit(solution)/shard_map/reshape | solution.py:97
  30.3 2.8 copy.156
  33.1 1.0 reshape.962
  34.1 24.9 %fusion.2 = f32[512,32,16]{1,2,0:T(8,128)S(1)} fusion(f32[32,512,64]{2,1,0:T(8,128)} %reshape.948, f32[16,512,64]{2,1,0:T(8,128)} %reshape.949), kind=kOutput, calls=%fused_computation.6 | convolution fusion | flops 201326592 | bytes 7340032 | tf_op jit(solution)/shard_map/klp,rlp->lkr/dot_general | solution.py:85
  59.0 15.9 %bitcast_reduce_fusion = f32[128,32,16]{1,2,0:T(8,128)S(1)} fusion(f32[512,32,16]{1,2,0:T(8,128)S(1)} %fusion.2, f32[512,32,32]{2,1,0:T(8,128)} %copy.141), kind=kOutput, calls=%fused_computation.20 | convolution fusion | flops 100859904 | bytes 3407872 | tf_op jit(solution)/shard_map/cab,cbr->car/dot_general | solution.py:89
  74.9 3.4 bitcast_reduce_fusion.1
  78.3 0.9 bitcast_reduce_fusion.2
  80.0 1.0 reshape.964
  82.3 1.9 collective-permute-start.6
  84.2 4.5 %collective-permute-start.7 = (f32[4,608]{1,0:T(4,128)}, f32[4,608]{1,0:T(4,128)}, u32[]{:S(2)}, u32[]{:S(2)}) collective-permute-start(f32[4,608]{1,0:T(4,128)} %get-tuple-element.34), channel_id=1, source_target_pairs={{1,0},{2,1},{3,2},{4,3},{5,4},{6,5},{7,6},{8,7},{9,8},{10,9},{11,1... | collective-permute-start | bytes 29192 | tf_op jit(solution)/shard_map/ppermute | solution.py:29
  88.8 0.9 reshape.969
  89.6 1.8 convolution_bitcast_fusion.3
  91.4 1.6 copy.177
  93.0 1.0 reshape.970
  94.1 1.2 compare_select_fusion.12
  95.3 1.1 fusion.113
  96.4 1.8 copy.179
  98.3 0.9 copy.157
  99.2 1.3 maximum_maximum_fusion.3
  101.6 1.1 copy.159
  104.0 1.9 collective-permute-start.4
  105.9 4.5 %collective-permute-start.5 = (f32[4,608]{1,0:T(4,128)}, f32[4,608]{1,0:T(4,128)}, u32[]{:S(2)}, u32[]{:S(2)}) collective-permute-start(f32[4,608]{1,0:T(4,128)} %get-tuple-element.20), channel_id=1, source_target_pairs={{1,0},{2,1},{3,2},{4,3},{5,4},{6,5},{7,6},{8,7},{9,8},{10,9},{11,1... | collective-permute-start | bytes 29192 | tf_op jit(solution)/shard_map/ppermute | solution.py:29
  110.5 1.2 copy.142
  113.2 0.9 bitcast_add_fusion
  114.2 1.1 copy.143
  115.9 2.3 collective-permute-start.2
  119.0 1.3 fusion.112
  121.1 0.8 reshape.968
  131.2 0.8 multiply_add_fusion.2
  133.7 0.9 multiply_add_fusion.3
  134.6 2.5 compare_select_fusion.2
  137.1 1.4 maximum_add_fusion.own_points
  143.9 4.5 %collective-permute-start.3 = (f32[4,608]{1,0:T(4,128)}, f32[4,608]{1,0:T(4,128)}, u32[]{:S(2)}, u32[]{:S(2)}) collective-permute-start(f32[4,608]{1,0:T(4,128)} %get-tuple-element.12), channel_id=1, source_target_pairs={{1,0},{2,1},{3,2},{4,3},{5,4},{6,5},{7,6},{8,7},{9,8},{10,9},{11,1... | collective-permute-start | bytes 29192 | tf_op jit(solution)/shard_map/ppermute | solution.py:29
  148.5 1.9 collective-permute-start
  151.1 4.5 %collective-permute-start.1 = (f32[19,1024]{1,0:T(8,128)}, f32[19,1024]{1,0:T(8,128)S(1)}, u32[]{:S(2)}, u32[]{:S(2)}) collective-permute-start(f32[19,1024]{1,0:T(8,128)} %pad_maximum_fusion.3), channel_id=1, source_target_pairs={{1,0},{2,1},{3,2},{4,3},{5,4},{6,5},{7,6},{8,7},{9,8},{10,9},{11,1... | collective-permute-start | bytes 233480 | tf_op jit(solution)/shard_map/ppermute | solution.py:41
  158.4 1.0 gather_fusion.1
  159.4 0.8 reshape.985
  161.0 2.4 gather_fusion
  163.4 2.5 reshape.977
  165.9 2.4 slice.177
  169.1 1.0 fusion.136
  170.7 0.9 reshape.1020
  171.7 0.8 reshape.959
  172.5 1.3 fusion.133
  175.8 1.2 copy.165
  176.9 2.5 copy.166
  179.7 0.8 copy.149
  180.5 0.8 copy.151
  181.4 2.4 copy.152
  183.8 3.2 copy.153
  187.0 4.0 %fusion.65 = f32[32,32,16]{1,2,0:T(8,128)S(1)} fusion(f32[32,3,32,16]{2,3,1,0:T(8,128)} %copy.166, f32[32,3,32]{2,1,0:T(4,128)} %copy.164, f32[32,32]{1,0:T(8,128)} %bitcast.144, f32[32,3,32]{2,1,0:T(4,128)} %copy.163, f32[32,32]{1,0:T(8,128)} %bitcast.145, f32[32,3,32]{2,1,0:T(4,128)} %copy.162, f32[32,32]{1,0:T(8,128)} %bitcast.143), kind=kOutput, calls=%fused_computation.68 | convolution fusion | flops 19857408 | bytes 311296 | tf_op jit(solution)/shard_map/cjab,cjbr->car/dot_general | solution.py:101
  191.1 10.9 %fusion.60 = f32[128,32,16]{1,2,0:T(8,128)} fusion(f32[128,3,32,16]{2,3,1,0:T(8,128)S(1)} %copy-done.6, f32[128,3,32]{2,1,0:T(4,128)S(1)} %copy-done.19, f32[128,32]{1,0:T(8,128)S(1)} %copy-done.25, f32[128,3,32]{2,1,0:T(4,128)S(1)} %copy-done.18, f32[128,32]{1,0:T(8,128)S(1)} %copy-done.24, f32[128,3,32]{2,1,0:T(4,128)S(1)} %copy.147, ...), kind=kOutput, calls=%fused_computation.63 | convolution fusion | flops 79429632 | bytes 1245184 | tf_op jit(solution)/shard_map/cjab,cjbr->car/dot_general | solution.py:101
  202.1 0.9 convolution_bitcast_fusion.4
  203.1 10.6 %fusion.68 = f32[8,32,16]{1,2,0:T(8,128)S(1)} fusion(f32[8,32]{1,0:T(8,128)S(1)} %copy-done.33, f32[32,32]{1,0:T(8,128)} %bitcast.141, f32[8,32]{1,0:T(8,128)S(1)} %bitcast.150, f32[32,32]{1,0:T(8,128)} %bitcast.142, f32[8,32]{1,0:T(8,128)} %bitcast.151, f32[32,32]{1,0:T(8,128)} %bitcast.140, f32[8,32]{1,0:T(8,128)S(1)} %bitcast.149, ...), kind=kOutput, calls=%fused_computation.69 | convolution fusion | flops 52953088 | bytes 98304 | tf_op jit(solution)/shard_map/cuab,ubr->car/dot_general | solution.py:344
  215.3 2.1 fusion.63
  217.8 9.1 %fusion.139 = f32[512,16,32]{2,1,0:T(8,128)S(1)} fusion(f32[512,32,16]{1,2,0:T(8,128)S(1)} %bitcast.121, f32[512,32,32]{2,1,0:T(8,128)S(1)} %bitcast.120), kind=kOutput, calls=%fused_computation.249 | convolution fusion | flops 100663296 | bytes 4194304 | tf_op jit(solution)/shard_map/cab,car->cbr/dot_general | solution.py:97
  226.9 12.8 %fusion.37 = f32[16,512,64]{2,0,1:T(8,128)S(1)} fusion(f32[512,16,32]{2,1,0:T(8,128)S(1)} %fusion.139, f32[32,512,64]{2,1,0:T(8,128)S(1)} %bitcast.118), kind=kOutput, calls=%fused_computation.42 | convolution fusion | flops 201326592 | bytes 7340032 | tf_op jit(solution)/shard_map/klp,lkr->rlp/dot_general | solution.py:275
  239.8 3.3 copy.183
  243.0 3.9 %reshape.975 = f32[16,32768]{1,0:T(8,128)} reshape(f32[16,512,64]{2,1,0:T(8,128)} %copy.183) | data formatting | bytes 4194304 | tf_op jit(solution)/shard_map/reshape | solution.py:275
  246.9 86.4 %near_potential.1 = f32[16,32768]{1,0:T(8,128)S(1)} custom-call(s32[8192]{0:T(1024)S(1)} %reshape.945.ids, f32[64]{0:T(128)S(1)} %reshape.946.origin, f32[3,32768]{1,0:T(4,128)S(1)} %maximum_add_fusion.own_points, f32[16,32768]{1,0:T(8,128)S(1)} %copy-done, f32[19,1024]{1,0:T(8,128)S(1)} %collective-permute-done.low_halo, ...), custom_call_target="tpu_custom_call" | custom-call | flops 6442450944 | bytes 5242880 | tf_op jit(solution)/shard_map/near_potential/pallas_call | solution.py:251
  333.3 1.6 add.633
  (198 shorter events, 36.2 us)
Async XLA Ops:
  6.5 196.5 %all-reduce.2.cloned.1.call-start = ((), (), s32[]{:S(2)}) async-start(), calls=%async_computation | async-start | bytes 524288 | tf_op jit(solution)/shard_map/psum | solution.py:339
  6.6 0.5 copy-start.31
  7.2 0.9 copy-start.28
  8.2 7.6 %copy-start = (f32[16,32768]{1,0:T(8,128)S(1)}, f32[16,32768]{1,0:T(8,128)}, u32[]{:S(2)}) copy-start(f32[16,32768]{1,0:T(8,128)} %own_charge.1) | copy-start | bytes 6291460
  21.7 8.4 %copy-start.15 = (f32[128,1024]{1,0:T(8,128)S(1)}, f32[128,1024]{1,0:T(8,128)}, u32[]{:S(2)}) copy-start(f32[128,1024]{1,0:T(8,128)} %param.25) | copy-start | bytes 1572868
  21.7 11.4 %copy-start.22 = (f32[32,1024]{1,0:T(8,128)S(1)}, f32[32,1024]{1,0:T(8,128)}, u32[]{:S(2)}) copy-start(f32[32,1024]{1,0:T(8,128)} %param.26) | copy-start | bytes 393220
  59.0 15.9 %copy-start.1 = (f32[128,32,32]{2,1,0:T(8,128)S(1)}, f32[128,32,32]{2,1,0:T(8,128)}, u32[]{:S(2)}) copy-start(f32[128,32,32]{2,1,0:T(8,128)} %copy.156) | copy-start | bytes 1572868
  59.0 19.3 %copy-start.4 = (f32[32,32,32]{2,1,0:T(8,128)S(1)}, f32[32,32,32]{2,1,0:T(8,128)}, u32[]{:S(2)}) copy-start(f32[32,32,32]{2,1,0:T(8,128)} %reshape.962) | copy-start | bytes 393220
  74.9 6.1 %copy-start.29 = (f32[8,96]{1,0:T(8,128)S(1)}, f32[8,96]{1,0:T(8,128)}, u32[]{:S(2)}) copy-start(f32[8,96]{1,0:T(8,128)} %param.30) | copy-start | bytes 9220
  79.2 9.5 %copy-start.14 = (f32[8,32,16]{1,2,0:T(8,128)}, f32[8,32,16]{1,2,0:T(8,128)S(1)}, u32[]{:S(2)}) copy-start(f32[8,32,16]{1,2,0:T(8,128)S(1)} %bitcast_reduce_fusion.2) | copy-start | bytes 49156
  81.0 7.7 %copy-start.20 = (f32[8,512]{1,0:T(8,128)}, f32[8,512]{1,0:T(8,128)S(1)}, u32[]{:S(2)}) copy-start(f32[8,512]{1,0:T(8,128)S(1)} %reshape.964) | copy-start | bytes 49156
  81.0 0.6 copy-start.27
  82.3 68.9 %collective-permute-start.6 = (f32[4,608]{1,0:T(4,128)}, f32[4,608]{1,0:T(4,128)}, u32[]{:S(2)}, u32[]{:S(2)}) collective-permute-start(f32[4,608]{1,0:T(4,128)} %get-tuple-element.33), channel_id=1, source_target_pairs={{0,1},{1,2},{2,3},{3,4},{4,5},{5,6},{6,7},{7,8},{8,9},{9,10},{10,1... | collective-permute-start | bytes 29192 | tf_op jit(solution)/shard_map/ppermute | solution.py:26
  84.2 71.5 %collective-permute-start.7 = (f32[4,608]{1,0:T(4,128)}, f32[4,608]{1,0:T(4,128)}, u32[]{:S(2)}, u32[]{:S(2)}) collective-permute-start(f32[4,608]{1,0:T(4,128)} %get-tuple-element.34), channel_id=1, source_target_pairs={{1,0},{2,1},{3,2},{4,3},{5,4},{6,5},{7,6},{8,7},{9,8},{10,9},{11,1... | collective-permute-start | bytes 29192 | tf_op jit(solution)/shard_map/ppermute | solution.py:29
  89.6 24.5 %copy-start.7 = (f32[8,32,32]{2,1,0:T(8,128)}, f32[8,32,32]{2,1,0:T(8,128)S(1)}, u32[]{:S(2)}) copy-start(f32[8,32,32]{2,1,0:T(8,128)S(1)} %reshape.969) | copy-start | bytes 98308
  95.3 1.1 copy-start.32
  99.2 1.3 copy-start.39
  99.2 1.3 copy-start.40
  100.6 13.6 %copy-start.21 = (f32[32,3]{1,0:T(8,128)}, f32[32,3]{1,0:T(8,128)S(1)}, u32[]{:S(2)}) copy-start(f32[32,3]{1,0:T(8,128)S(1)} %copy.154) | copy-start | bytes 1156
  102.7 11.5 %copy-start.10 = (f32[32,512]{1,0:T(8,128)}, f32[32,512]{1,0:T(8,128)S(1)}, u32[]{:S(2)}) copy-start(f32[32,512]{1,0:T(8,128)S(1)} %copy.159) | copy-start | bytes 196612
  104.0 39.9 %collective-permute-start.4 = (f32[4,608]{1,0:T(4,128)}, f32[4,608]{1,0:T(4,128)}, u32[]{:S(2)}, u32[]{:S(2)}) collective-permute-start(f32[4,608]{1,0:T(4,128)} %get-tuple-element.19), channel_id=1, source_target_pairs={{0,1},{1,2},{2,3},{3,4},{4,5},{5,6},{6,7},{7,8},{8,9},{9,10},{10,1... | collective-permute-start | bytes 29192 | tf_op jit(solution)/shard_map/ppermute | solution.py:26
  105.9 42.5 %collective-permute-start.5 = (f32[4,608]{1,0:T(4,128)}, f32[4,608]{1,0:T(4,128)}, u32[]{:S(2)}, u32[]{:S(2)}) collective-permute-start(f32[4,608]{1,0:T(4,128)} %get-tuple-element.20), channel_id=1, source_target_pairs={{1,0},{2,1},{3,2},{4,3},{5,4},{6,5},{7,6},{8,7},{9,8},{10,9},{11,1... | collective-permute-start | bytes 29192 | tf_op jit(solution)/shard_map/ppermute | solution.py:29
  114.2 43.6 %copy-start.12 = (f32[128,96]{1,0:T(8,128)}, f32[128,96]{1,0:T(8,128)S(1)}, u32[]{:S(2)}) copy-start(f32[128,96]{1,0:T(8,128)S(1)} %copy.144) | copy-start | bytes 147460
  114.2 36.2 %copy-start.11 = (f32[32,512]{1,0:T(8,128)S(1)}, f32[32,512]{1,0:T(8,128)}, u32[]{:S(2)}) copy-start(f32[32,512]{1,0:T(8,128)} %copy-done.10) | copy-start | bytes 196612
  115.9 44.3 %collective-permute-start.2 = (f32[4,608]{1,0:T(4,128)}, f32[4,608]{1,0:T(4,128)}, u32[]{:S(2)}, u32[]{:S(2)}) collective-permute-start(f32[4,608]{1,0:T(4,128)} %get-tuple-element.11), channel_id=1, source_target_pairs={{0,1},{1,2},{2,3},{3,4},{4,5},{5,6},{6,7},{7,8},{8,9},{9,10},{10,1... | collective-permute-start | bytes 29192 | tf_op jit(solution)/shard_map/ppermute | solution.py:26
  143.9 16.3 %collective-permute-start.3 = (f32[4,608]{1,0:T(4,128)}, f32[4,608]{1,0:T(4,128)}, u32[]{:S(2)}, u32[]{:S(2)}) collective-permute-start(f32[4,608]{1,0:T(4,128)} %get-tuple-element.12), channel_id=1, source_target_pairs={{1,0},{2,1},{3,2},{4,3},{5,4},{6,5},{7,6},{8,7},{9,8},{10,9},{11,1... | collective-permute-start | bytes 29192 | tf_op jit(solution)/shard_map/ppermute | solution.py:29
  148.5 98.4 %collective-permute-start = (f32[19,1024]{1,0:T(8,128)}, f32[19,1024]{1,0:T(8,128)S(1)}, u32[]{:S(2)}, u32[]{:S(2)}) collective-permute-start(f32[19,1024]{1,0:T(8,128)} %pad_maximum_fusion.2), channel_id=1, source_target_pairs={{0,1},{1,2},{2,3},{3,4},{4,5},{5,6},{6,7},{7,8},{8,9},{9,10},{10,1... | collective-permute-start | bytes 233480 | tf_op jit(solution)/shard_map/ppermute | solution.py:41
  151.1 95.7 %collective-permute-start.1 = (f32[19,1024]{1,0:T(8,128)}, f32[19,1024]{1,0:T(8,128)S(1)}, u32[]{:S(2)}, u32[]{:S(2)}) collective-permute-start(f32[19,1024]{1,0:T(8,128)} %pad_maximum_fusion.3), channel_id=1, source_target_pairs={{1,0},{2,1},{3,2},{4,3},{5,4},{6,5},{7,6},{8,7},{9,8},{10,9},{11,1... | collective-permute-start | bytes 233480 | tf_op jit(solution)/shard_map/ppermute | solution.py:41
  158.4 1.8 copy-start.13
  163.4 5.0 %copy-start.26 = (f32[8,3,96]{2,1,0:T(4,128)S(1)}, f32[8,3,96]{2,1,0:T(4,128)}, u32[]{:S(2)}) copy-start(f32[8,3,96]{2,1,0:T(4,128)} %slice.189) | copy-start | bytes 27652
  163.4 7.3 %copy-start.17 = (f32[8,3,512]{2,1,0:T(4,128)S(1)}, f32[8,3,512]{2,1,0:T(4,128)}, u32[]{:S(2)}) copy-start(f32[8,3,512]{2,1,0:T(4,128)} %slice.195) | copy-start | bytes 147460
  163.4 8.2 %slice-start.5 = ((f32[32,3,608]{2,1,0:T(4,128)}), f32[32,3,96]{2,1,0:T(4,128)S(1)}, s32[]{:S(2)}) async-start(f32[32,3,608]{2,1,0:T(4,128)} %reshape.985), calls=%async_computation.6 | async-start | bytes 131072 | tf_op jit(solution)/shard_map/slice | solution.py:292
  163.4 12.3 %slice-start.6 = ((f32[32,3,608]{2,1,0:T(4,128)}), f32[32,3,512]{2,1,0:T(4,128)S(1)}, s32[]{:S(2)}) async-start(f32[32,3,608]{2,1,0:T(4,128)} %reshape.985), calls=%async_computation.7 | async-start | bytes 524288 | tf_op jit(solution)/shard_map/slice | solution.py:291
  165.9 13.5 %slice-start.4 = ((f32[128,3,608]{2,1,0:T(4,128)}), f32[128,3,96]{2,1,0:T(4,128)S(1)}, s32[]{:S(2)}) async-start(f32[128,3,608]{2,1,0:T(4,128)} %reshape.977), calls=%async_computation.5 | async-start | bytes 524288 | tf_op jit(solution)/shard_map/slice | solution.py:292
  183.8 7.2 %copy-start.23 = (f32[128,32]{1,0:T(8,128)S(1)}, f32[128,32]{1,0:T(8,128)}, u32[]{:S(2)}) copy-start(f32[128,32]{1,0:T(8,128)} %copy.137) | copy-start | bytes 49156
  183.8 7.2 %copy-start.24 = (f32[128,32]{1,0:T(8,128)S(1)}, f32[128,32]{1,0:T(8,128)}, u32[]{:S(2)}) copy-start(f32[128,32]{1,0:T(8,128)} %copy.148) | copy-start | bytes 49156
  187.0 4.0 %copy-start.6 = (f32[128,3,32,16]{2,3,1,0:T(8,128)S(1)}, f32[128,3,32,16]{2,3,1,0:T(8,128)}, u32[]{:S(2)}) copy-start(f32[128,3,32,16]{2,3,1,0:T(8,128)} %copy.153) | copy-start | bytes 2359300
  187.0 4.0 %copy-start.18 = (f32[128,3,32]{2,1,0:T(4,128)S(1)}, f32[128,3,32]{2,1,0:T(4,128)}, u32[]{:S(2)}) copy-start(f32[128,3,32]{2,1,0:T(4,128)} %copy.149) | copy-start | bytes 147460
  187.0 4.0 %copy-start.19 = (f32[128,3,32]{2,1,0:T(4,128)S(1)}, f32[128,3,32]{2,1,0:T(4,128)}, u32[]{:S(2)}) copy-start(f32[128,3,32]{2,1,0:T(4,128)} %copy.151) | copy-start | bytes 147460
  187.0 4.0 %copy-start.25 = (f32[128,32]{1,0:T(8,128)S(1)}, f32[128,32]{1,0:T(8,128)}, u32[]{:S(2)}) copy-start(f32[128,32]{1,0:T(8,128)} %copy.150) | copy-start | bytes 49156
  191.0 11.0 %copy-start.16 = (f32[8,3,32,16]{3,2,1,0:T(8,128)S(1)}, f32[8,3,32,16]{3,2,1,0:T(8,128)}, u32[]{:S(2)}) copy-start(f32[8,3,32,16]{3,2,1,0:T(8,128)} %reshape.1020) | copy-start | bytes 147460
  191.0 11.0 %copy-start.30 = (f32[8,3,32]{2,1,0:T(4,128)S(1)}, f32[8,3,32]{2,1,0:T(4,128)}, u32[]{:S(2)}) copy-start(f32[8,3,32]{2,1,0:T(4,128)} %copy.172) | copy-start | bytes 9220
  191.1 11.0 %copy-start.34 = (f32[8,1,1,32]{3,2,0,1:T(1,128)S(1)}, f32[8,1,1,32]{3,2,0,1:T(1,128)}, u32[]{:S(2)}) copy-start(f32[8,1,1,32]{3,2,0,1:T(1,128)} %get-tuple-element.38) | copy-start | bytes 3076
  191.1 11.0 %copy-start.35 = (f32[8,1,1,32]{3,2,0,1:T(1,128)S(1)}, f32[8,1,1,32]{3,2,0,1:T(1,128)}, u32[]{:S(2)}) copy-start(f32[8,1,1,32]{3,2,0,1:T(1,128)} %get-tuple-element.39) | copy-start | bytes 3076
  191.1 11.0 %copy-start.36 = (f32[8,1,1,32]{3,2,0,1:T(1,128)S(1)}, f32[8,1,1,32]{3,2,0,1:T(1,128)}, u32[]{:S(2)}) copy-start(f32[8,1,1,32]{3,2,0,1:T(1,128)} %get-tuple-element.40) | copy-start | bytes 3076
  191.1 12.0 %copy-start.33 = (f32[8,32]{1,0:T(8,128)S(1)}, f32[8,32]{1,0:T(8,128)}, u32[]{:S(2)}) copy-start(f32[8,32]{1,0:T(8,128)} %fusion.112) | copy-start | bytes 3076
  191.1 12.0 %copy-start.37 = (f32[8,1,1,32]{3,2,0,1:T(1,128)S(1)}, f32[8,1,1,32]{3,2,0,1:T(1,128)}, u32[]{:S(2)}) copy-start(f32[8,1,1,32]{3,2,0,1:T(1,128)} %get-tuple-element.35) | copy-start | bytes 3076
  191.1 12.0 %copy-start.38 = (f32[8,1,1,32]{3,2,0,1:T(1,128)S(1)}, f32[8,1,1,32]{3,2,0,1:T(1,128)}, u32[]{:S(2)}) copy-start(f32[8,1,1,32]{3,2,0,1:T(1,128)} %get-tuple-element.36) | copy-start | bytes 3076
  203.1 10.7 %copy-start.8 = (f32[8,32,32]{2,1,0:T(8,128)S(1)}, f32[8,32,32]{2,1,0:T(8,128)}, u32[]{:S(2)}) copy-start(f32[8,32,32]{2,1,0:T(8,128)} %copy-done.7) | copy-start | bytes 98308
  203.1 10.9 %copy-start.5 = (f32[32,32,32]{2,1,0:T(8,128)S(1)}, f32[32,32,32]{2,1,0:T(8,128)}, u32[]{:S(2)}) copy-start(f32[32,32,32]{2,1,0:T(8,128)} %reshape.962) | copy-start | bytes 393220
  203.1 11.6 %copy-start.9 = (f32[128,32,16]{1,2,0:T(8,128)S(1)}, f32[128,32,16]{1,2,0:T(8,128)}, u32[]{:S(2)}) copy-start(f32[128,32,16]{1,2,0:T(8,128)} %fusion.60) | copy-start | bytes 786436
  203.1 14.7 %slice-start.2 = ((s8[8388608]{0:T(1024)(128)(4,1)}), s8[4194304]{0:T(1024)(128)(4,1)S(1)}, s32[]{:S(2)}) async-start(s8[8388608]{0:T(1024)(128)(4,1)} %bitcast.119), calls=%async_computation.3 | async-start | bytes 8388608
  213.7 1.6 copy-start.2
  214.0 3.8 %slice-start.3 = ((s8[8388608]{0:T(1024)(128)(4,1)}), s8[4194304]{0:T(1024)(128)(4,1)S(1)}, s32[]{:S(2)}) async-start(s8[8388608]{0:T(1024)(128)(4,1)} %bitcast.119), calls=%async_computation.4 | async-start | bytes 8388608
  217.4 9.5 %slice-start = ((s8[8388608]{0:T(1024)(128)(4,1)}), s8[4194304]{0:T(1024)(128)(4,1)S(1)}, s32[]{:S(2)}) async-start(s8[8388608]{0:T(1024)(128)(4,1)} %bitcast.117), calls=%async_computation.1 | async-start | bytes 8388608
  217.8 9.1 %slice-start.1 = ((s8[8388608]{0:T(1024)(128)(4,1)}), s8[4194304]{0:T(1024)(128)(4,1)S(1)}, s32[]{:S(2)}) async-start(s8[8388608]{0:T(1024)(128)(4,1)} %bitcast.117), calls=%async_computation.2 | async-start | bytes 8388608
  246.9 86.4 %copy-start.3 = (f32[16,32768]{1,0:T(8,128)S(1)}, f32[16,32768]{1,0:T(8,128)}, u32[]{:S(2)}) copy-start(f32[16,32768]{1,0:T(8,128)} %reshape.975) | copy-start | bytes 6291460
Sparse Core Ops, SparseCore 0:
  98.4 90.4 all-reduce.1

commit v2 on v1

v2 whole, which is shorter than its diff:
```python
import jax
import jax.numpy as jnp
from jax import lax
from jax.experimental import pallas as pl
from jax.experimental.pallas import tpu as pltpu
from jax.sharding import PartitionSpec as P

LEAF = 64
K = 32
R = 16
NREACH = 16


inv_four_pi = 0.07957747154594767
soft_square = 0.01
row_columns = 64


def leaf_halos(jitter, charge):
    count = lax.axis_size("gx")
    forward = [(i, i + 1) for i in range(count - 1)]
    backward = [(target, source) for source, target in forward]
    width = NREACH * LEAF
    last = jnp.concatenate([jitter[:, -width:], charge[:, -width:]], axis=0)
    first = jnp.concatenate([jitter[:, :width], charge[:, :width]], axis=0)
    return lax.ppermute(last, "gx", forward), lax.ppermute(first, "gx", backward)


def column_place(column):
    row_number = column >> 6
    middle = column & (row_columns - 1)
    across = jnp.where((row_number & 1) == 0, middle, row_columns - 1 - middle)
    return across.astype(jnp.float32), (4 * row_number).astype(jnp.float32)


GROUP = 16
BATCH = 8
bf16 = jnp.bfloat16
f32 = jnp.float32


def split_two(value):
    high = value.astype(bf16)
    return high, (value - high.astype(f32)).astype(bf16)


def split_three(value):
    first = value.astype(bf16).astype(f32)
    rest = value - first
    second = rest.astype(bf16).astype(f32)
    return first, second, rest - second


def lanes_of(tile):
    return pl.ds(pl.multiple_of(tile * 128, 128), 128)


def near_kernel(
    ids, own_jitter, own_charge, low_halo, high_halo, out, points, feats, charges, targets, kernels, weights
):
    halo_tiles = low_halo.shape[1] // 128
    own_tiles = own_jitter.shape[1] // 128
    here = lax.axis_index("gx")
    first_id = here * (2 * own_tiles) - NREACH
    high_side = jnp.where(lax.broadcasted_iota(jnp.int32, (1, 128), 1) < LEAF, 0.0, 1.0)
    left_half = lax.broadcasted_iota(jnp.int32, (32, 128), 1).astype(bf16) < 64
    row = lax.broadcasted_iota(jnp.int32, (8, 128), 0)
    is_three = row == 3
    is_four = row == 4
    below_five = row < 5
    one_three = jnp.where(is_three, 1.0, 0.0)
    one_four = jnp.where(is_four, 1.0, 0.0)

    def stage(tile, place, charge):
        number = tile + (here * own_tiles - halo_tiles)
        across, beside = column_place(number >> 1)
        beside = beside + (2 * (number & 1)).astype(f32)
        points[0:1, lanes_of(tile)] = across + place[0:1]
        points[1:2, lanes_of(tile)] = (beside + high_side) + place[1:2]
        points[2:3, lanes_of(tile)] = place[2:3]
        points[3:8, lanes_of(tile)] = jnp.zeros((5, 128), f32)
        charge = charge * inv_four_pi
        charges[2 * tile] = jnp.concatenate(split_two(charge), 0)
        charges[2 * tile + 1] = jnp.concatenate(split_two(pltpu.roll(charge, 64, 1)), 0)

    def stage_halo(halo, first):
        def step(i, carry):
            stage(first + i, halo[0:3, lanes_of(i)], halo[3:19, lanes_of(i)])
            return carry

        lax.fori_loop(0, halo_tiles, step, 0, unroll=2)

    def stage_own(i, carry):
        stage(halo_tiles + i, own_jitter[:, lanes_of(i)], own_charge[:, lanes_of(i)])
        return carry

    stage_halo(low_halo, 0)
    stage_halo(high_halo, halo_tiles + own_tiles)
    lax.fori_loop(0, own_tiles, stage_own, 0, unroll=4)

    def back(slot):
        total = lax.dot_general(
            kernels[slot], weights[slot], (((1,), (1,)), ((), ())), preferred_element_type=f32
        )
        total = jnp.transpose(total[:LEAF] + total[LEAF:])
        return total[:R] + total[R:]

    def emit(first):
        parts = [back(slot) for slot in range(BATCH)]
        first = jnp.maximum(first, 0)
        for half in range(BATCH // 2):
            place = pl.ds(pl.multiple_of((first + 2 * half) * LEAF, 128), 128)
            out[:, place] = jnp.concatenate([parts[2 * half], parts[2 * half + 1]], 1)

    def do_group(group, carry):
        base = group * GROUP
        across, beside = column_place(((first_id + NREACH) >> 2) + group * (GROUP // 4))
        row_sign = jnp.where(((first_id + NREACH + base) >> 8) % 2 == 0, 1.5, -1.5)
        shift = jnp.where(row == 0, across + row_sign, jnp.where(row == 1, beside + 1.5, 0.0))

        def local(tile):
            place = points[:, lanes_of(tile)] - shift
            square = place * place
            return place, jnp.broadcast_to(square[0:1] + square[1:2] + square[2:3], (8, 128))

        def source_rows(i, carry):
            place, square = local(base // 2 + i)
            rows = place * (-2.0) + jnp.where(is_three, square + soft_square, one_four)

            def put(entry, value):
                first, second, third = split_three(value)
                one = jnp.where(below_five, first, pltpu.roll(second, 5, 0))
                two = jnp.where(is_three, second, one)
                three = jnp.where(below_five, third + one_four, pltpu.roll(first, 5, 0))
                feats[entry] = jnp.concatenate([one, two, three, jnp.zeros_like(one)], 0).astype(bf16)

            put(2 * i, rows)
            put(2 * i + 1, pltpu.roll(rows, 64, 1))
            return carry

        def target_rows(i, carry):
            place, square = local(base // 2 + NREACH // 2 + i)
            first, second, third = split_three(place + jnp.where(is_four, square, one_three))
            one = jnp.where(below_five, first, pltpu.roll(first, 5, 0))
            two = jnp.where(below_five, second + one_three, pltpu.roll(second, 5, 0))
            three = jnp.where(below_five, jnp.where(is_four, third, first), pltpu.roll(third, 5, 0))
            rows = jnp.concatenate([one, two, three, jnp.zeros_like(one)], 0)
            targets[lanes_of(i), :] = jnp.transpose(rows).astype(bf16)
            return carry

        lax.fori_loop(0, (GROUP + 2 * NREACH) // 2, source_rows, 0, unroll=True)
        lax.fori_loop(0, GROUP // 2, target_rows, 0, unroll=True)

        def front(leaf, slot):
            target = targets[pl.ds(pl.multiple_of(leaf * LEAF, LEAF), LEAF), :]
            entry = base + leaf
            for j in range(4):
                sides = []
                for h in range(2):
                    one = ids[4 * j + 2 * h, entry] - first_id
                    two = (ids[4 * j + 2 * h + 1, entry] - first_id) ^ 1
                    sides.append(jnp.where(left_half, feats[one - base], feats[two - base]))
                    weights[slot, :, (2 * j + h) * 128 : (2 * j + h + 1) * 128] = jnp.where(
                        left_half, charges[one], charges[two]
                    )
                square = jnp.dot(target, jnp.concatenate(sides, 1), preferred_element_type=f32)
                high, low = split_two(lax.rsqrt(square))
                kernels[slot, 0:LEAF, j * 256 : (j + 1) * 256] = high
                kernels[slot, LEAF : 2 * LEAF, j * 256 : (j + 1) * 256] = low

        def step(i, carry):
            emit(base + BATCH * i - BATCH)
            for slot in range(BATCH):
                front(BATCH * i + slot, slot)
            return carry

        lax.fori_loop(0, GROUP // BATCH, step, 0)
        return carry

    kernels[...] = jnp.zeros_like(kernels)
    weights[...] = jnp.zeros_like(weights)
    lax.fori_loop(0, own_tiles * 2 // GROUP, do_group, 0)
    emit(own_tiles * 2 - BATCH)


def near_potential(ids, own_jitter, own_charge, low_halo, high_halo):
    panels = own_jitter.shape[1]
    leaves = (panels + 2 * low_halo.shape[1]) // LEAF
    pairs = panels * 16 * LEAF
    vmem = pl.BlockSpec(memory_space=pltpu.VMEM)
    smem = pl.BlockSpec(memory_space=pltpu.SMEM)
    return pl.pallas_call(
        near_kernel,
        out_shape=jax.ShapeDtypeStruct((R, panels), f32),
        in_specs=[smem, vmem, vmem, vmem, vmem],
        out_specs=vmem,
        scratch_shapes=[
            pltpu.VMEM((8, leaves * LEAF), f32),
            pltpu.VMEM((GROUP + 2 * NREACH, 32, 128), bf16),
            pltpu.VMEM((leaves, 2 * R, 128), bf16),
            pltpu.VMEM((GROUP * LEAF, 32), bf16),
            pltpu.VMEM((BATCH, 2 * LEAF, 16 * LEAF), bf16),
            pltpu.VMEM((BATCH, 2 * R, 16 * LEAF), bf16),
        ],
        compiler_params=pltpu.CompilerParams(vmem_limit_bytes=40 * 2**20),
        cost_estimate=pl.CostEstimate(
            flops=pairs * 192, bytes_accessed=panels * 160, transcendentals=pairs
        ),
        name="near_potential",
    )(ids, own_jitter, own_charge, low_halo, high_halo)


EDGE = 16
ROWS = R * K
WIDE = ROWS + 3 * K


def lane_digits(shape, dim):
    index = lax.broadcasted_iota(jnp.int32, shape, dim)
    return index >> 5, (index >> 3) & 3, index & 7


def matvec(matrix, vector, out, add):
    for_rows = 4

    def step(block, carry):
        start = pl.multiple_of(block * for_rows * K, for_rows * K)
        sums = [jnp.zeros((K, 128), f32) for _ in range(for_rows)]
        for column in range(K):
            values = matrix(column)
            for i in range(for_rows):
                sums[i] = sums[i] + values * vector[pl.ds(start + i * K + column, 1), :]
        for i in range(for_rows):
            place = pl.ds(start + i * K, K)
            out[place, :] = out[place, :] + sums[i] if add else sums[i]
        return carry

    lax.fori_loop(0, R // for_rows, step, 0)


def fold(ref, shifts):
    def step(i, carry):
        place = pl.ds(pl.multiple_of(i * 64, 64), 64)
        value = ref[place, :]
        for shift in shifts:
            value = value + pltpu.roll(value, shift, 1)
        ref[place, :] = value
        return carry

    lax.fori_loop(0, ROWS // 64, step, 0)


def centre_lanes(ids, level_width):
    first = ids * level_width
    row_number = first >> 6
    middle = (first & (row_columns - 1)).astype(f32) + 0.5 * (level_width - 1)
    across = jnp.where((row_number & 1) == 0, middle, row_columns - 1 - middle)
    return across, 4.0 * row_number.astype(f32) + 1.5


def up_kernel(
    tops, basis, charge, trans0, trans1, trans2, trans3, prox1, prox2, prox3,
    et, payload, last_out, first_out, terms, leaf_rows, coef0, coef, flipped, columns,
):
    here = lax.axis_index("gx")
    quarter = lax.broadcasted_iota(jnp.int32, (R, 256), 1).astype(f32)

    def moments(tile, carry):
        lanes = pl.ds(pl.multiple_of(tile * 256, 256), 256)
        high, low = split_two(basis[:, lanes])
        right = jnp.concatenate([high, low, high], 1)
        value = charge[:, lanes]
        pieces = [
            split_two(jnp.where((quarter >= 64.0 * i) & (quarter < 64.0 * (i + 1)), value, 0.0))
            for i in range(4)
        ]
        highs = jnp.concatenate([p[0] for p in pieces], 0)
        lows = jnp.concatenate([p[1] for p in pieces], 0)
        left = jnp.concatenate([highs, highs, lows], 1)
        leaf_rows[pl.ds(pl.multiple_of(tile * 64, 64), 64), 0:K] = lax.dot_general(
            left, right, (((1,), (1,)), ((), ())), preferred_element_type=f32
        )
        return carry

    lax.fori_loop(0, basis.shape[1] // 256, moments, 0, unroll=4)

    def leaf_coefs(r, carry):
        place = pl.ds(pl.multiple_of(r * K, K), K)
        for j0 in range(4):
            parts = [
                leaf_rows[pl.ds((j2 * 16 + j1 * 4 + j0) * R + r, 8, stride=64 * R), :]
                for j1 in range(4)
                for j2 in range(4)
            ]
            coef0[j0, place, :] = jnp.transpose(jnp.concatenate(parts, 0))[0:K]
        return carry

    lax.fori_loop(0, R, leaf_coefs, 0, unroll=2)

    def digits_first(q, rows):
        parts = [
            columns[q, pl.ds(rows[0] * a + rows[1] * b + rows[2], 8, stride=rows[3]), :]
            for a in range(4)
            for b in range(4)
        ]
        return jnp.transpose(jnp.concatenate(parts, 0))

    def flip(source, entries):
        for q in range(8):
            columns[q, 0 : source.shape[0], :] = source[:, q * 128 : (q + 1) * 128]
        for q in range(8):
            for entry, rows in entries:
                et[entry, q * 128 : (q + 1) * 128, :] = digits_first(q, rows)

    flip(trans0, [(j0, (4, 16, j0, 64)) for j0 in range(4)])
    flip(trans1, [(4, (1, 4, 0, 16))])
    flip(trans2, [(5, (0, 1, 0, 4))])
    flip(trans3, [(6, (0, 0, 0, 1))])

    def lift_from(entry, vector, out, add):
        matvec(lambda b: et[entry, pl.ds(b, K, stride=K), :], vector, out, add)

    for j0 in range(4):
        lift_from(j0, coef0.at[j0], coef.at[0], j0 > 0)
    lift_from(4, coef.at[0], coef.at[1], False)
    fold(coef.at[1], (32, 64))
    lift_from(5, coef.at[1], coef.at[2], False)
    fold(coef.at[2], (8, 16))
    lift_from(6, coef.at[2], coef.at[3], False)

    j1, j2, c3 = lane_digits((1, 128), 1)
    for level, (prox, ids, rows) in enumerate(
        (
            (prox1, c3 * 16 + j2 * 4 + j1 + here * 128, (1, 4, 0, 16)),
            (prox2, c3 * 4 + j2 + here * 32, (0, 1, 0, 4)),
            (prox3, c3 + here * 8, (0, 0, 0, 1)),
        )
    ):
        if level == 0:
            columns[level, 0:128, :] = jnp.transpose(
                jnp.concatenate([prox[...], jnp.zeros((128 - 3 * K, 128), f32)], 0)
            )
        else:
            columns[level, 0 : prox.shape[0], :] = jnp.concatenate(
                [prox[...], jnp.zeros((prox.shape[0], 128 - 3 * K), f32)], 1
            )
        offsets = digits_first(level, rows)
        across, beside = centre_lanes(ids, 4**level)
        payload[level, 0:ROWS, :] = coef[level]
        payload[level, ROWS : ROWS + K, :] = across + float(4**level) * offsets[0:K]
        payload[level, ROWS + K : ROWS + 2 * K, :] = beside + 4.0 * offsets[K : 2 * K]
        payload[level, ROWS + 2 * K : WIDE, :] = offsets[2 * K : 3 * K]

    def flip_payload(source, width):
        for q in range(0, width, 128):
            size = min(128, width - q)
            block = source[q : q + size, :]
            if size < 128:
                block = jnp.concatenate([block, jnp.zeros((128 - size, 128), f32)], 0)
            flipped[:, q : q + 128] = jnp.transpose(block)

    last_rows = ([31, 63, 95, 127], [7, 15, 23, 31], [4, 5, 6, 7])
    first_rows = ([0, 32, 64, 96], [0, 8, 16, 24], [0, 1, 2, 3])
    last_out[...] = jnp.zeros_like(last_out)
    first_out[...] = jnp.zeros_like(first_out)
    for level in range(3):
        flip_payload(payload.at[level], WIDE)
        for i in range(4):
            target = level * 4 + i
            last_out[target : target + 1, :] = flipped[last_rows[level][i] : last_rows[level][i] + 1, 0:WIDE]
            first_out[target : target + 1, :] = flipped[first_rows[level][i] : first_rows[level][i] + 1, 0:WIDE]
    flip_payload(coef.at[3], ROWS)
    top_ids = lax.broadcasted_iota(jnp.int32, (terms.shape[0], ROWS), 0)
    total = jnp.zeros(terms.shape, f32)
    for c in range(8):
        total = total + jnp.where(top_ids == tops[here * 8 + c], flipped[c : c + 1, 0:ROWS], 0.0)
    terms[...] = total


def upward_pass(tops, basis, charge, trans0, trans1, trans2, trans3, prox1, prox2, prox3, top_count):
    vmem = pl.BlockSpec(memory_space=pltpu.VMEM)
    smem = pl.BlockSpec(memory_space=pltpu.SMEM)
    leaves = trans0.shape[0]
    return pl.pallas_call(
        up_kernel,
        out_shape=[
            jax.ShapeDtypeStruct((7, K * K, 128), f32),
            jax.ShapeDtypeStruct((3, WIDE, 128), f32),
            jax.ShapeDtypeStruct((EDGE, WIDE), f32),
            jax.ShapeDtypeStruct((EDGE, WIDE), f32),
            jax.ShapeDtypeStruct((top_count, ROWS), f32),
        ],
        in_specs=[smem] + [vmem] * 9,
        out_specs=[vmem] * 5,
        scratch_shapes=[
            pltpu.VMEM((leaves * R, 128), f32),
            pltpu.VMEM((4, ROWS, 128), f32),
            pltpu.VMEM((4, ROWS, 128), f32),
            pltpu.VMEM((128, 640), f32),
            pltpu.VMEM((8, leaves, 128), f32),
        ],
        compiler_params=pltpu.CompilerParams(vmem_limit_bytes=40 * 2**20),
        cost_estimate=pl.CostEstimate(
            flops=leaves * 200000, bytes_accessed=leaves * 20000, transcendentals=0
        ),
        name="upward_pass",
    )(tops, basis, charge, trans0, trans1, trans2, trans3, prox1, prox2, prox3)


def down_kernel(
    tops, et, payload, low_halo, high_halo, coef_top, prox_top, list1, list2, list3, basis, near_field,
    out, split_rows, split_top, gathered, green_rows, local, leaf_local, leaf_rows, columns,
):
    here = lax.axis_index("gx")
    top_count = coef_top.shape[0]
    j1, j2, c3 = lane_digits((1, 128), 1)

    def split_to(ref, columns, value):
        parts = split_three(value)
        for i in range(3):
            ref[i, :, columns] = parts[i].astype(bf16)

    def pick(ref, hot):
        hot = hot.astype(f32).astype(bf16)
        total = jnp.dot(ref[0], hot, preferred_element_type=f32)
        total = total + jnp.dot(ref[1], hot, preferred_element_type=f32)
        return total + jnp.dot(ref[2], hot, preferred_element_type=f32)

    def couple_picked(target, out_ref, add):
        def step(b, carry):
            square = None
            for axis_id in range(3):
                spread = target(axis_id) - gathered[pl.ds(ROWS + axis_id * K + b, 1), :]
                square = spread * spread if square is None else square + spread * spread
            green_rows[pl.ds(pl.multiple_of(b * K, K), K), :] = inv_four_pi * lax.rsqrt(square + soft_square)
            return carry

        lax.fori_loop(0, K, step, 0, unroll=4)
        matvec(lambda b: green_rows[b * K : (b + 1) * K, :], gathered, out_ref, add)

    def descend_from(entry, vector, out_ref, add):
        matvec(lambda a: et[entry, a * K : (a + 1) * K, :], vector, out_ref, add)

    my_top = jnp.zeros((1, 128), jnp.int32)
    for c in range(8):
        my_top = jnp.where(c3 == c, tops[here * 8 + c], my_top)
    for q in range(0, split_top.shape[2], 128):
        rows = min(128, top_count - q)

        def flip_top(block):
            if block.shape[1] < 128:
                block = jnp.concatenate([block, jnp.zeros((rows, 128 - block.shape[1]), f32)], 1)
            if rows < 128:
                block = jnp.concatenate([block, jnp.zeros((128 - rows, 128), f32)], 0)
            return jnp.transpose(block)

        def keep_top(first, value):
            parts = split_three(value)
            for i in range(3):
                split_top[i, first : first + value.shape[0], q : q + 128] = parts[i].astype(bf16)

        for w in range(0, ROWS, 128):
            keep_top(w, flip_top(coef_top[q : q + rows, w : w + 128]))
        offsets = flip_top(prox_top[q : q + rows, :])
        across, beside = centre_lanes(lax.broadcasted_iota(jnp.int32, (1, 128), 1) + q, 64)
        keep_top(ROWS, across + 64.0 * offsets[0:K])
        keep_top(ROWS + K, beside + 4.0 * offsets[K : 2 * K])
        keep_top(ROWS + 2 * K, offsets[2 * K : 3 * K])
    top_rows = lax.broadcasted_iota(jnp.int32, (split_top.shape[2], 128), 0)
    targets = pick(split_top.at[:, ROWS:WIDE, :], top_rows == my_top)
    leaf_local[0, 0 : 3 * K, :] = targets
    lane_block = lax.broadcasted_iota(jnp.int32, (1, 128), 1) >> 3
    local[0] = jnp.zeros((ROWS, 128), f32)

    def top_block(block, carry):
        source = block * 16 + lane_block
        far = jnp.abs(source - my_top) >= 2
        gathered[...] = pick(split_top, (top_rows == jnp.where(far, source, -1)))
        couple_picked(lambda axis_id: leaf_local[0, axis_id * K : (axis_id + 1) * K, :], local.at[0], True)
        return carry

    lax.fori_loop(0, (top_count + 15) // 16, top_block, 0)
    fold(local.at[0], (8, 16, 32, 64))

    halo = jnp.concatenate([low_halo[...], high_halo[...], jnp.zeros((128 - 2 * EDGE, WIDE), f32)], 0)
    for w in range(0, WIDE, 128):
        size = min(128, WIDE - w)
        block = halo[:, w : w + size]
        if size < 128:
            block = jnp.concatenate([block, jnp.zeros((128, 128 - size), f32)], 1)
        parts = split_three(jnp.transpose(block))
        for i in range(3):
            split_rows[i, w : w + size, 128:256] = parts[i][0:size].astype(bf16)

    def lane_list(ref, rows, base):
        count = ref.shape[1]
        values = jnp.concatenate([(ref[...] - base).astype(f32), jnp.zeros((125, count), f32)], 0)
        if count < 128:
            values = jnp.concatenate([values, jnp.zeros((128, 128 - count), f32)], 1)
        columns[...] = jnp.transpose(values)
        parts = [
            columns[pl.ds(rows[0] * a + rows[1] * b, 8, stride=rows[2]), :] for a in range(4) for b in range(4)
        ]
        return jnp.transpose(jnp.concatenate(parts, 0)).astype(jnp.int32)

    source = lax.broadcasted_iota(jnp.int32, (256, 128), 0)
    edge = source - 128
    s1, s2, s3 = (source >> 5) & 3, (source >> 3) & 3, source & 7

    def source_ids(level, own, own_count, count):
        low = edge - 4 * level
        high = edge - EDGE - 4 * level
        ids = jnp.where(source < own_count, own, -1000)
        ids = jnp.where((low >= 0) & (low < 4), low - 4, ids)
        return jnp.where((high >= 0) & (high < 4), high + count, ids)

    def place_of(level):
        return lambda axis_id: payload[level, ROWS + axis_id * K : ROWS + (axis_id + 1) * K, :]

    picked = lane_list(list3, (0, 0, 1), here * 8)
    wanted = jnp.where(j2 == 0, picked[0:1], jnp.where(j2 == 1, picked[1:2], jnp.where(j2 == 2, picked[2:3], -5000)))
    split_to(split_rows, slice(0, 128), payload[2])
    gathered[...] = pick(split_rows, source_ids(2, s3, 8, 8) == wanted)
    couple_picked(place_of(2), local.at[1], False)
    fold(local.at[1], (8, 16))
    descend_from(6, local.at[0], local.at[1], True)

    picked = lane_list(list2, (0, 1, 4), here * 32)
    wanted = jnp.where(j1 == 0, picked[0:1], jnp.where(j1 == 1, picked[1:2], jnp.where(j1 == 2, picked[2:3], -5000)))
    split_to(split_rows, slice(0, 128), payload[1])
    gathered[...] = pick(split_rows, source_ids(1, s3 * 4 + s2, 32, 32) == wanted)
    couple_picked(place_of(1), local.at[0], False)
    fold(local.at[0], (32, 64))
    descend_from(5, local.at[1], local.at[0], True)

    picked = lane_list(list1, (1, 4, 16), here * 128)
    split_to(split_rows, slice(0, 128), payload[0])
    ids = source_ids(0, s3 * 16 + s2 * 4 + s1, 128, 128)
    for j in range(3):
        gathered[...] = pick(split_rows, ids == picked[j : j + 1])
        couple_picked(place_of(0), local.at[1], j > 0)
    descend_from(4, local.at[0], local.at[1], True)
    for j0 in range(4):
        descend_from(j0, local.at[1], leaf_local.at[j0], False)

    def leaf_terms(r, carry):
        place = pl.ds(pl.multiple_of(r * K, K), K)
        for j0 in range(4):
            value = jnp.transpose(
                jnp.concatenate([leaf_local[j0, place, :], jnp.zeros((128 - K, 128), f32)], 0)
            )
            for a in range(4):
                for b in range(4):
                    leaf_rows[pl.ds((b * 16 + a * 4 + j0) * R + r, 8, stride=64 * R), :] = value[
                        a * 32 + b * 8 : a * 32 + b * 8 + 8
                    ]
        return carry

    lax.fori_loop(0, R, leaf_terms, 0, unroll=2)
    half = lax.broadcasted_iota(jnp.int32, (R, 128), 1) < 64

    def potential(tile, carry):
        lanes = pl.ds(pl.multiple_of(tile * 256, 256), 256)
        high, low = split_two(basis[:, lanes])
        left, left_low = split_two(leaf_rows[pl.ds(pl.multiple_of(tile * 64, 64), 64), 0:K])
        total = jnp.dot(left, high, preferred_element_type=f32)
        total = total + jnp.dot(left, low, preferred_element_type=f32)
        total = total + jnp.dot(left_low, high, preferred_element_type=f32)
        one = jnp.where(half, total[0:16, 0:128], total[16:32, 0:128])
        two = jnp.where(half, total[32:48, 128:256], total[48:64, 128:256])
        out[:, lanes] = near_field[:, lanes] + jnp.concatenate([one, two], 1)
        return carry

    lax.fori_loop(0, basis.shape[1] // 256, potential, 0, unroll=4)


def downward_pass(
    tops, et, payload, low_halo, high_halo, coef_top, prox_top, list1, list2, list3, basis, near_field
):
    vmem = pl.BlockSpec(memory_space=pltpu.VMEM)
    smem = pl.BlockSpec(memory_space=pltpu.SMEM)
    panels = basis.shape[1]
    top_count = coef_top.shape[0]
    top_lanes = (top_count + 127) // 128 * 128
    return pl.pallas_call(
        down_kernel,
        out_shape=jax.ShapeDtypeStruct((R, panels), f32),
        in_specs=[smem] + [vmem] * 11,
        out_specs=vmem,
        scratch_shapes=[
            pltpu.VMEM((3, WIDE, 256), bf16),
            pltpu.VMEM((3, WIDE, top_lanes), bf16),
            pltpu.VMEM((WIDE, 128), f32),
            pltpu.VMEM((K * K, 128), f32),
            pltpu.VMEM((2, ROWS, 128), f32),
            pltpu.VMEM((4, ROWS, 128), f32),
            pltpu.VMEM((panels // LEAF * R, 128), f32),
            pltpu.VMEM((128, 128), f32),
        ],
        compiler_params=pltpu.CompilerParams(vmem_limit_bytes=40 * 2**20),
        cost_estimate=pl.CostEstimate(
            flops=panels * 4000, bytes_accessed=panels * 400, transcendentals=panels * 20
        ),
        name="downward_pass",
    )(tops, et, payload, low_halo, high_halo, coef_top, prox_top, list1, list2, list3, basis, near_field)


def body(
    charge, jitter, basis, near, trans0, trans1, trans2, trans3,
    prox1, prox2, prox3, prox_top, list1, list2, list3, top_of,
):
    count = lax.axis_size("gx")
    forward = [(i, i + 1) for i in range(count - 1)]
    backward = [(target, source) for source, target in forward]
    low_leaves, high_leaves = leaf_halos(jitter, charge)
    et, payload, last, first, terms = upward_pass(
        top_of, basis, charge, trans0, trans1, trans2, trans3, prox1.T, prox2, prox3, prox_top.shape[0]
    )
    low_halo = lax.ppermute(last, "gx", forward)
    high_halo = lax.ppermute(first, "gx", backward)
    coef_top = lax.psum(terms, "gx")
    near_field = near_potential(near.T, jitter, charge, low_leaves, high_leaves)
    near_field, coef_top = lax.optimization_barrier((near_field, coef_top))
    return downward_pass(
        top_of, et, payload, low_halo, high_halo, coef_top, prox_top, list1.T, list2.T, list3.T, basis, near_field
    )


def solution(mesh):
    placed = (
        P(None, ("groups", "gx")),
        P(None, ("groups", "gx")),
        P(None, ("groups", "gx")),
        P(("groups", "gx"), None),
        P(("groups", "gx"), None),
        P(("groups", "gx"), None),
        P(("groups", "gx"), None),
        P(("groups", "gx"), None),
        P(("groups", "gx"), None),
        P(("groups", "gx"), None),
        P(("groups", "gx"), None),
        P("groups", None),
        P(("groups", "gx"), None),
        P(("groups", "gx"), None),
        P(("groups", "gx"), None),
        P("groups"),
    )
    return jax.shard_map(
        body, mesh=mesh, in_specs=placed, out_specs=P(None, ("groups", "gx")), check_vma=False
    )
```

time: 348 us -> 203 us (0.58); the launches traced: 342 us -> 202 us
  matrix products: 99.3 us -> 0 us
  local copies, waits for them, and re-layouts: 89.6 us -> 23.4 us
  Pallas kernels: 86.4 us -> 151 us
  other arithmetic: 25.8 us -> 0.67 us
  starting transfers between devices: 26.2 us -> 13.1 us
    dot_general x15 -> x0, matrix products: 99.3 us -> none  [the longest x1 24.9 us: leaf_moments(): jnp.einsum('klp,rlp->lkr', shaped_basis, shaped_charge, precision=highest)]
    pallas_call x0 -> x2, Pallas kernels: none -> 63.9 us  [the longest x1 35 us: downward_pass(): pl.pallas_call(down_kernel, out_shape=jax.ShapeDtypeStruct((R, panels), f...]
    reshape x23 -> x0, local copies, waits for them, and re-layouts: 45.1 us -> none  [the longest x4 13 us: descend(): trans.reshape(-1, K, K)]
    unnamed x92 -> x48, local copies, waits for them, and re-layouts: 4.97 us -> 21.8 us
    ppermute x6 -> x2, starting transfers between devices: 19.8 us -> 6.64 us  [the longest x1 4.72 us: body(): high_halo = lax.ppermute(first, 'gx', backward)]
    slice x22 -> x2, local copies, waits for them, and re-layouts: 12.2 us -> 1.62 us  [leaf_halos(): first = jnp.concatenate([jitter[:, :width], charge[:, :width]], axis=0)]
    add x10 -> x0, other arithmetic: 8.5 us -> none  [the longest x8 5.58 us: proxy_points(): centre[:, :, None]]
    gather x7 -> x0, local copies, waits for them, and re-layouts: 7.98 us -> none  [the longest x6 7.41 us: couple_level(): picked = extended[row_ids]]
  transfers between devices with their start and end apart: 9 -> 5, of which waited for: 0 -> 0; matrix products, arithmetic and copies ran while one was open for 40% -> 0% of each run, Pallas kernels for 0% -> 58%
where the time goes in v2:
time: 203 us; the launch traced here: 202 us
  Pallas kernels  151 us (74%)
  local copies, waits for them, and re-layouts  23.4 us (12%)
  between operations  13.6 us (7%)
  starting transfers between devices  13.1 us (6%)
    pallas_call x1, Pallas kernels, near_potential(): pl.pallas_call(near_kernel, out_shape=jax.ShapeDtypeStruct((R, panels), f...  87.6 us
    pallas_call x1, Pallas kernels, downward_pass(): pl.pallas_call(down_kernel, out_shape=jax.ShapeDtypeStruct((R, panels), f...  35 us
    pallas_call x1, Pallas kernels, upward_pass(): pl.pallas_call(up_kernel, out_shape=[jax.ShapeDtypeStruct((7, K * K, 128)...  28.9 us
    unnamed x48, local copies, waits for them, and re-layouts  21.8 us
    ppermute x1, starting transfers between devices, body(): high_halo = lax.ppermute(first, 'gx', backward)  4.72 us
    ppermute x1, starting transfers between devices, leaf_halos(): lax.ppermute(first, 'gx', backward)  4.53 us
  transfers between devices with their start and end apart: 5, of which 0 were waited for; matrix products, arithmetic and copies ran while one was open for 0% of the time, Pallas kernels for 58%

profile of v2, /device:TPU:8, one launch (start us, length us, event | category | flops | bytes accessed | tf_op | source)
XLA Modules:
  0.0 202.2 jit_solution(17263618372935694567)
XLA Ops:
  6.5 0.0 all-reduce.2.cloned.1.call-start
  6.5 0.7 fusion.1
  7.3 0.9 fusion
  8.2 1.9 collective-permute-start.2
  10.1 0.7 pad_maximum_fusion.1
  10.8 4.5 %collective-permute-start.3 = (f32[19,1024]{1,0:T(8,128)}, f32[19,1024]{1,0:T(8,128)S(1)}, u32[]{:S(2)}, u32[]{:S(2)}) collective-permute-start(f32[19,1024]{1,0:T(8,128)} %pad_maximum_fusion.1), channel_id=1, source_target_pairs={{1,0},{2,1},{3,2},{4,3},{5,4},{6,5},{7,6},{8,7},{9,8},{10,9},{11,1... | collective-permute-start | bytes 233480 | tf_op jit(solution)/shard_map/ppermute | solution.py:26
  15.3 0.0 copy-start
  15.3 2.2 %copy-done = f32[32,32768]{1,0:T(8,128)S(1)} copy-done((f32[32,32768]{1,0:T(8,128)S(1)}, f32[32,32768]{1,0:T(8,128)}, u32[]{:S(2)}) %copy-start) | copy-done | bytes 4194328
  17.5 0.0 copy-start.4
  17.5 1.6 copy-done.4
  19.1 0.0 copy-start.6
  19.1 1.6 copy-done.6
  20.7 0.0 copy-start.9
  20.7 1.0 copy-done.9
  21.7 0.0 copy-start.10
  21.7 0.9 copy-done.10
  22.6 0.0 copy-start.12
  22.6 0.8 copy-done.12
  23.4 0.0 copy-start.13
  23.4 0.8 copy-done.13
  24.2 0.0 copy-start.14
  24.2 0.7 copy-done.14
  24.9 0.0 copy-start.16
  24.9 0.7 copy-done.16
  25.6 0.0 copy-start.21
  25.6 0.7 copy-done.21
  26.2 0.0 copy-start.5
  26.2 0.0 copy-start.23
  26.2 28.9 %upward_pass.1 = (f32[7,1024,128]{2,1,0:T(8,128)S(1)}, f32[3,608,128]{2,1,0:T(8,128)S(1)}, f32[16,608]{1,0:T(8,128)S(1)}, f32[16,608]{1,0:T(8,128)S(1)}, f32[32,512]{1,0:T(8,128)}) custom-call(s32[128]{0:T(128)S(1)} %copy-done.21, f32[32,32768]{1,0:T(8,128)S(1)} %copy-done, f32[16,32768]{1,0:T(8,128)S(1)} %copy-done.4, f32[512,1024]{1,0:T(8,128)S(1)} %copy-done.6, ...), custom_call_target="tpu_custom_call" | custom-call | flops 102400000 | bytes 10240000 | tf_op jit(solution)/shard_map/upward_pass/pallas_call | solution.py:384
  55.1 0.0 copy-start.2
  55.1 1.8 copy-done.2
  56.9 0.0 all-reduce.2.cloned.1.call-update
  56.9 1.9 collective-permute-start
  58.9 4.7 %collective-permute-start.1 = (f32[16,608]{1,0:T(8,128)S(1)}, f32[16,608]{1,0:T(8,128)S(1)}, u32[]{:S(2)}, u32[]{:S(2)}) collective-permute-start(f32[16,608]{1,0:T(8,128)S(1)} %get-tuple-element.15), channel_id=1, source_target_pairs={{1,0},{2,1},{3,2},{4,3},{5,4},{6,5},{7,6},{8,7},{9,8},{10,9},{11,1... | collective-permute-start | bytes 116744 | tf_op jit(solution)/shard_map/ppermute | solution.py:620
  63.6 0.0 collective-permute-done.2.low_halo
  63.6 0.0 collective-permute-done.3.high_halo
  63.6 0.0 copy-done.5
  63.6 0.0 copy-done.23
  63.6 0.0 copy-start.17
  63.7 1.0 copy-done.17
  64.7 0.0 copy-start.15
  64.7 0.0 copy-start.18
  64.7 0.0 copy-start.19
  64.7 0.0 copy-start.20
  64.7 0.0 copy-start.22
  64.7 87.6 %near_potential.1.near_field = f32[16,32768]{1,0:T(8,128)S(1)} custom-call(s32[16,512]{1,0:T(8,128)S(1)} %bitcast.9, f32[3,32768]{1,0:T(4,128)S(1)} %copy-done.17, f32[16,32768]{1,0:T(8,128)S(1)} %copy-done.5, f32[19,1024]{1,0:T(8,128)S(1)} %collective-permute-done.2.low_halo, f32[19,1024]{1,0:T(8,128)S(1)} %collective-permute-done.3.high_halo), custom_call_target="tpu_custom_call" | custom-call | flops 6442450944 | bytes 5242880 | tf_op jit(solution)/shard_map/near_potential/pallas_call | solution.py:192
  152.3 0.0 copy-start.7
  152.3 1.4 copy-done.7
  153.7 0.0 all-reduce.2.cloned.1.call-done.coef_top
  153.7 0.0 collective-permute-done.low_halo
  153.7 0.0 collective-permute-done.1.high_halo
  153.7 0.0 copy-done.15
  153.7 0.0 copy-done.18
  153.7 0.0 copy-done.19
  153.7 0.0 copy-done.20
  153.8 0.0 copy-done.22
  153.8 0.0 copy-start.1
  153.8 2.2 %copy-done.1 = f32[32,32768]{1,0:T(8,128)S(1)} copy-done((f32[32,32768]{1,0:T(8,128)S(1)}, f32[32,32768]{1,0:T(8,128)}, u32[]{:S(2)}) %copy-start.1) | copy-done | bytes 4194328
  156.0 0.0 copy-start.3
  156.0 2.0 %copy-done.3 = f32[7,1024,128]{2,1,0:T(8,128)S(1)} copy-done((f32[7,1024,128]{2,1,0:T(8,128)S(1)}, f32[7,1024,128]{2,1,0:T(8,128)}, u32[]{:S(2)}) %copy-start.3) | copy-done | bytes 3670040
  158.0 1.6 copy-done.8
  159.6 0.0 copy-start.11
  159.6 0.8 copy-done.11
  160.4 35.0 %downward_pass.1 = f32[16,32768]{1,0:T(8,128)} custom-call(s32[128]{0:T(128)S(1)} %copy-done.22, f32[7,1024,128]{2,1,0:T(8,128)S(1)} %copy-done.3, f32[3,608,128]{2,1,0:T(8,128)S(1)} %get-tuple-element.13.payload, f32[16,608]{1,0:T(8,128)S(1)} %collective-permute-done.low_halo, f32[16,608]{1,0:T(8,128)S(1)} %collective-permute-done.1.high_halo, ...), custom_call_target="tpu_custom_call" | custom-call | flops 131072000 | bytes 13107200 | tf_op jit(solution)/shard_map/downward_pass/pallas_call | solution.py:585
  (2 shorter events, 0.0 us)
Async XLA Ops:
  6.5 147.2 %all-reduce.2.cloned.1.call-start = ((), (), s32[]{:S(2)}) async-start(), calls=%async_computation | async-start | bytes 131072 | tf_op jit(solution)/shard_map/psum | solution.py:621
  8.2 55.4 %collective-permute-start.2 = (f32[19,1024]{1,0:T(8,128)S(1)}, f32[19,1024]{1,0:T(8,128)S(1)}, u32[]{:S(2)}, u32[]{:S(2)}) collective-permute-start(f32[19,1024]{1,0:T(8,128)S(1)} %pad_maximum_fusion), channel_id=1, source_target_pairs={{0,1},{1,2},{2,3},{3,4},{4,5},{5,6},{6,7},{7,8},{8,9},{9,10},{10,1... | collective-permute-start | bytes 233480 | tf_op jit(solution)/shard_map/ppermute | solution.py:26
  10.8 52.8 %collective-permute-start.3 = (f32[19,1024]{1,0:T(8,128)}, f32[19,1024]{1,0:T(8,128)S(1)}, u32[]{:S(2)}, u32[]{:S(2)}) collective-permute-start(f32[19,1024]{1,0:T(8,128)} %pad_maximum_fusion.1), channel_id=1, source_target_pairs={{1,0},{2,1},{3,2},{4,3},{5,4},{6,5},{7,6},{8,7},{9,8},{10,9},{11,1... | collective-permute-start | bytes 233480 | tf_op jit(solution)/shard_map/ppermute | solution.py:26
  15.3 2.2 %copy-start = (f32[32,32768]{1,0:T(8,128)S(1)}, f32[32,32768]{1,0:T(8,128)}, u32[]{:S(2)}) copy-start(f32[32,32768]{1,0:T(8,128)} %basis.3) | copy-start | bytes 12582916
  17.5 1.6 copy-start.4
  19.1 1.6 copy-start.6
  20.7 1.0 copy-start.9
  21.7 0.9 copy-start.10
  22.6 0.8 copy-start.12
  23.4 0.8 copy-start.13
  24.2 0.7 copy-start.14
  24.9 0.7 copy-start.16
  25.6 0.7 copy-start.21
  26.2 37.4 %copy-start.5 = (f32[16,32768]{1,0:T(8,128)S(1)}, f32[16,32768]{1,0:T(8,128)}, u32[]{:S(2)}) copy-start(f32[16,32768]{1,0:T(8,128)} %own_charge.1) | copy-start | bytes 6291460
  26.2 37.4 %copy-start.23 = (s32[512,16]{0,1:T(8,128)S(1)}, s32[512,16]{0,1:T(8,128)}, u32[]{:S(2)}) copy-start(s32[512,16]{0,1:T(8,128)} %param.19) | copy-start | bytes 98308
  55.1 1.8 copy-start.2
  56.9 96.8 %collective-permute-start = (f32[16,608]{1,0:T(8,128)S(1)}, f32[16,608]{1,0:T(8,128)S(1)}, u32[]{:S(2)}, u32[]{:S(2)}) collective-permute-start(f32[16,608]{1,0:T(8,128)S(1)} %get-tuple-element.14), channel_id=1, source_target_pairs={{0,1},{1,2},{2,3},{3,4},{4,5},{5,6},{6,7},{7,8},{8,9},{9,10},{10,1... | collective-permute-start | bytes 116744 | tf_op jit(solution)/shard_map/ppermute | solution.py:619
  58.9 94.8 %collective-permute-start.1 = (f32[16,608]{1,0:T(8,128)S(1)}, f32[16,608]{1,0:T(8,128)S(1)}, u32[]{:S(2)}, u32[]{:S(2)}) collective-permute-start(f32[16,608]{1,0:T(8,128)S(1)} %get-tuple-element.15), channel_id=1, source_target_pairs={{1,0},{2,1},{3,2},{4,3},{5,4},{6,5},{7,6},{8,7},{9,8},{10,9},{11,1... | collective-permute-start | bytes 116744 | tf_op jit(solution)/shard_map/ppermute | solution.py:620
  63.6 1.0 copy-start.17
  64.7 89.0 %copy-start.15 = (f32[32,96]{1,0:T(8,128)S(1)}, f32[32,96]{1,0:T(8,128)}, u32[]{:S(2)}) copy-start(f32[32,96]{1,0:T(8,128)} %prox_top.1) | copy-start | bytes 36868
  64.7 89.0 %copy-start.18 = (s32[128,3]{0,1:T(4,128)S(1)}, s32[128,3]{0,1:T(4,128)}, u32[]{:S(2)}) copy-start(s32[128,3]{0,1:T(4,128)} %param.28) | copy-start | bytes 4612
  64.7 89.0 %copy-start.19 = (s32[32,3]{0,1:T(4,128)S(1)}, s32[32,3]{0,1:T(4,128)}, u32[]{:S(2)}) copy-start(s32[32,3]{0,1:T(4,128)} %param.29) | copy-start | bytes 1156
  64.7 89.1 %copy-start.20 = (s32[8,3]{0,1:T(4,128)S(1)}, s32[8,3]{0,1:T(4,128)}, u32[]{:S(2)}) copy-start(s32[8,3]{0,1:T(4,128)} %param.30) | copy-start | bytes 292
  64.7 89.1 %copy-start.22 = (s32[128]{0:T(128)S(1)}, s32[128]{0:T(128)}, u32[]{:S(2)}) copy-start(s32[128]{0:T(128)} %tops.3) | copy-start | bytes 1540
  152.3 1.4 copy-start.7
  153.8 2.2 %copy-start.1 = (f32[32,32768]{1,0:T(8,128)S(1)}, f32[32,32768]{1,0:T(8,128)}, u32[]{:S(2)}) copy-start(f32[32,32768]{1,0:T(8,128)} %basis.3) | copy-start | bytes 12582916
  156.0 2.0 %copy-start.3 = (f32[7,1024,128]{2,1,0:T(8,128)S(1)}, f32[7,1024,128]{2,1,0:T(8,128)}, u32[]{:S(2)}) copy-start(f32[7,1024,128]{2,1,0:T(8,128)} %copy-done.2) | copy-start | bytes 11010052
  158.0 1.6 copy-start.8
  159.6 0.8 copy-start.11
Sparse Core Ops, SparseCore 0:
  57.1 87.3 all-reduce.1

commit v3 on v2

--- a/solution.py
+++ b/solution.py
@@ -56,7 +56,7 @@
 
 
 def near_kernel(
-    ids, own_jitter, own_charge, low_halo, high_halo, out, points, feats, charges, targets, kernels, weights
+    ids, own_jitter, own_charge, low_halo, high_halo, out, points, feats0, feats1, charges, targets0, targets1, kernels, weights
 ):
     halo_tiles = low_halo.shape[1] // 128
     own_tiles = own_jitter.shape[1] // 128
@@ -75,10 +75,8 @@
         number = tile + (here * own_tiles - halo_tiles)
         across, beside = column_place(number >> 1)
         beside = beside + (2 * (number & 1)).astype(f32)
-        points[0:1, lanes_of(tile)] = across + place[0:1]
-        points[1:2, lanes_of(tile)] = (beside + high_side) + place[1:2]
-        points[2:3, lanes_of(tile)] = place[2:3]
-        points[3:8, lanes_of(tile)] = jnp.zeros((5, 128), f32)
+        centre = jnp.where(row == 0, across, jnp.where(row == 1, beside + high_side, 0.0))
+        points[:, lanes_of(tile)] = centre + jnp.concatenate([place, jnp.zeros((5, 128), f32)], 0)
         charge = charge * inv_four_pi
         charges[2 * tile] = jnp.concatenate(split_two(charge), 0)
         charges[2 * tile + 1] = jnp.concatenate(split_two(pltpu.roll(charge, 64, 1)), 0)
@@ -112,10 +110,10 @@
             place = pl.ds(pl.multiple_of((first + 2 * half) * LEAF, 128), 128)
             out[:, place] = jnp.concatenate([parts[2 * half], parts[2 * half + 1]], 1)
 
-    def do_group(group, carry):
+    def fill(group, feats, targets, part, part_count):
         base = group * GROUP
         across, beside = column_place(((first_id + NREACH) >> 2) + group * (GROUP // 4))
-        row_sign = jnp.where(((first_id + NREACH + base) >> 8) % 2 == 0, 1.5, -1.5)
+        row_sign = jnp.where((((first_id + NREACH + base) >> 8) & 1) == 0, 1.5, -1.5)
         shift = jnp.where(row == 0, across + row_sign, jnp.where(row == 1, beside + 1.5, 0.0))
 
         def local(tile):
@@ -123,7 +121,7 @@
             square = place * place
             return place, jnp.broadcast_to(square[0:1] + square[1:2] + square[2:3], (8, 128))
 
-        def source_rows(i, carry):
+        def source_rows(i):
             place, square = local(base // 2 + i)
             rows = place * (-2.0) + jnp.where(is_three, square + soft_square, one_four)
 
@@ -136,9 +134,8 @@
 
             put(2 * i, rows)
             put(2 * i + 1, pltpu.roll(rows, 64, 1))
-            return carry
-
-        def target_rows(i, carry):
+
+        def target_rows(i):
             place, square = local(base // 2 + NREACH // 2 + i)
             first, second, third = split_three(place + jnp.where(is_four, square, one_three))
             one = jnp.where(below_five, first, pltpu.roll(first, 5, 0))
@@ -146,40 +143,54 @@
             three = jnp.where(below_five, jnp.where(is_four, third, first), pltpu.roll(third, 5, 0))
             rows = jnp.concatenate([one, two, three, jnp.zeros_like(one)], 0)
             targets[lanes_of(i), :] = jnp.transpose(rows).astype(bf16)
-            return carry
-
-        lax.fori_loop(0, (GROUP + 2 * NREACH) // 2, source_rows, 0, unroll=True)
-        lax.fori_loop(0, GROUP // 2, target_rows, 0, unroll=True)
-
-        def front(leaf, slot):
-            target = targets[pl.ds(pl.multiple_of(leaf * LEAF, LEAF), LEAF), :]
-            entry = base + leaf
-            for j in range(4):
-                sides = []
-                for h in range(2):
-                    one = ids[4 * j + 2 * h, entry] - first_id
-                    two = (ids[4 * j + 2 * h + 1, entry] - first_id) ^ 1
-                    sides.append(jnp.where(left_half, feats[one - base], feats[two - base]))
-                    weights[slot, :, (2 * j + h) * 128 : (2 * j + h + 1) * 128] = jnp.where(
-                        left_half, charges[one], charges[two]
-                    )
-                square = jnp.dot(target, jnp.concatenate(sides, 1), preferred_element_type=f32)
-                high, low = split_two(lax.rsqrt(square))
-                kernels[slot, 0:LEAF, j * 256 : (j + 1) * 256] = high
-                kernels[slot, LEAF : 2 * LEAF, j * 256 : (j + 1) * 256] = low
-
-        def step(i, carry):
-            emit(base + BATCH * i - BATCH)
-            for slot in range(BATCH):
-                front(BATCH * i + slot, slot)
-            return carry
-
-        lax.fori_loop(0, GROUP // BATCH, step, 0)
+
+        sources = (GROUP + 2 * NREACH) // 2 // part_count
+        for i in range(sources):
+            source_rows(part * sources + i)
+        own = GROUP // 2 // part_count
+        for i in range(own):
+            target_rows(part * own + i)
+
+    def front(base, leaf, slot, feats, targets):
+        target = targets[pl.ds(pl.multiple_of(leaf * LEAF, LEAF), LEAF), :]
+        entry = base + leaf
+        for j in range(4):
+            sides = []
+            for h in range(2):
+                one = ids[4 * j + 2 * h, entry] - first_id
+                two = (ids[4 * j + 2 * h + 1, entry] - first_id) ^ 1
+                sides.append(jnp.where(left_half, feats[one - base], feats[two - base]))
+                weights[slot, :, (2 * j + h) * 128 : (2 * j + h + 1) * 128] = jnp.where(
+                    left_half, charges[one], charges[two]
+                )
+            square = jnp.dot(target, jnp.concatenate(sides, 1), preferred_element_type=f32)
+            high, low = split_two(lax.rsqrt(square))
+            kernels[slot, 0:LEAF, j * 256 : (j + 1) * 256] = high
+            kernels[slot, LEAF : 2 * LEAF, j * 256 : (j + 1) * 256] = low
+
+    group_count = own_tiles * 2 // GROUP
+
+    def do_two_groups(i, carry):
+        for half in range(2):
+            now = (feats0, targets0) if half == 0 else (feats1, targets1)
+            later = (feats1, targets1) if half == 0 else (feats0, targets0)
+            group = 2 * i + half
+            following = jnp.minimum(group + 1, group_count - 1)
+
+            def step(part, inner):
+                emit(group * GROUP + BATCH * part - BATCH)
+                for slot in range(BATCH):
+                    front(group * GROUP, BATCH * part + slot, slot, *now)
+                fill(following, *later, part, GROUP // BATCH)
+                return inner
+
+            lax.fori_loop(0, GROUP // BATCH, step, 0)
         return carry
 
     kernels[...] = jnp.zeros_like(kernels)
     weights[...] = jnp.zeros_like(weights)
-    lax.fori_loop(0, own_tiles * 2 // GROUP, do_group, 0)
+    fill(0, feats0, targets0, 0, 1)
+    lax.fori_loop(0, group_count // 2, do_two_groups, 0)
     emit(own_tiles * 2 - BATCH)
 
 
@@ -197,12 +208,14 @@
         scratch_shapes=[
             pltpu.VMEM((8, leaves * LEAF), f32),
             pltpu.VMEM((GROUP + 2 * NREACH, 32, 128), bf16),
+            pltpu.VMEM((GROUP + 2 * NREACH, 32, 128), bf16),
             pltpu.VMEM((leaves, 2 * R, 128), bf16),
+            pltpu.VMEM((GROUP * LEAF, 32), bf16),
             pltpu.VMEM((GROUP * LEAF, 32), bf16),
             pltpu.VMEM((BATCH, 2 * LEAF, 16 * LEAF), bf16),
             pltpu.VMEM((BATCH, 2 * R, 16 * LEAF), bf16),
         ],
-        compiler_params=pltpu.CompilerParams(vmem_limit_bytes=40 * 2**20),
+        compiler_params=pltpu.CompilerParams(vmem_limit_bytes=16 * 2**20),
         cost_estimate=pl.CostEstimate(
             flops=pairs * 192, bytes_accessed=panels * 160, transcendentals=pairs
         ),
@@ -211,6 +224,7 @@
 
 
 EDGE = 16
+CHUNKS = 4
 ROWS = R * K
 WIDE = ROWS + 3 * K
 
@@ -220,8 +234,11 @@
     return index >> 5, (index >> 3) & 3, index & 7
 
 
-def matvec(matrix, vector, out, add):
-    for_rows = 4
+def lane_of_tile(tile):
+    return (tile & 3) * 32 + ((tile >> 2) & 3) * 8 + (tile >> 4)
+
+
+def matvec(matrix, vector, out, add, for_rows=4):
 
     def step(block, carry):
         start = pl.multiple_of(block * for_rows * K, for_rows * K)
@@ -259,8 +276,8 @@
 
 
 def up_kernel(
-    tops, basis, charge, trans0, trans1, trans2, trans3, prox1, prox2, prox3,
-    et, payload, last_out, first_out, terms, leaf_rows, coef0, coef, flipped, columns,
+    tops, basis_hbm, charge_hbm, trans0_hbm, trans1, trans2, trans3, prox1, prox2, prox3,
+    et, payload, last_out, first_out, terms, leaf_rows, coef0, coef, flipped, columns, by_column, basis, charge, trans0, sems,
 ):
     here = lax.axis_index("gx")
     quarter = lax.broadcasted_iota(jnp.int32, (R, 256), 1).astype(f32)
@@ -277,22 +294,32 @@
         highs = jnp.concatenate([p[0] for p in pieces], 0)
         lows = jnp.concatenate([p[1] for p in pieces], 0)
         left = jnp.concatenate([highs, highs, lows], 1)
-        leaf_rows[pl.ds(pl.multiple_of(tile * 64, 64), 64), 0:K] = lax.dot_general(
-            left, right, (((1,), (1,)), ((), ())), preferred_element_type=f32
-        )
-        return carry
-
-    lax.fori_loop(0, basis.shape[1] // 256, moments, 0, unroll=4)
+        total = lax.dot_general(left, right, (((1,), (1,)), ((), ())), preferred_element_type=f32)
+        total = jnp.concatenate([total, jnp.zeros((64, 128 - K), f32)], 1)
+        leaf_rows[pl.ds(lane_of_tile(tile), 64, stride=128), :] = total
+        return carry
+
+    tiles = basis.shape[1] // 256
+    chunk = basis.shape[1] // CHUNKS
+    copies = []
+    for i in range(CHUNKS):
+        lanes = pl.ds(i * chunk, chunk)
+        copies.append(pltpu.make_async_copy(basis_hbm.at[:, lanes], basis.at[:, lanes], sems.at[2 * i]))
+        copies.append(pltpu.make_async_copy(charge_hbm.at[:, lanes], charge.at[:, lanes], sems.at[2 * i + 1]))
+    copies.append(pltpu.make_async_copy(trans0_hbm, trans0, sems.at[2 * CHUNKS]))
+    for copy in copies:
+        copy.start()
+    for i in range(CHUNKS):
+        copies[2 * i].wait()
+        copies[2 * i + 1].wait()
+        lax.fori_loop(i * tiles // CHUNKS, (i + 1) * tiles // CHUNKS, moments, 0, unroll=4)
+    copies[2 * CHUNKS].wait()
 
     def leaf_coefs(r, carry):
         place = pl.ds(pl.multiple_of(r * K, K), K)
         for j0 in range(4):
-            parts = [
-                leaf_rows[pl.ds((j2 * 16 + j1 * 4 + j0) * R + r, 8, stride=64 * R), :]
-                for j1 in range(4)
-                for j2 in range(4)
-            ]
-            coef0[j0, place, :] = jnp.transpose(jnp.concatenate(parts, 0))[0:K]
+            rows = leaf_rows[pl.ds(pl.multiple_of((j0 * R + r) * 128, 128), 128), :]
+            coef0[j0, place, :] = jnp.transpose(rows)[0:K]
         return carry
 
     lax.fori_loop(0, R, leaf_coefs, 0, unroll=2)
@@ -318,7 +345,9 @@
     flip(trans3, [(6, (0, 0, 0, 1))])
 
     def lift_from(entry, vector, out, add):
-        matvec(lambda b: et[entry, pl.ds(b, K, stride=K), :], vector, out, add)
+        for b in range(K):
+            by_column[b * K : (b + 1) * K, :] = et[entry, pl.ds(b, K, stride=K), :]
+        matvec(lambda b: by_column[b * K : (b + 1) * K, :], vector, out, add)
 
     for j0 in range(4):
         lift_from(j0, coef0.at[j0], coef.at[0], j0 > 0)
@@ -390,7 +419,7 @@
             jax.ShapeDtypeStruct((EDGE, WIDE), f32),
             jax.ShapeDtypeStruct((top_count, ROWS), f32),
         ],
-        in_specs=[smem] + [vmem] * 9,
+        in_specs=[smem] + [pl.BlockSpec(memory_space=pltpu.HBM)] * 3 + [vmem] * 6,
         out_specs=[vmem] * 5,
         scratch_shapes=[
             pltpu.VMEM((leaves * R, 128), f32),
@@ -398,8 +427,13 @@
             pltpu.VMEM((4, ROWS, 128), f32),
             pltpu.VMEM((128, 640), f32),
             pltpu.VMEM((8, leaves, 128), f32),
+            pltpu.VMEM((K * K, 128), f32),
+            pltpu.VMEM(basis.shape, f32),
+            pltpu.VMEM(charge.shape, f32),
+            pltpu.VMEM(trans0.shape, f32),
+            pltpu.SemaphoreType.DMA((2 * CHUNKS + 1,)),
         ],
-        compiler_params=pltpu.CompilerParams(vmem_limit_bytes=40 * 2**20),
+        compiler_params=pltpu.CompilerParams(vmem_limit_bytes=54 * 2**20),
         cost_estimate=pl.CostEstimate(
             flops=leaves * 200000, bytes_accessed=leaves * 20000, transcendentals=0
         ),
@@ -597,7 +631,7 @@
             pltpu.VMEM((panels // LEAF * R, 128), f32),
             pltpu.VMEM((128, 128), f32),
         ],
-        compiler_params=pltpu.CompilerParams(vmem_limit_bytes=40 * 2**20),
+        compiler_params=pltpu.CompilerParams(vmem_limit_bytes=16 * 2**20),
         cost_estimate=pl.CostEstimate(
             flops=panels * 4000, bytes_accessed=panels * 400, transcendentals=panels * 20
         ),

time: 203 us -> 181 us (0.89)
  local copies, waits for them, and re-layouts: 23.4 us -> 10.7 us
  Pallas kernels: 151 us -> 143 us
    unnamed x48 -> x28, local copies, waits for them, and re-layouts: 21.8 us -> 9.1 us
    pallas_call x1, Pallas kernels: 87.6 us -> 80.6 us  [near_potential(): pl.pallas_call(near_kernel, out_shape=jax.ShapeDtypeStruct((R, panels), f...]
  transfers between devices with their start and end apart: 5 -> 5, of which waited for: 0 -> 0; matrix products, arithmetic and copies ran while one was open for 0% -> 0% of each run, Pallas kernels for 58% -> 60%
where the time goes in v3:
time: 181 us; the launch traced here: 180 us
  Pallas kernels  143 us (79%)
  between operations  13.6 us (8%)
  starting transfers between devices  13.1 us (7%)
  local copies, waits for them, and re-layouts  10.7 us (6%)
    pallas_call x1, Pallas kernels, near_potential(): pl.pallas_call(near_kernel, out_shape=jax.ShapeDtypeStruct((R, panels), f...  80.6 us
    pallas_call x1, Pallas kernels, downward_pass(): pl.pallas_call(down_kernel, out_shape=jax.ShapeDtypeStruct((R, panels), f...  35 us
    pallas_call x1, Pallas kernels, upward_pass(): pl.pallas_call(up_kernel, out_shape=[jax.ShapeDtypeStruct((7, K * K, 128)...  27.3 us
    unnamed x28, local copies, waits for them, and re-layouts  9.1 us
    ppermute x1, starting transfers between devices, body(): high_halo = lax.ppermute(first, 'gx', backward)  4.72 us
    ppermute x1, starting transfers between devices, leaf_halos(): lax.ppermute(first, 'gx', backward)  4.54 us
  transfers between devices with their start and end apart: 5, of which 0 were waited for; matrix products, arithmetic and copies ran while one was open for 0% of the time, Pallas kernels for 60%

profile of v3, /device:TPU:8, one launch (start us, length us, event | category | flops | bytes accessed | tf_op | source)
XLA Modules:
  0.0 180.4 jit_solution(18106666917020028584)
XLA Ops:
  6.5 0.0 all-reduce.2.cloned.1.call-start
  6.5 0.7 fusion.1
  7.3 0.9 fusion
  8.2 1.9 %collective-permute-start.2 = (f32[19,1024]{1,0:T(8,128)S(1)}, f32[19,1024]{1,0:T(8,128)S(1)}, u32[]{:S(2)}, u32[]{:S(2)}) collective-permute-start(f32[19,1024]{1,0:T(8,128)S(1)} %pad_maximum_fusion), channel_id=1, source_target_pairs={{0,1},{1,2},{2,3},{3,4},{4,5},{5,6},{6,7},{7,8},{8,9},{9,10},{10,1... | collective-permute-start | bytes 233480 | tf_op jit(solution)/shard_map/ppermute | solution.py:26
  10.1 4.5 %collective-permute-start.3 = (f32[19,1024]{1,0:T(8,128)S(1)}, f32[19,1024]{1,0:T(8,128)S(1)}, u32[]{:S(2)}, u32[]{:S(2)}) collective-permute-start(f32[19,1024]{1,0:T(8,128)S(1)} %pad_maximum_fusion.1), channel_id=1, source_target_pairs={{1,0},{2,1},{3,2},{4,3},{5,4},{6,5},{7,6},{8,7},{9,8},{10,9},{11,1... | collective-permute-start | bytes 233480 | tf_op jit(solution)/shard_map/ppermute | solution.py:26
  14.7 0.0 copy-start.2
  14.7 0.0 copy-start.13
  14.7 27.3 %upward_pass.1 = (f32[7,1024,128]{2,1,0:T(8,128)}, f32[3,608,128]{2,1,0:T(8,128)}, f32[16,608]{1,0:T(8,128)}, f32[16,608]{1,0:T(8,128)}, f32[32,512]{1,0:T(8,128)}) custom-call(s32[128]{0:T(128)} %tops.3, f32[32,32768]{1,0:T(8,128)} %basis.1, f32[16,32768]{1,0:T(8,128)} %own_charge.1, f32[512,1024]{1,0:T(8,128)} %trans0_hbm.1, f32[128,1024]{1,0:T(8,128)} %trans1.1, ...), custom_call_target="tpu_custom_call" | custom-call | flops 102400000 | bytes 10240000 | tf_op jit(solution)/shard_map/upward_pass/pallas_call | solution.py:413
  42.0 0.0 all-reduce.2.cloned.1.call-update
  42.0 1.9 %collective-permute-start = (f32[16,608]{1,0:T(8,128)}, f32[16,608]{1,0:T(8,128)S(1)}, u32[]{:S(2)}, u32[]{:S(2)}) collective-permute-start(f32[16,608]{1,0:T(8,128)} %get-tuple-element.14), channel_id=1, source_target_pairs={{0,1},{1,2},{2,3},{3,4},{4,5},{5,6},{6,7},{7,8},{8,9},{9,10},{10,1... | collective-permute-start | bytes 116744 | tf_op jit(solution)/shard_map/ppermute | solution.py:653
  44.0 4.7 %collective-permute-start.1 = (f32[16,608]{1,0:T(8,128)}, f32[16,608]{1,0:T(8,128)S(1)}, u32[]{:S(2)}, u32[]{:S(2)}) collective-permute-start(f32[16,608]{1,0:T(8,128)} %get-tuple-element.15), channel_id=1, source_target_pairs={{1,0},{2,1},{3,2},{4,3},{5,4},{6,5},{7,6},{8,7},{9,8},{10,9},{11,1... | collective-permute-start | bytes 116744 | tf_op jit(solution)/shard_map/ppermute | solution.py:654
  48.7 0.0 collective-permute-done.2.low_halo
  48.7 0.0 collective-permute-done.3.high_halo
  48.7 0.0 copy-done.2
  48.7 0.0 copy-done.13
  48.7 0.0 copy-start.8
  48.7 1.0 copy-done.8
  49.8 0.0 copy-start.5
  49.8 0.0 copy-start.7
  49.8 0.0 copy-start.9
  49.8 0.0 copy-start.10
  49.8 0.0 copy-start.11
  49.8 0.0 copy-start.12
  49.8 80.6 %near_potential.1.near_field = f32[16,32768]{1,0:T(8,128)S(1)} custom-call(s32[16,512]{1,0:T(8,128)S(1)} %bitcast.8, f32[3,32768]{1,0:T(4,128)S(1)} %copy-done.8, f32[16,32768]{1,0:T(8,128)S(1)} %copy-done.2, f32[19,1024]{1,0:T(8,128)S(1)} %collective-permute-done.2.low_halo, f32[19,1024]{1,0:T(8,128)S(1)} %collective-permute-done.3.high_halo), custom_call_target="tpu_custom_call" | custom-call | flops 6442450944 | bytes 5242880 | tf_op jit(solution)/shard_map/near_potential/pallas_call | solution.py:203
  130.4 0.0 copy-start.3
  130.4 1.4 copy-done.3
  131.8 0.0 all-reduce.2.cloned.1.call-done.coef_top
  131.8 0.0 collective-permute-done.low_halo
  131.8 0.0 collective-permute-done.1.high_halo
  131.8 0.0 copy-done.5
  131.8 0.0 copy-done.7
  131.8 0.0 copy-done.9
  131.8 0.0 copy-done.10
  131.8 0.0 copy-done.11
  131.8 0.0 copy-done.12
  131.8 0.0 copy-start
  131.8 2.2 %copy-done = f32[32,32768]{1,0:T(8,128)S(1)} copy-done((f32[32,32768]{1,0:T(8,128)S(1)}, f32[32,32768]{1,0:T(8,128)}, u32[]{:S(2)}) %copy-start) | copy-done | bytes 4194328
  134.0 0.0 copy-start.1
  134.0 2.0 %copy-done.1 = f32[7,1024,128]{2,1,0:T(8,128)S(1)} copy-done((f32[7,1024,128]{2,1,0:T(8,128)S(1)}, f32[7,1024,128]{2,1,0:T(8,128)}, u32[]{:S(2)}) %copy-start.1) | copy-done | bytes 3670040
  136.1 0.0 copy-start.4
  136.1 1.6 copy-done.4
  137.7 0.0 copy-start.6
  137.7 0.8 copy-done.6
  138.5 35.0 %downward_pass.1 = f32[16,32768]{1,0:T(8,128)} custom-call(s32[128]{0:T(128)S(1)} %copy-done.12, f32[7,1024,128]{2,1,0:T(8,128)S(1)} %copy-done.1, f32[3,608,128]{2,1,0:T(8,128)S(1)} %copy-done.5, f32[16,608]{1,0:T(8,128)S(1)} %collective-permute-done.low_halo, f32[16,608]{1,0:T(8,128)S(1)} %collective-permute-done.1.high_halo, f32[32,512]{1,0:T(8,128)S(1)} %copy-done.6, ...), custom_call_target="tpu_custom_call" | custom-call | flops 131072000 | bytes 13107200 | tf_op jit(solution)/shard_map/downward_pass/pallas_call | solution.py:619
  (2 shorter events, 0.0 us)
Async XLA Ops:
  6.5 125.2 %all-reduce.2.cloned.1.call-start = ((), (), s32[]{:S(2)}) async-start(), calls=%async_computation | async-start | bytes 131072 | tf_op jit(solution)/shard_map/psum | solution.py:655
  8.2 40.5 %collective-permute-start.2 = (f32[19,1024]{1,0:T(8,128)S(1)}, f32[19,1024]{1,0:T(8,128)S(1)}, u32[]{:S(2)}, u32[]{:S(2)}) collective-permute-start(f32[19,1024]{1,0:T(8,128)S(1)} %pad_maximum_fusion), channel_id=1, source_target_pairs={{0,1},{1,2},{2,3},{3,4},{4,5},{5,6},{6,7},{7,8},{8,9},{9,10},{10,1... | collective-permute-start | bytes 233480 | tf_op jit(solution)/shard_map/ppermute | solution.py:26
  10.1 38.6 %collective-permute-start.3 = (f32[19,1024]{1,0:T(8,128)S(1)}, f32[19,1024]{1,0:T(8,128)S(1)}, u32[]{:S(2)}, u32[]{:S(2)}) collective-permute-start(f32[19,1024]{1,0:T(8,128)S(1)} %pad_maximum_fusion.1), channel_id=1, source_target_pairs={{1,0},{2,1},{3,2},{4,3},{5,4},{6,5},{7,6},{8,7},{9,8},{10,9},{11,1... | collective-permute-start | bytes 233480 | tf_op jit(solution)/shard_map/ppermute | solution.py:26
  14.7 34.0 %copy-start.2 = (f32[16,32768]{1,0:T(8,128)S(1)}, f32[16,32768]{1,0:T(8,128)}, u32[]{:S(2)}) copy-start(f32[16,32768]{1,0:T(8,128)} %own_charge.1) | copy-start | bytes 6291460
  14.7 34.0 %copy-start.13 = (s32[512,16]{0,1:T(8,128)S(1)}, s32[512,16]{0,1:T(8,128)}, u32[]{:S(2)}) copy-start(s32[512,16]{0,1:T(8,128)} %param.19) | copy-start | bytes 98308
  42.0 89.7 %collective-permute-start = (f32[16,608]{1,0:T(8,128)}, f32[16,608]{1,0:T(8,128)S(1)}, u32[]{:S(2)}, u32[]{:S(2)}) collective-permute-start(f32[16,608]{1,0:T(8,128)} %get-tuple-element.14), channel_id=1, source_target_pairs={{0,1},{1,2},{2,3},{3,4},{4,5},{5,6},{6,7},{7,8},{8,9},{9,10},{10,1... | collective-permute-start | bytes 116744 | tf_op jit(solution)/shard_map/ppermute | solution.py:653
  44.0 87.8 %collective-permute-start.1 = (f32[16,608]{1,0:T(8,128)}, f32[16,608]{1,0:T(8,128)S(1)}, u32[]{:S(2)}, u32[]{:S(2)}) collective-permute-start(f32[16,608]{1,0:T(8,128)} %get-tuple-element.15), channel_id=1, source_target_pairs={{1,0},{2,1},{3,2},{4,3},{5,4},{6,5},{7,6},{8,7},{9,8},{10,9},{11,1... | collective-permute-start | bytes 116744 | tf_op jit(solution)/shard_map/ppermute | solution.py:654
  48.7 1.0 copy-start.8
  49.8 82.0 %copy-start.5 = (f32[3,608,128]{2,1,0:T(8,128)S(1)}, f32[3,608,128]{2,1,0:T(8,128)}, u32[]{:S(2)}) copy-start(f32[3,608,128]{2,1,0:T(8,128)} %get-tuple-element.13.payload) | copy-start | bytes 2801668
  49.8 82.0 %copy-start.7 = (f32[32,96]{1,0:T(8,128)S(1)}, f32[32,96]{1,0:T(8,128)}, u32[]{:S(2)}) copy-start(f32[32,96]{1,0:T(8,128)} %prox_top.1) | copy-start | bytes 36868
  49.8 82.0 %copy-start.9 = (s32[128,3]{0,1:T(4,128)S(1)}, s32[128,3]{0,1:T(4,128)}, u32[]{:S(2)}) copy-start(s32[128,3]{0,1:T(4,128)} %param.28) | copy-start | bytes 4612
  49.8 82.0 %copy-start.10 = (s32[32,3]{0,1:T(4,128)S(1)}, s32[32,3]{0,1:T(4,128)}, u32[]{:S(2)}) copy-start(s32[32,3]{0,1:T(4,128)} %param.29) | copy-start | bytes 1156
  49.8 82.0 %copy-start.11 = (s32[8,3]{0,1:T(4,128)S(1)}, s32[8,3]{0,1:T(4,128)}, u32[]{:S(2)}) copy-start(s32[8,3]{0,1:T(4,128)} %param.30) | copy-start | bytes 292
  49.8 82.0 %copy-start.12 = (s32[128]{0:T(128)S(1)}, s32[128]{0:T(128)}, u32[]{:S(2)}) copy-start(s32[128]{0:T(128)} %tops.3) | copy-start | bytes 1540
  130.4 1.4 copy-start.3
  131.8 2.2 %copy-start = (f32[32,32768]{1,0:T(8,128)S(1)}, f32[32,32768]{1,0:T(8,128)}, u32[]{:S(2)}) copy-start(f32[32,32768]{1,0:T(8,128)} %basis.1) | copy-start | bytes 12582916
  134.0 2.0 %copy-start.1 = (f32[7,1024,128]{2,1,0:T(8,128)S(1)}, f32[7,1024,128]{2,1,0:T(8,128)}, u32[]{:S(2)}) copy-start(f32[7,1024,128]{2,1,0:T(8,128)} %get-tuple-element.12.et) | copy-start | bytes 11010052
  136.1 1.6 copy-start.4
  137.7 0.8 copy-start.6
Sparse Core Ops, SparseCore 0:
  42.2 87.4 all-reduce.1

commit v4 on v3

--- a/solution.py
+++ b/solution.py
@@ -276,8 +276,8 @@
 
 
 def up_kernel(
-    tops, basis_hbm, charge_hbm, trans0_hbm, trans1, trans2, trans3, prox1, prox2, prox3,
-    et, payload, last_out, first_out, terms, leaf_rows, coef0, coef, flipped, columns, by_column, basis, charge, trans0, sems,
+    basis_hbm, charge_hbm, trans0_hbm, trans1, trans2, trans3, prox1, prox2, prox3,
+    et, payload, last_out, first_out, lifted, leaf_rows, coef0, coef, flipped, columns, by_column, basis, charge, trans0, sems,
 ):
     here = lax.axis_index("gx")
     quarter = lax.broadcasted_iota(jnp.int32, (R, 256), 1).astype(f32)
@@ -312,7 +312,7 @@
     for i in range(CHUNKS):
         copies[2 * i].wait()
         copies[2 * i + 1].wait()
-        lax.fori_loop(i * tiles // CHUNKS, (i + 1) * tiles // CHUNKS, moments, 0, unroll=4)
+        lax.fori_loop(i * tiles // CHUNKS, (i + 1) * tiles // CHUNKS, moments, 0, unroll=8)
     copies[2 * CHUNKS].wait()
 
     def leaf_coefs(r, carry):
@@ -399,16 +399,11 @@
             last_out[target : target + 1, :] = flipped[last_rows[level][i] : last_rows[level][i] + 1, 0:WIDE]
             first_out[target : target + 1, :] = flipped[first_rows[level][i] : first_rows[level][i] + 1, 0:WIDE]
     flip_payload(coef.at[3], ROWS)
-    top_ids = lax.broadcasted_iota(jnp.int32, (terms.shape[0], ROWS), 0)
-    total = jnp.zeros(terms.shape, f32)
-    for c in range(8):
-        total = total + jnp.where(top_ids == tops[here * 8 + c], flipped[c : c + 1, 0:ROWS], 0.0)
-    terms[...] = total
-
-
-def upward_pass(tops, basis, charge, trans0, trans1, trans2, trans3, prox1, prox2, prox3, top_count):
+    lifted[...] = flipped[0:8, 0:ROWS]
+
+
+def upward_pass(basis, charge, trans0, trans1, trans2, trans3, prox1, prox2, prox3):
     vmem = pl.BlockSpec(memory_space=pltpu.VMEM)
-    smem = pl.BlockSpec(memory_space=pltpu.SMEM)
     leaves = trans0.shape[0]
     return pl.pallas_call(
         up_kernel,
@@ -417,9 +412,9 @@
             jax.ShapeDtypeStruct((3, WIDE, 128), f32),
             jax.ShapeDtypeStruct((EDGE, WIDE), f32),
             jax.ShapeDtypeStruct((EDGE, WIDE), f32),
-            jax.ShapeDtypeStruct((top_count, ROWS), f32),
+            jax.ShapeDtypeStruct((8, ROWS), f32),
         ],
-        in_specs=[smem] + [pl.BlockSpec(memory_space=pltpu.HBM)] * 3 + [vmem] * 6,
+        in_specs=[pl.BlockSpec(memory_space=pltpu.HBM)] * 3 + [vmem] * 6,
         out_specs=[vmem] * 5,
         scratch_shapes=[
             pltpu.VMEM((leaves * R, 128), f32),
@@ -438,15 +433,23 @@
             flops=leaves * 200000, bytes_accessed=leaves * 20000, transcendentals=0
         ),
         name="upward_pass",
-    )(tops, basis, charge, trans0, trans1, trans2, trans3, prox1, prox2, prox3)
+    )(basis, charge, trans0, trans1, trans2, trans3, prox1, prox2, prox3)
 
 
 def down_kernel(
-    tops, et, payload, low_halo, high_halo, coef_top, prox_top, list1, list2, list3, basis, near_field,
-    out, split_rows, split_top, gathered, green_rows, local, leaf_local, leaf_rows, columns,
+    tops, et_hbm, payload, low_halo, high_halo, lifted, top_row, prox_top, list1, list2, list3, basis_hbm, near_hbm,
+    out, split_rows, split_top, split_place, top_column, gathered, green_rows, local, leaf_local, leaf_rows, columns,
+    et, basis, near_field, sems,
 ):
+    copies = [
+        pltpu.make_async_copy(et_hbm, et, sems.at[0]),
+        pltpu.make_async_copy(basis_hbm, basis, sems.at[1]),
+        pltpu.make_async_copy(near_hbm, near_field, sems.at[2]),
+    ]
+    for copy in copies:
+        copy.start()
     here = lax.axis_index("gx")
-    top_count = coef_top.shape[0]
+    top_count = prox_top.shape[0]
     j1, j2, c3 = lane_digits((1, 128), 1)
 
     def split_to(ref, columns, value):
@@ -478,38 +481,44 @@
     my_top = jnp.zeros((1, 128), jnp.int32)
     for c in range(8):
         my_top = jnp.where(c3 == c, tops[here * 8 + c], my_top)
+    def flip_top(block):
+        rows, width = block.shape
+        if width < 128:
+            block = jnp.concatenate([block, jnp.zeros((rows, 128 - width), f32)], 1)
+        if rows < 128:
+            block = jnp.concatenate([block, jnp.zeros((128 - rows, 128), f32)], 0)
+        return jnp.transpose(block)
+
+    def keep(ref, first, q, value):
+        parts = split_three(value)
+        for i in range(3):
+            ref[i, first : first + value.shape[0], q : q + 128] = parts[i].astype(bf16)
+
+    cluster_count = lifted.shape[0]
     for q in range(0, split_top.shape[2], 128):
-        rows = min(128, top_count - q)
-
-        def flip_top(block):
-            if block.shape[1] < 128:
-                block = jnp.concatenate([block, jnp.zeros((rows, 128 - block.shape[1]), f32)], 1)
-            if rows < 128:
-                block = jnp.concatenate([block, jnp.zeros((128 - rows, 128), f32)], 0)
-            return jnp.transpose(block)
-
-        def keep_top(first, value):
-            parts = split_three(value)
-            for i in range(3):
-                split_top[i, first : first + value.shape[0], q : q + 128] = parts[i].astype(bf16)
-
+        rows = min(128, cluster_count - q)
         for w in range(0, ROWS, 128):
-            keep_top(w, flip_top(coef_top[q : q + rows, w : w + 128]))
-        offsets = flip_top(prox_top[q : q + rows, :])
+            keep(split_top, w, q, flip_top(lifted[q : q + rows, w : w + 128]))
+        owners = top_row[:, q : q + rows].astype(f32)
+        if rows < 128:
+            owners = jnp.concatenate([owners, jnp.full((1, 128 - rows), -9.0, f32)], 1)
+        top_column[q : q + 128, :] = jnp.transpose(jnp.broadcast_to(owners, (128, 128))).astype(jnp.int32)
+    for q in range(0, split_place.shape[2], 128):
+        offsets = flip_top(prox_top[q : q + min(128, top_count - q), :])
         across, beside = centre_lanes(lax.broadcasted_iota(jnp.int32, (1, 128), 1) + q, 64)
-        keep_top(ROWS, across + 64.0 * offsets[0:K])
-        keep_top(ROWS + K, beside + 4.0 * offsets[K : 2 * K])
-        keep_top(ROWS + 2 * K, offsets[2 * K : 3 * K])
-    top_rows = lax.broadcasted_iota(jnp.int32, (split_top.shape[2], 128), 0)
-    targets = pick(split_top.at[:, ROWS:WIDE, :], top_rows == my_top)
-    leaf_local[0, 0 : 3 * K, :] = targets
+        keep(split_place, 0, q, across + 64.0 * offsets[0:K])
+        keep(split_place, K, q, beside + 4.0 * offsets[K : 2 * K])
+        keep(split_place, 2 * K, q, offsets[2 * K : 3 * K])
+    top_rows = lax.broadcasted_iota(jnp.int32, (split_place.shape[2], 128), 0)
+    leaf_local[0, 0 : 3 * K, :] = pick(split_place, top_rows == my_top)
     lane_block = lax.broadcasted_iota(jnp.int32, (1, 128), 1) >> 3
     local[0] = jnp.zeros((ROWS, 128), f32)
 
     def top_block(block, carry):
         source = block * 16 + lane_block
-        far = jnp.abs(source - my_top) >= 2
-        gathered[...] = pick(split_top, (top_rows == jnp.where(far, source, -1)))
+        wanted = jnp.where(jnp.abs(source - my_top) >= 2, source, -1)
+        gathered[0:ROWS, :] = pick(split_top, top_column[...] == wanted)
+        gathered[ROWS:WIDE, :] = pick(split_place, top_rows == wanted)
         couple_picked(lambda axis_id: leaf_local[0, axis_id * K : (axis_id + 1) * K, :], local.at[0], True)
         return carry
 
@@ -557,6 +566,7 @@
     gathered[...] = pick(split_rows, source_ids(2, s3, 8, 8) == wanted)
     couple_picked(place_of(2), local.at[1], False)
     fold(local.at[1], (8, 16))
+    copies[0].wait()
     descend_from(6, local.at[0], local.at[1], True)
 
     picked = lane_list(list2, (0, 1, 4), here * 32)
@@ -580,9 +590,9 @@
     def leaf_terms(r, carry):
         place = pl.ds(pl.multiple_of(r * K, K), K)
         for j0 in range(4):
-            value = jnp.transpose(
-                jnp.concatenate([leaf_local[j0, place, :], jnp.zeros((128 - K, 128), f32)], 0)
-            )
+            high, low = split_two(leaf_local[j0, place, :])
+            high, low = high.astype(f32), low.astype(f32)
+            value = jnp.transpose(jnp.concatenate([high, high, low, jnp.zeros_like(low)], 0))
             for a in range(4):
                 for b in range(4):
                     leaf_rows[pl.ds((b * 16 + a * 4 + j0) * R + r, 8, stride=64 * R), :] = value[
@@ -592,51 +602,61 @@
 
     lax.fori_loop(0, R, leaf_terms, 0, unroll=2)
     half = lax.broadcasted_iota(jnp.int32, (R, 128), 1) < 64
+    copies[1].wait()
+    copies[2].wait()
 
     def potential(tile, carry):
         lanes = pl.ds(pl.multiple_of(tile * 256, 256), 256)
         high, low = split_two(basis[:, lanes])
-        left, left_low = split_two(leaf_rows[pl.ds(pl.multiple_of(tile * 64, 64), 64), 0:K])
-        total = jnp.dot(left, high, preferred_element_type=f32)
-        total = total + jnp.dot(left, low, preferred_element_type=f32)
-        total = total + jnp.dot(left_low, high, preferred_element_type=f32)
+        left = leaf_rows[pl.ds(pl.multiple_of(tile * 64, 64), 64), 0 : 3 * K].astype(bf16)
+        total = jnp.dot(left, jnp.concatenate([high, low, high], 0), preferred_element_type=f32)
         one = jnp.where(half, total[0:16, 0:128], total[16:32, 0:128])
         two = jnp.where(half, total[32:48, 128:256], total[48:64, 128:256])
         out[:, lanes] = near_field[:, lanes] + jnp.concatenate([one, two], 1)
         return carry
 
-    lax.fori_loop(0, basis.shape[1] // 256, potential, 0, unroll=4)
+    lax.fori_loop(0, basis.shape[1] // 256, potential, 0, unroll=8)
 
 
 def downward_pass(
-    tops, et, payload, low_halo, high_halo, coef_top, prox_top, list1, list2, list3, basis, near_field
+    tops, et, payload, low_halo, high_halo, lifted, prox_top, list1, list2, list3, basis, near_field
 ):
     vmem = pl.BlockSpec(memory_space=pltpu.VMEM)
     smem = pl.BlockSpec(memory_space=pltpu.SMEM)
     panels = basis.shape[1]
-    top_count = coef_top.shape[0]
-    top_lanes = (top_count + 127) // 128 * 128
+    hbm = pl.BlockSpec(memory_space=pltpu.HBM)
+    cluster_lanes = (lifted.shape[0] + 127) // 128 * 128
+    top_lanes = (prox_top.shape[0] + 127) // 128 * 128
     return pl.pallas_call(
         down_kernel,
         out_shape=jax.ShapeDtypeStruct((R, panels), f32),
-        in_specs=[smem] + [vmem] * 11,
+        in_specs=[smem, hbm] + [vmem] * 9 + [hbm] * 2,
         out_specs=vmem,
         scratch_shapes=[
             pltpu.VMEM((3, WIDE, 256), bf16),
-            pltpu.VMEM((3, WIDE, top_lanes), bf16),
+            pltpu.VMEM((3, ROWS, cluster_lanes), bf16),
+            pltpu.VMEM((3, 3 * K, top_lanes), bf16),
+            pltpu.VMEM((cluster_lanes, 128), jnp.int32),
             pltpu.VMEM((WIDE, 128), f32),
             pltpu.VMEM((K * K, 128), f32),
             pltpu.VMEM((2, ROWS, 128), f32),
             pltpu.VMEM((4, ROWS, 128), f32),
             pltpu.VMEM((panels // LEAF * R, 128), f32),
             pltpu.VMEM((128, 128), f32),
+            pltpu.VMEM(et.shape, f32),
+            pltpu.VMEM(basis.shape, f32),
+            pltpu.VMEM(near_field.shape, f32),
+            pltpu.SemaphoreType.DMA((3,)),
         ],
-        compiler_params=pltpu.CompilerParams(vmem_limit_bytes=16 * 2**20),
+        compiler_params=pltpu.CompilerParams(vmem_limit_bytes=54 * 2**20),
         cost_estimate=pl.CostEstimate(
             flops=panels * 4000, bytes_accessed=panels * 400, transcendentals=panels * 20
         ),
         name="downward_pass",
-    )(tops, et, payload, low_halo, high_halo, coef_top, prox_top, list1, list2, list3, basis, near_field)
+    )(
+        tops, et, payload, low_halo, high_halo, lifted, tops.reshape(1, -1), prox_top,
+        list1, list2, list3, basis, near_field,
+    )
 
 
 def body(
@@ -647,16 +667,16 @@
     forward = [(i, i + 1) for i in range(count - 1)]
     backward = [(target, source) for source, target in forward]
     low_leaves, high_leaves = leaf_halos(jitter, charge)
-    et, payload, last, first, terms = upward_pass(
-        top_of, basis, charge, trans0, trans1, trans2, trans3, prox1.T, prox2, prox3, prox_top.shape[0]
+    et, payload, last, first, lifted = upward_pass(
+        basis, charge, trans0, trans1, trans2, trans3, prox1.T, prox2, prox3
     )
     low_halo = lax.ppermute(last, "gx", forward)
     high_halo = lax.ppermute(first, "gx", backward)
-    coef_top = lax.psum(terms, "gx")
+    lifted = lax.all_gather(lifted, "gx", tiled=True)
     near_field = near_potential(near.T, jitter, charge, low_leaves, high_leaves)
-    near_field, coef_top = lax.optimization_barrier((near_field, coef_top))
+    near_field, lifted = lax.optimization_barrier((near_field, lifted))
     return downward_pass(
-        top_of, et, payload, low_halo, high_halo, coef_top, prox_top, list1.T, list2.T, list3.T, basis, near_field
+        top_of, et, payload, low_halo, high_halo, lifted, prox_top, list1.T, list2.T, list3.T, basis, near_field
     )
 
 

time: 181 us -> 177 us (0.978)
  the two profiles are of different devices: /device:TPU:8 before, /device:TPU:0 now
where the time goes in v4:
time: 177 us
  Pallas kernels  136 us (77%)
  blocking collectives  26.6 us (15%)
  starting transfers between devices  10.1 us (6%)
  local copies, waits for them, and re-layouts  3.62 us (2%)
    pallas_call x1, Pallas kernels, near_potential(): pl.pallas_call(near_kernel, out_shape=jax.ShapeDtypeStruct((R, panels), f...  80.5 us
    pallas_call x1, Pallas kernels, downward_pass(): pl.pallas_call(down_kernel, out_shape=jax.ShapeDtypeStruct((R, panels), f...  30.9 us
    all_gather x1, blocking collectives, body(): lifted = lax.all_gather(lifted, 'gx', tiled=True)  26.6 us
    pallas_call x1, Pallas kernels, upward_pass(): pl.pallas_call(up_kernel, out_shape=[jax.ShapeDtypeStruct((7, K * K, 128)...  24.7 us
    ppermute x1, starting transfers between devices, body(): low_halo = lax.ppermute(last, 'gx', forward)  5.16 us
  transfers between devices with their start and end apart: 4, of which 0 were waited for; matrix products, arithmetic and copies ran while one was open for 0% of the time, Pallas kernels for 60%

profile of v4, /device:TPU:0, one launch (start us, length us, event | category | flops | bytes accessed | tf_op | source)
XLA Modules:
  0.0 176.8 jit_solution(4364730824115741529)
XLA Ops:
  0.0 0.7 fusion.1
  0.7 0.9 fusion
  1.6 2.4 %collective-permute-start.2 = (f32[19,1024]{1,0:T(8,128)S(1)}, f32[19,1024]{1,0:T(8,128)S(1)}, u32[]{:S(2)}, u32[]{:S(2)}) collective-permute-start(f32[19,1024]{1,0:T(8,128)S(1)} %pad_maximum_fusion), channel_id=1, source_target_pairs={{0,1},{1,2},{2,3},{3,4},{4,5},{5,6},{6,7},{7,8},{8,9},{9,10},{10,1... | collective-permute-start | bytes 233480 | tf_op jit(solution)/shard_map/ppermute | solution.py:26
  4.0 1.3 collective-permute-start.3
  5.3 0.0 copy-start
  5.4 0.0 copy-start.2
  5.4 0.0 copy-start.3
  5.4 24.7 %upward_pass.1 = (f32[7,1024,128]{2,1,0:T(8,128)}, f32[3,608,128]{2,1,0:T(8,128)}, f32[16,608]{1,0:T(8,128)}, f32[16,608]{1,0:T(8,128)}, f32[8,512]{1,0:T(8,128)}) custom-call(f32[32,32768]{1,0:T(8,128)} %basis_hbm.3, f32[16,32768]{1,0:T(8,128)} %own_charge.1, f32[512,1024]{1,0:T(8,128)} %trans0_hbm.1, f32[128,1024]{1,0:T(8,128)} %trans1.1, ...), custom_call_target="tpu_custom_call" | custom-call | flops 102400000 | bytes 10240000 | tf_op jit(solution)/shard_map/upward_pass/pallas_call | solution.py:408
  30.1 5.2 %collective-permute-start = (f32[16,608]{1,0:T(8,128)}, f32[16,608]{1,0:T(8,128)S(1)}, u32[]{:S(2)}, u32[]{:S(2)}) collective-permute-start(f32[16,608]{1,0:T(8,128)} %get-tuple-element.14), channel_id=1, source_target_pairs={{0,1},{1,2},{2,3},{3,4},{4,5},{5,6},{6,7},{7,8},{8,9},{9,10},{10,1... | collective-permute-start | bytes 116744 | tf_op jit(solution)/shard_map/ppermute | solution.py:673
  35.2 1.3 collective-permute-start.1
  36.5 26.6 %all_gather.3.lifted = f32[128,512]{1,0:T(8,128)} all-gather(f32[8,512]{1,0:T(8,128)} %get-tuple-element.16), channel_id=1, replica_groups=mesh['groups'=2,'gx'=16] {'gx'}, dimensions={0}, use_global_device_ids=true | all-gather | bytes 278528 | tf_op jit(solution)/shard_map/all_gather | solution.py:675
  63.2 0.0 collective-permute-done.2.low_halo
  63.2 0.0 collective-permute-done.3.high_halo
  63.2 0.0 copy-done
  63.2 0.0 copy-done.2
  63.2 0.0 copy-done.3
  63.2 80.5 %near_potential.1.near_hbm = f32[16,32768]{1,0:T(8,128)S(1)} custom-call(s32[16,512]{1,0:T(8,128)S(1)} %bitcast.6, f32[3,32768]{1,0:T(4,128)S(1)} %copy-done.2, f32[16,32768]{1,0:T(8,128)S(1)} %copy-done, f32[19,1024]{1,0:T(8,128)S(1)} %collective-permute-done.2.low_halo, f32[19,1024]{1,0:T(8,128)S(1)} %collective-permute-done.3.high_halo), custom_call_target="tpu_custom_call" | custom-call | flops 6442450944 | bytes 5242880 | tf_op jit(solution)/shard_map/near_potential/pallas_call | solution.py:203
  143.8 0.0 copy-start.1
  143.8 1.4 copy-done.1
  145.2 0.0 collective-permute-done.low_halo
  145.2 0.0 copy-start.4
  145.2 0.0 collective-permute-done.1.high_halo
  145.2 0.0 copy-start.5
  145.2 0.6 copy-done.4
  145.8 0.0 copy-done.5
  145.8 30.9 %downward_pass.1 = f32[16,32768]{1,0:T(8,128)} custom-call(s32[128]{0:T(128)} %tops.1, f32[7,1024,128]{2,1,0:T(8,128)} %get-tuple-element.12.et_hbm, f32[3,608,128]{2,1,0:T(8,128)} %get-tuple-element.13.payload, f32[16,608]{1,0:T(8,128)} %copy-done.4, f32[16,608]{1,0:T(8,128)} %copy-done.5, f32[128,512]{1,0:T(8,128)} %all_gather.3.lifted, s32[1,128]{1,0:T(1,128)} %bitcast.8, ...), custom_call_target="tpu_custom_call" | custom-call | flops 131072000 | bytes 13107200 | tf_op jit(solution)/shard_map/downward_pass/pallas_call | solution.py:630
  (2 shorter events, 0.0 us)
Async XLA Ops:
  1.6 61.5 %collective-permute-start.2 = (f32[19,1024]{1,0:T(8,128)S(1)}, f32[19,1024]{1,0:T(8,128)S(1)}, u32[]{:S(2)}, u32[]{:S(2)}) collective-permute-start(f32[19,1024]{1,0:T(8,128)S(1)} %pad_maximum_fusion), channel_id=1, source_target_pairs={{0,1},{1,2},{2,3},{3,4},{4,5},{5,6},{6,7},{7,8},{8,9},{9,10},{10,1... | collective-permute-start | bytes 233480 | tf_op jit(solution)/shard_map/ppermute | solution.py:26
  4.0 59.2 %collective-permute-start.3 = (f32[19,1024]{1,0:T(8,128)S(1)}, f32[19,1024]{1,0:T(8,128)S(1)}, u32[]{:S(2)}, u32[]{:S(2)}) collective-permute-start(f32[19,1024]{1,0:T(8,128)S(1)} %pad_maximum_fusion.1), channel_id=1, source_target_pairs={{1,0},{2,1},{3,2},{4,3},{5,4},{6,5},{7,6},{8,7},{9,8},{10,9},{11,1... | collective-permute-start | bytes 233480 | tf_op jit(solution)/shard_map/ppermute | solution.py:26
  5.3 57.9 %copy-start = (f32[16,32768]{1,0:T(8,128)S(1)}, f32[16,32768]{1,0:T(8,128)}, u32[]{:S(2)}) copy-start(f32[16,32768]{1,0:T(8,128)} %own_charge.1) | copy-start | bytes 6291460
  5.4 57.8 %copy-start.2 = (f32[3,32768]{1,0:T(4,128)S(1)}, f32[3,32768]{1,0:T(4,128)}, u32[]{:S(2)}) copy-start(f32[3,32768]{1,0:T(4,128)} %own_jitter.1) | copy-start | bytes 1179652
  5.4 57.8 %copy-start.3 = (s32[512,16]{0,1:T(8,128)S(1)}, s32[512,16]{0,1:T(8,128)}, u32[]{:S(2)}) copy-start(s32[512,16]{0,1:T(8,128)} %param.19) | copy-start | bytes 98308
  30.1 115.1 %collective-permute-start = (f32[16,608]{1,0:T(8,128)}, f32[16,608]{1,0:T(8,128)S(1)}, u32[]{:S(2)}, u32[]{:S(2)}) collective-permute-start(f32[16,608]{1,0:T(8,128)} %get-tuple-element.14), channel_id=1, source_target_pairs={{0,1},{1,2},{2,3},{3,4},{4,5},{5,6},{6,7},{7,8},{8,9},{9,10},{10,1... | collective-permute-start | bytes 116744 | tf_op jit(solution)/shard_map/ppermute | solution.py:673
  35.2 109.9 %collective-permute-start.1 = (f32[16,608]{1,0:T(8,128)}, f32[16,608]{1,0:T(8,128)S(1)}, u32[]{:S(2)}, u32[]{:S(2)}) collective-permute-start(f32[16,608]{1,0:T(8,128)} %get-tuple-element.15), channel_id=1, source_target_pairs={{1,0},{2,1},{3,2},{4,3},{5,4},{6,5},{7,6},{8,7},{9,8},{10,9},{11,1... | collective-permute-start | bytes 116744 | tf_op jit(solution)/shard_map/ppermute | solution.py:674
  143.8 1.4 copy-start.1
  145.2 0.6 copy-start.4
  145.2 0.6 copy-start.5

commit v5 on v4

--- a/solution.py
+++ b/solution.py
@@ -255,6 +255,27 @@
     lax.fori_loop(0, R // for_rows, step, 0)
 
 
+def matvec_packed(matrix, vector, packed, out, add, shifts=()):
+    block = lane_digits((1, 128), 1)[0]
+    for i in range(4):
+        value = vector[i * K : (i + 1) * K, :]
+        for q in range(1, 4):
+            value = jnp.where(block == q, vector[(4 * q + i) * K : (4 * q + i + 1) * K, :], value)
+        packed[i * K : (i + 1) * K, :] = value
+    sums = [jnp.zeros((K, 128), f32) for _ in range(4)]
+    for column in range(K):
+        values = matrix(column)
+        for i in range(4):
+            sums[i] = sums[i] + values * packed[i * K + column : i * K + column + 1, :]
+    for i in range(4):
+        for q in range(4):
+            part = jnp.where(block == q, sums[i], 0.0)
+            for shift in (32, 64) + tuple(shifts):
+                part = part + pltpu.roll(part, shift, 1)
+            place = slice((4 * q + i) * K, (4 * q + i + 1) * K)
+            out[place, :] = out[place, :] + part if add else part
+
+
 def fold(ref, shifts):
     def step(i, carry):
         place = pl.ds(pl.multiple_of(i * 64, 64), 64)
@@ -276,8 +297,8 @@
 
 
 def up_kernel(
-    basis_hbm, charge_hbm, trans0_hbm, trans1, trans2, trans3, prox1, prox2, prox3,
-    et, payload, last_out, first_out, lifted, leaf_rows, coef0, coef, flipped, columns, by_column, basis, charge, trans0, sems,
+    tops, basis_hbm, charge_hbm, trans0_hbm, trans1, trans2, trans3, prox1, prox2, prox3,
+    et, payload, last_out, first_out, terms, leaf_rows, coef0, coef, flipped, columns, by_column, packed, basis, charge, trans0, sems,
 ):
     here = lax.axis_index("gx")
     quarter = lax.broadcasted_iota(jnp.int32, (R, 256), 1).astype(f32)
@@ -347,14 +368,17 @@
     def lift_from(entry, vector, out, add):
         for b in range(K):
             by_column[b * K : (b + 1) * K, :] = et[entry, pl.ds(b, K, stride=K), :]
-        matvec(lambda b: by_column[b * K : (b + 1) * K, :], vector, out, add)
+        if entry < 5:
+            matvec(lambda b: by_column[b * K : (b + 1) * K, :], vector, out, add)
+        else:
+            shifts = (8, 16) if entry == 5 else ()
+            matvec_packed(lambda b: by_column[b * K : (b + 1) * K, :], vector, packed, out, add, shifts)
 
     for j0 in range(4):
         lift_from(j0, coef0.at[j0], coef.at[0], j0 > 0)
     lift_from(4, coef.at[0], coef.at[1], False)
     fold(coef.at[1], (32, 64))
     lift_from(5, coef.at[1], coef.at[2], False)
-    fold(coef.at[2], (8, 16))
     lift_from(6, coef.at[2], coef.at[3], False)
 
     j1, j2, c3 = lane_digits((1, 128), 1)
@@ -399,10 +423,14 @@
             last_out[target : target + 1, :] = flipped[last_rows[level][i] : last_rows[level][i] + 1, 0:WIDE]
             first_out[target : target + 1, :] = flipped[first_rows[level][i] : first_rows[level][i] + 1, 0:WIDE]
     flip_payload(coef.at[3], ROWS)
-    lifted[...] = flipped[0:8, 0:ROWS]
-
-
-def upward_pass(basis, charge, trans0, trans1, trans2, trans3, prox1, prox2, prox3):
+    top_ids = lax.broadcasted_iota(jnp.int32, terms.shape, 0)
+    total = jnp.zeros(terms.shape, f32)
+    for c in range(8):
+        total = total + jnp.where(top_ids == tops[here * 8 + c], flipped[c : c + 1, 0:ROWS], 0.0)
+    terms[...] = total
+
+
+def upward_pass(tops, basis, charge, trans0, trans1, trans2, trans3, prox1, prox2, prox3, top_count):
     vmem = pl.BlockSpec(memory_space=pltpu.VMEM)
     leaves = trans0.shape[0]
     return pl.pallas_call(
@@ -412,9 +440,9 @@
             jax.ShapeDtypeStruct((3, WIDE, 128), f32),
             jax.ShapeDtypeStruct((EDGE, WIDE), f32),
             jax.ShapeDtypeStruct((EDGE, WIDE), f32),
-            jax.ShapeDtypeStruct((8, ROWS), f32),
+            jax.ShapeDtypeStruct((top_count, ROWS), f32),
         ],
-        in_specs=[pl.BlockSpec(memory_space=pltpu.HBM)] * 3 + [vmem] * 6,
+        in_specs=[pl.BlockSpec(memory_space=pltpu.SMEM)] + [pl.BlockSpec(memory_space=pltpu.HBM)] * 3 + [vmem] * 6,
         out_specs=[vmem] * 5,
         scratch_shapes=[
             pltpu.VMEM((leaves * R, 128), f32),
@@ -423,6 +451,7 @@
             pltpu.VMEM((128, 640), f32),
             pltpu.VMEM((8, leaves, 128), f32),
             pltpu.VMEM((K * K, 128), f32),
+            pltpu.VMEM((4 * K, 128), f32),
             pltpu.VMEM(basis.shape, f32),
             pltpu.VMEM(charge.shape, f32),
             pltpu.VMEM(trans0.shape, f32),
@@ -433,12 +462,12 @@
             flops=leaves * 200000, bytes_accessed=leaves * 20000, transcendentals=0
         ),
         name="upward_pass",
-    )(basis, charge, trans0, trans1, trans2, trans3, prox1, prox2, prox3)
+    )(tops, basis, charge, trans0, trans1, trans2, trans3, prox1, prox2, prox3)
 
 
 def down_kernel(
-    tops, et_hbm, payload, low_halo, high_halo, lifted, top_row, prox_top, list1, list2, list3, basis_hbm, near_hbm,
-    out, split_rows, split_top, split_place, top_column, gathered, green_rows, local, leaf_local, leaf_rows, columns,
+    tops, et_hbm, payload, low_halo, high_halo, coef_top, prox_top, list1, list2, list3, basis_hbm, near_hbm,
+    out, split_rows, split_top, split_place, gathered, green_rows, local, leaf_local, leaf_rows, columns, packed,
     et, basis, near_field, sems,
 ):
     copies = [
@@ -463,7 +492,7 @@
         total = total + jnp.dot(ref[1], hot, preferred_element_type=f32)
         return total + jnp.dot(ref[2], hot, preferred_element_type=f32)
 
-    def couple_picked(target, out_ref, add):
+    def couple_picked(target, out_ref, add, shifts=None):
         def step(b, carry):
             square = None
             for axis_id in range(3):
@@ -473,10 +502,16 @@
             return carry
 
         lax.fori_loop(0, K, step, 0, unroll=4)
-        matvec(lambda b: green_rows[b * K : (b + 1) * K, :], gathered, out_ref, add)
+        if shifts is None:
+            matvec(lambda b: green_rows[b * K : (b + 1) * K, :], gathered, out_ref, add)
+        else:
+            matvec_packed(lambda b: green_rows[b * K : (b + 1) * K, :], gathered, packed, out_ref, add, shifts)
 
     def descend_from(entry, vector, out_ref, add):
-        matvec(lambda a: et[entry, a * K : (a + 1) * K, :], vector, out_ref, add)
+        if entry < 5:
+            matvec(lambda a: et[entry, a * K : (a + 1) * K, :], vector, out_ref, add)
+        else:
+            matvec_packed(lambda a: et[entry, a * K : (a + 1) * K, :], vector, packed, out_ref, add)
 
     my_top = jnp.zeros((1, 128), jnp.int32)
     for c in range(8):
@@ -494,16 +529,9 @@
         for i in range(3):
             ref[i, first : first + value.shape[0], q : q + 128] = parts[i].astype(bf16)
 
-    cluster_count = lifted.shape[0]
     for q in range(0, split_top.shape[2], 128):
-        rows = min(128, cluster_count - q)
         for w in range(0, ROWS, 128):
-            keep(split_top, w, q, flip_top(lifted[q : q + rows, w : w + 128]))
-        owners = top_row[:, q : q + rows].astype(f32)
-        if rows < 128:
-            owners = jnp.concatenate([owners, jnp.full((1, 128 - rows), -9.0, f32)], 1)
-        top_column[q : q + 128, :] = jnp.transpose(jnp.broadcast_to(owners, (128, 128))).astype(jnp.int32)
-    for q in range(0, split_place.shape[2], 128):
+            keep(split_top, w, q, flip_top(coef_top[q : q + min(128, top_count - q), w : w + 128]))
         offsets = flip_top(prox_top[q : q + min(128, top_count - q), :])
         across, beside = centre_lanes(lax.broadcasted_iota(jnp.int32, (1, 128), 1) + q, 64)
         keep(split_place, 0, q, across + 64.0 * offsets[0:K])
@@ -517,7 +545,7 @@
     def top_block(block, carry):
         source = block * 16 + lane_block
         wanted = jnp.where(jnp.abs(source - my_top) >= 2, source, -1)
-        gathered[0:ROWS, :] = pick(split_top, top_column[...] == wanted)
+        gathered[0:ROWS, :] = pick(split_top, top_rows == wanted)
         gathered[ROWS:WIDE, :] = pick(split_place, top_rows == wanted)
         couple_picked(lambda axis_id: leaf_local[0, axis_id * K : (axis_id + 1) * K, :], local.at[0], True)
         return carry
@@ -564,8 +592,7 @@
     wanted = jnp.where(j2 == 0, picked[0:1], jnp.where(j2 == 1, picked[1:2], jnp.where(j2 == 2, picked[2:3], -5000)))
     split_to(split_rows, slice(0, 128), payload[2])
     gathered[...] = pick(split_rows, source_ids(2, s3, 8, 8) == wanted)
-    couple_picked(place_of(2), local.at[1], False)
-    fold(local.at[1], (8, 16))
+    couple_picked(place_of(2), local.at[1], False, (8, 16))
     copies[0].wait()
     descend_from(6, local.at[0], local.at[1], True)
 
@@ -619,30 +646,29 @@
 
 
 def downward_pass(
-    tops, et, payload, low_halo, high_halo, lifted, prox_top, list1, list2, list3, basis, near_field
+    tops, et, payload, low_halo, high_halo, coef_top, prox_top, list1, list2, list3, basis, near_field
 ):
     vmem = pl.BlockSpec(memory_space=pltpu.VMEM)
     smem = pl.BlockSpec(memory_space=pltpu.SMEM)
     panels = basis.shape[1]
     hbm = pl.BlockSpec(memory_space=pltpu.HBM)
-    cluster_lanes = (lifted.shape[0] + 127) // 128 * 128
     top_lanes = (prox_top.shape[0] + 127) // 128 * 128
     return pl.pallas_call(
         down_kernel,
         out_shape=jax.ShapeDtypeStruct((R, panels), f32),
-        in_specs=[smem, hbm] + [vmem] * 9 + [hbm] * 2,
+        in_specs=[smem, hbm] + [vmem] * 8 + [hbm] * 2,
         out_specs=vmem,
         scratch_shapes=[
             pltpu.VMEM((3, WIDE, 256), bf16),
-            pltpu.VMEM((3, ROWS, cluster_lanes), bf16),
+            pltpu.VMEM((3, ROWS, top_lanes), bf16),
             pltpu.VMEM((3, 3 * K, top_lanes), bf16),
-            pltpu.VMEM((cluster_lanes, 128), jnp.int32),
             pltpu.VMEM((WIDE, 128), f32),
             pltpu.VMEM((K * K, 128), f32),
             pltpu.VMEM((2, ROWS, 128), f32),
             pltpu.VMEM((4, ROWS, 128), f32),
             pltpu.VMEM((panels // LEAF * R, 128), f32),
             pltpu.VMEM((128, 128), f32),
+            pltpu.VMEM((4 * K, 128), f32),
             pltpu.VMEM(et.shape, f32),
             pltpu.VMEM(basis.shape, f32),
             pltpu.VMEM(near_field.shape, f32),
@@ -654,7 +680,7 @@
         ),
         name="downward_pass",
     )(
-        tops, et, payload, low_halo, high_halo, lifted, tops.reshape(1, -1), prox_top,
+        tops, et, payload, low_halo, high_halo, coef_top, prox_top,
         list1, list2, list3, basis, near_field,
     )
 
@@ -667,16 +693,16 @@
     forward = [(i, i + 1) for i in range(count - 1)]
     backward = [(target, source) for source, target in forward]
     low_leaves, high_leaves = leaf_halos(jitter, charge)
-    et, payload, last, first, lifted = upward_pass(
-        basis, charge, trans0, trans1, trans2, trans3, prox1.T, prox2, prox3
+    et, payload, last, first, terms = upward_pass(
+        top_of, basis, charge, trans0, trans1, trans2, trans3, prox1.T, prox2, prox3, prox_top.shape[0]
     )
     low_halo = lax.ppermute(last, "gx", forward)
     high_halo = lax.ppermute(first, "gx", backward)
-    lifted = lax.all_gather(lifted, "gx", tiled=True)
+    coef_top = lax.psum(terms, "gx")
     near_field = near_potential(near.T, jitter, charge, low_leaves, high_leaves)
-    near_field, lifted = lax.optimization_barrier((near_field, lifted))
+    near_field, coef_top = lax.optimization_barrier((near_field, coef_top))
     return downward_pass(
-        top_of, et, payload, low_halo, high_halo, lifted, prox_top, list1.T, list2.T, list3.T, basis, near_field
+        top_of, et, payload, low_halo, high_halo, coef_top, prox_top, list1.T, list2.T, list3.T, basis, near_field
     )
 
 

time: 177 us -> 162 us (0.915)
  the two profiles are of different devices: /device:TPU:0 before, /device:TPU:8 now
where the time goes in v5:
time: 162 us; the launch traced here: 161 us
  Pallas kernels  131 us (81%)
  between operations  13.6 us (8%)
  starting transfers between devices  13.1 us (8%)
  local copies, waits for them, and re-layouts  3.65 us (2%)
    pallas_call x1, Pallas kernels, near_potential(): pl.pallas_call(near_kernel, out_shape=jax.ShapeDtypeStruct((R, panels), f...  80.6 us
    pallas_call x1, Pallas kernels, downward_pass(): pl.pallas_call(down_kernel, out_shape=jax.ShapeDtypeStruct((R, panels), f...  27.9 us
    pallas_call x1, Pallas kernels, upward_pass(): pl.pallas_call(up_kernel, out_shape=[jax.ShapeDtypeStruct((7, K * K, 128)...  22.4 us
    ppermute x1, starting transfers between devices, body(): high_halo = lax.ppermute(first, 'gx', backward)  4.72 us
    ppermute x1, starting transfers between devices, leaf_halos(): lax.ppermute(first, 'gx', backward)  4.54 us
  transfers between devices with their start and end apart: 5, of which 0 were waited for; matrix products, arithmetic and copies ran while one was open for 0% of the time, Pallas kernels for 64%

profile of v5, /device:TPU:8, one launch (start us, length us, event | category | flops | bytes accessed | tf_op | source)
XLA Modules:
  0.0 161.3 jit_solution(16318703153311853474)
XLA Ops:
  6.5 0.0 all-reduce.2.cloned.1.call-start
  6.5 0.7 fusion.1
  7.3 0.9 fusion
  8.2 1.9 %collective-permute-start.2 = (f32[19,1024]{1,0:T(8,128)S(1)}, f32[19,1024]{1,0:T(8,128)S(1)}, u32[]{:S(2)}, u32[]{:S(2)}) collective-permute-start(f32[19,1024]{1,0:T(8,128)S(1)} %pad_maximum_fusion), channel_id=1, source_target_pairs={{0,1},{1,2},{2,3},{3,4},{4,5},{5,6},{6,7},{7,8},{8,9},{9,10},{10,1... | collective-permute-start | bytes 233480 | tf_op jit(solution)/shard_map/ppermute | solution.py:26
  10.1 4.5 %collective-permute-start.3 = (f32[19,1024]{1,0:T(8,128)S(1)}, f32[19,1024]{1,0:T(8,128)S(1)}, u32[]{:S(2)}, u32[]{:S(2)}) collective-permute-start(f32[19,1024]{1,0:T(8,128)S(1)} %pad_maximum_fusion.1), channel_id=1, source_target_pairs={{1,0},{2,1},{3,2},{4,3},{5,4},{6,5},{7,6},{8,7},{9,8},{10,9},{11,1... | collective-permute-start | bytes 233480 | tf_op jit(solution)/shard_map/ppermute | solution.py:26
  14.7 0.0 copy-start
  14.7 0.0 copy-start.2
  14.7 0.0 copy-start.3
  14.7 22.4 %upward_pass.1 = (f32[7,1024,128]{2,1,0:T(8,128)}, f32[3,608,128]{2,1,0:T(8,128)}, f32[16,608]{1,0:T(8,128)}, f32[16,608]{1,0:T(8,128)}, f32[32,512]{1,0:T(8,128)}) custom-call(s32[128]{0:T(128)} %tops.3, f32[32,32768]{1,0:T(8,128)} %basis_hbm.3, f32[16,32768]{1,0:T(8,128)} %own_charge.1, f32[512,1024]{1,0:T(8,128)} %trans0_hbm.1, f32[128,1024]{1,0:T(8,128)} %trans1.1, ...), custom_call_target="tpu_custom_call" | custom-call | flops 102400000 | bytes 10240000 | tf_op jit(solution)/shard_map/upward_pass/pallas_call | solution.py:436
  37.1 0.0 all-reduce.2.cloned.1.call-update
  37.1 1.9 %collective-permute-start = (f32[16,608]{1,0:T(8,128)}, f32[16,608]{1,0:T(8,128)S(1)}, u32[]{:S(2)}, u32[]{:S(2)}) collective-permute-start(f32[16,608]{1,0:T(8,128)} %get-tuple-element.14), channel_id=1, source_target_pairs={{0,1},{1,2},{2,3},{3,4},{4,5},{5,6},{6,7},{7,8},{8,9},{9,10},{10,1... | collective-permute-start | bytes 116744 | tf_op jit(solution)/shard_map/ppermute | solution.py:699
  39.1 4.7 %collective-permute-start.1 = (f32[16,608]{1,0:T(8,128)}, f32[16,608]{1,0:T(8,128)S(1)}, u32[]{:S(2)}, u32[]{:S(2)}) collective-permute-start(f32[16,608]{1,0:T(8,128)} %get-tuple-element.15), channel_id=1, source_target_pairs={{1,0},{2,1},{3,2},{4,3},{5,4},{6,5},{7,6},{8,7},{9,8},{10,9},{11,1... | collective-permute-start | bytes 116744 | tf_op jit(solution)/shard_map/ppermute | solution.py:700
  43.8 0.0 collective-permute-done.2.low_halo
  43.8 0.0 collective-permute-done.3.high_halo
  43.8 0.0 copy-done
  43.8 0.0 copy-done.2
  43.8 0.0 copy-done.3
  43.8 80.6 %near_potential.1.near_hbm = f32[16,32768]{1,0:T(8,128)S(1)} custom-call(s32[16,512]{1,0:T(8,128)S(1)} %bitcast.5, f32[3,32768]{1,0:T(4,128)S(1)} %copy-done.2, f32[16,32768]{1,0:T(8,128)S(1)} %copy-done, f32[19,1024]{1,0:T(8,128)S(1)} %collective-permute-done.2.low_halo, f32[19,1024]{1,0:T(8,128)S(1)} %collective-permute-done.3.high_halo), custom_call_target="tpu_custom_call" | custom-call | flops 6442450944 | bytes 5242880 | tf_op jit(solution)/shard_map/near_potential/pallas_call | solution.py:203
  124.4 0.0 copy-start.1
  124.4 1.4 copy-done.1
  125.8 0.0 all-reduce.2.cloned.1.call-done.coef_top
  125.8 0.0 collective-permute-done.low_halo
  125.8 0.0 copy-start.4
  125.8 0.0 collective-permute-done.1.high_halo
  125.8 0.0 copy-start.5
  125.8 0.6 copy-done.4
  126.4 0.0 copy-done.5
  126.4 27.9 %downward_pass.1 = f32[16,32768]{1,0:T(8,128)} custom-call(s32[128]{0:T(128)} %tops.3, f32[7,1024,128]{2,1,0:T(8,128)} %get-tuple-element.12.et_hbm, f32[3,608,128]{2,1,0:T(8,128)} %get-tuple-element.13.payload, f32[16,608]{1,0:T(8,128)} %copy-done.4, f32[16,608]{1,0:T(8,128)} %copy-done.5, f32[32,512]{1,0:T(8,128)} %all-reduce.2.cloned.1.call-done.coef_top, ...), custom_call_target="tpu_custom_call" | custom-call | flops 131072000 | bytes 13107200 | tf_op jit(solution)/shard_map/downward_pass/pallas_call | solution.py:656
  (2 shorter events, 0.0 us)
Async XLA Ops:
  6.5 119.3 %all-reduce.2.cloned.1.call-start = ((), (), s32[]{:S(2)}) async-start(), calls=%async_computation | async-start | bytes 131072 | tf_op jit(solution)/shard_map/psum | solution.py:701
  8.2 35.6 %collective-permute-start.2 = (f32[19,1024]{1,0:T(8,128)S(1)}, f32[19,1024]{1,0:T(8,128)S(1)}, u32[]{:S(2)}, u32[]{:S(2)}) collective-permute-start(f32[19,1024]{1,0:T(8,128)S(1)} %pad_maximum_fusion), channel_id=1, source_target_pairs={{0,1},{1,2},{2,3},{3,4},{4,5},{5,6},{6,7},{7,8},{8,9},{9,10},{10,1... | collective-permute-start | bytes 233480 | tf_op jit(solution)/shard_map/ppermute | solution.py:26
  10.1 33.7 %collective-permute-start.3 = (f32[19,1024]{1,0:T(8,128)S(1)}, f32[19,1024]{1,0:T(8,128)S(1)}, u32[]{:S(2)}, u32[]{:S(2)}) collective-permute-start(f32[19,1024]{1,0:T(8,128)S(1)} %pad_maximum_fusion.1), channel_id=1, source_target_pairs={{1,0},{2,1},{3,2},{4,3},{5,4},{6,5},{7,6},{8,7},{9,8},{10,9},{11,1... | collective-permute-start | bytes 233480 | tf_op jit(solution)/shard_map/ppermute | solution.py:26
  14.7 29.1 %copy-start = (f32[16,32768]{1,0:T(8,128)S(1)}, f32[16,32768]{1,0:T(8,128)}, u32[]{:S(2)}) copy-start(f32[16,32768]{1,0:T(8,128)} %own_charge.1) | copy-start | bytes 6291460
  14.7 29.1 %copy-start.2 = (f32[3,32768]{1,0:T(4,128)S(1)}, f32[3,32768]{1,0:T(4,128)}, u32[]{:S(2)}) copy-start(f32[3,32768]{1,0:T(4,128)} %own_jitter.1) | copy-start | bytes 1179652
  14.7 29.1 %copy-start.3 = (s32[512,16]{0,1:T(8,128)S(1)}, s32[512,16]{0,1:T(8,128)}, u32[]{:S(2)}) copy-start(s32[512,16]{0,1:T(8,128)} %param.19) | copy-start | bytes 98308
  37.1 88.7 %collective-permute-start = (f32[16,608]{1,0:T(8,128)}, f32[16,608]{1,0:T(8,128)S(1)}, u32[]{:S(2)}, u32[]{:S(2)}) collective-permute-start(f32[16,608]{1,0:T(8,128)} %get-tuple-element.14), channel_id=1, source_target_pairs={{0,1},{1,2},{2,3},{3,4},{4,5},{5,6},{6,7},{7,8},{8,9},{9,10},{10,1... | collective-permute-start | bytes 116744 | tf_op jit(solution)/shard_map/ppermute | solution.py:699
  39.1 86.8 %collective-permute-start.1 = (f32[16,608]{1,0:T(8,128)}, f32[16,608]{1,0:T(8,128)S(1)}, u32[]{:S(2)}, u32[]{:S(2)}) collective-permute-start(f32[16,608]{1,0:T(8,128)} %get-tuple-element.15), channel_id=1, source_target_pairs={{1,0},{2,1},{3,2},{4,3},{5,4},{6,5},{7,6},{8,7},{9,8},{10,9},{11,1... | collective-permute-start | bytes 116744 | tf_op jit(solution)/shard_map/ppermute | solution.py:700
  124.4 1.4 copy-start.1
  125.8 0.6 copy-start.4
  125.8 0.6 copy-start.5
Sparse Core Ops, SparseCore 0:
  37.2 87.3 all-reduce.1

commit v6 on v5

--- a/solution.py
+++ b/solution.py
@@ -34,7 +34,7 @@
 
 
 GROUP = 16
-BATCH = 8
+BATCH = 16
 bf16 = jnp.bfloat16
 f32 = jnp.float32
 
@@ -465,9 +465,119 @@
     )(tops, basis, charge, trans0, trans1, trans2, trans3, prox1, prox2, prox3)
 
 
+def pick(ref, hot):
+    hot = hot.astype(f32).astype(bf16)
+    total = jnp.dot(ref[0], hot, preferred_element_type=f32)
+    total = total + jnp.dot(ref[1], hot, preferred_element_type=f32)
+    return total + jnp.dot(ref[2], hot, preferred_element_type=f32)
+
+
+def couple_picked(gathered, green_rows, packed, target, out_ref, add, shifts=None):
+    def step(b, carry):
+        square = None
+        for axis_id in range(3):
+            spread = target(axis_id) - gathered[pl.ds(ROWS + axis_id * K + b, 1), :]
+            square = spread * spread if square is None else square + spread * spread
+        green_rows[pl.ds(pl.multiple_of(b * K, K), K), :] = inv_four_pi * lax.rsqrt(square + soft_square)
+        return carry
+
+    lax.fori_loop(0, K, step, 0, unroll=4)
+    if shifts is None:
+        matvec(lambda b: green_rows[b * K : (b + 1) * K, :], gathered, out_ref, add)
+    else:
+        matvec_packed(lambda b: green_rows[b * K : (b + 1) * K, :], gathered, packed, out_ref, add, shifts)
+
+
+def couple_kernel(
+    payload, low_halo, high_halo, list1, list2, list3, far, split_rows, gathered, green_rows, columns, packed
+):
+    here = lax.axis_index("gx")
+    j1, j2, c3 = lane_digits((1, 128), 1)
+
+    def split_to(ref, lanes, value):
+        parts = split_three(value)
+        for i in range(3):
+            ref[i, :, lanes] = parts[i].astype(bf16)
+
+    halo = jnp.concatenate([low_halo[...], high_halo[...], jnp.zeros((128 - 2 * EDGE, WIDE), f32)], 0)
+    for w in range(0, WIDE, 128):
+        size = min(128, WIDE - w)
+        block = halo[:, w : w + size]
+        if size < 128:
+            block = jnp.concatenate([block, jnp.zeros((128, 128 - size), f32)], 1)
+        parts = split_three(jnp.transpose(block))
+        for i in range(3):
+            split_rows[i, w : w + size, 128:256] = parts[i][0:size].astype(bf16)
+
+    def lane_list(ref, rows, base):
+        count = ref.shape[1]
+        values = jnp.concatenate([(ref[...] - base).astype(f32), jnp.zeros((125, count), f32)], 0)
+        if count < 128:
+            values = jnp.concatenate([values, jnp.zeros((128, 128 - count), f32)], 1)
+        columns[...] = jnp.transpose(values)
+        parts = [
+            columns[pl.ds(rows[0] * a + rows[1] * b, 8, stride=rows[2]), :] for a in range(4) for b in range(4)
+        ]
+        return jnp.transpose(jnp.concatenate(parts, 0)).astype(jnp.int32)
+
+    source = lax.broadcasted_iota(jnp.int32, (256, 128), 0)
+    edge = source - 128
+    s1, s2, s3 = (source >> 5) & 3, (source >> 3) & 3, source & 7
+
+    def source_ids(level, own, own_count, count):
+        low = edge - 4 * level
+        high = edge - EDGE - 4 * level
+        ids = jnp.where(source < own_count, own, -1000)
+        ids = jnp.where((low >= 0) & (low < 4), low - 4, ids)
+        return jnp.where((high >= 0) & (high < 4), high + count, ids)
+
+    def place_of(level):
+        return lambda axis_id: payload[level, ROWS + axis_id * K : ROWS + (axis_id + 1) * K, :]
+
+    picked = lane_list(list3, (0, 0, 1), here * 8)
+    wanted = jnp.where(j2 == 0, picked[0:1], jnp.where(j2 == 1, picked[1:2], jnp.where(j2 == 2, picked[2:3], -5000)))
+    split_to(split_rows, slice(0, 128), payload[2])
+    gathered[...] = pick(split_rows, source_ids(2, s3, 8, 8) == wanted)
+    couple_picked(gathered, green_rows, packed, place_of(2), far.at[2], False, (8, 16))
+
+    picked = lane_list(list2, (0, 1, 4), here * 32)
+    wanted = jnp.where(j1 == 0, picked[0:1], jnp.where(j1 == 1, picked[1:2], jnp.where(j1 == 2, picked[2:3], -5000)))
+    split_to(split_rows, slice(0, 128), payload[1])
+    gathered[...] = pick(split_rows, source_ids(1, s3 * 4 + s2, 32, 32) == wanted)
+    couple_picked(gathered, green_rows, packed, place_of(1), far.at[1], False)
+    fold(far.at[1], (32, 64))
+
+    picked = lane_list(list1, (1, 4, 16), here * 128)
+    split_to(split_rows, slice(0, 128), payload[0])
+    ids = source_ids(0, s3 * 16 + s2 * 4 + s1, 128, 128)
+    for j in range(3):
+        gathered[...] = pick(split_rows, ids == picked[j : j + 1])
+        couple_picked(gathered, green_rows, packed, place_of(0), far.at[0], j > 0)
+
+
+def couplings(payload, low_halo, high_halo, list1, list2, list3):
+    vmem = pl.BlockSpec(memory_space=pltpu.VMEM)
+    return pl.pallas_call(
+        couple_kernel,
+        out_shape=jax.ShapeDtypeStruct((3, ROWS, 128), f32),
+        in_specs=[vmem] * 6,
+        out_specs=vmem,
+        scratch_shapes=[
+            pltpu.VMEM((3, WIDE, 256), bf16),
+            pltpu.VMEM((WIDE, 128), f32),
+            pltpu.VMEM((K * K, 128), f32),
+            pltpu.VMEM((128, 128), f32),
+            pltpu.VMEM((4 * K, 128), f32),
+        ],
+        compiler_params=pltpu.CompilerParams(vmem_limit_bytes=16 * 2**20),
+        cost_estimate=pl.CostEstimate(flops=20000000, bytes_accessed=2000000, transcendentals=600000),
+        name="couplings",
+    )(payload, low_halo, high_halo, list1, list2, list3)
+
+
 def down_kernel(
-    tops, et_hbm, payload, low_halo, high_halo, coef_top, prox_top, list1, list2, list3, basis_hbm, near_hbm,
-    out, split_rows, split_top, split_place, gathered, green_rows, local, leaf_local, leaf_rows, columns, packed,
+    tops, et_hbm, far, coef_top, prox_top, basis_hbm, near_hbm,
+    out, split_top, split_place, gathered, green_rows, local, leaf_local, leaf_rows, packed,
     et, basis, near_field, sems,
 ):
     copies = [
@@ -481,32 +591,6 @@
     top_count = prox_top.shape[0]
     j1, j2, c3 = lane_digits((1, 128), 1)
 
-    def split_to(ref, columns, value):
-        parts = split_three(value)
-        for i in range(3):
-            ref[i, :, columns] = parts[i].astype(bf16)
-
-    def pick(ref, hot):
-        hot = hot.astype(f32).astype(bf16)
-        total = jnp.dot(ref[0], hot, preferred_element_type=f32)
-        total = total + jnp.dot(ref[1], hot, preferred_element_type=f32)
-        return total + jnp.dot(ref[2], hot, preferred_element_type=f32)
-
-    def couple_picked(target, out_ref, add, shifts=None):
-        def step(b, carry):
-            square = None
-            for axis_id in range(3):
-                spread = target(axis_id) - gathered[pl.ds(ROWS + axis_id * K + b, 1), :]
-                square = spread * spread if square is None else square + spread * spread
-            green_rows[pl.ds(pl.multiple_of(b * K, K), K), :] = inv_four_pi * lax.rsqrt(square + soft_square)
-            return carry
-
-        lax.fori_loop(0, K, step, 0, unroll=4)
-        if shifts is None:
-            matvec(lambda b: green_rows[b * K : (b + 1) * K, :], gathered, out_ref, add)
-        else:
-            matvec_packed(lambda b: green_rows[b * K : (b + 1) * K, :], gathered, packed, out_ref, add, shifts)
-
     def descend_from(entry, vector, out_ref, add):
         if entry < 5:
             matvec(lambda a: et[entry, a * K : (a + 1) * K, :], vector, out_ref, add)
@@ -547,69 +631,21 @@
         wanted = jnp.where(jnp.abs(source - my_top) >= 2, source, -1)
         gathered[0:ROWS, :] = pick(split_top, top_rows == wanted)
         gathered[ROWS:WIDE, :] = pick(split_place, top_rows == wanted)
-        couple_picked(lambda axis_id: leaf_local[0, axis_id * K : (axis_id + 1) * K, :], local.at[0], True)
+        couple_picked(
+            gathered, green_rows, packed,
+            lambda axis_id: leaf_local[0, axis_id * K : (axis_id + 1) * K, :], local.at[0], True,
+        )
         return carry
 
     lax.fori_loop(0, (top_count + 15) // 16, top_block, 0)
     fold(local.at[0], (8, 16, 32, 64))
 
-    halo = jnp.concatenate([low_halo[...], high_halo[...], jnp.zeros((128 - 2 * EDGE, WIDE), f32)], 0)
-    for w in range(0, WIDE, 128):
-        size = min(128, WIDE - w)
-        block = halo[:, w : w + size]
-        if size < 128:
-            block = jnp.concatenate([block, jnp.zeros((128, 128 - size), f32)], 1)
-        parts = split_three(jnp.transpose(block))
-        for i in range(3):
-            split_rows[i, w : w + size, 128:256] = parts[i][0:size].astype(bf16)
-
-    def lane_list(ref, rows, base):
-        count = ref.shape[1]
-        values = jnp.concatenate([(ref[...] - base).astype(f32), jnp.zeros((125, count), f32)], 0)
-        if count < 128:
-            values = jnp.concatenate([values, jnp.zeros((128, 128 - count), f32)], 1)
-        columns[...] = jnp.transpose(values)
-        parts = [
-            columns[pl.ds(rows[0] * a + rows[1] * b, 8, stride=rows[2]), :] for a in range(4) for b in range(4)
-        ]
-        return jnp.transpose(jnp.concatenate(parts, 0)).astype(jnp.int32)
-
-    source = lax.broadcasted_iota(jnp.int32, (256, 128), 0)
-    edge = source - 128
-    s1, s2, s3 = (source >> 5) & 3, (source >> 3) & 3, source & 7
-
-    def source_ids(level, own, own_count, count):
-        low = edge - 4 * level
-        high = edge - EDGE - 4 * level
-        ids = jnp.where(source < own_count, own, -1000)
-        ids = jnp.where((low >= 0) & (low < 4), low - 4, ids)
-        return jnp.where((high >= 0) & (high < 4), high + count, ids)
-
-    def place_of(level):
-        return lambda axis_id: payload[level, ROWS + axis_id * K : ROWS + (axis_id + 1) * K, :]
-
-    picked = lane_list(list3, (0, 0, 1), here * 8)
-    wanted = jnp.where(j2 == 0, picked[0:1], jnp.where(j2 == 1, picked[1:2], jnp.where(j2 == 2, picked[2:3], -5000)))
-    split_to(split_rows, slice(0, 128), payload[2])
-    gathered[...] = pick(split_rows, source_ids(2, s3, 8, 8) == wanted)
-    couple_picked(place_of(2), local.at[1], False, (8, 16))
     copies[0].wait()
+    local[1] = far[2]
     descend_from(6, local.at[0], local.at[1], True)
-
-    picked = lane_list(list2, (0, 1, 4), here * 32)
-    wanted = jnp.where(j1 == 0, picked[0:1], jnp.where(j1 == 1, picked[1:2], jnp.where(j1 == 2, picked[2:3], -5000)))
-    split_to(split_rows, slice(0, 128), payload[1])
-    gathered[...] = pick(split_rows, source_ids(1, s3 * 4 + s2, 32, 32) == wanted)
-    couple_picked(place_of(1), local.at[0], False)
-    fold(local.at[0], (32, 64))
+    local[0] = far[1]
     descend_from(5, local.at[1], local.at[0], True)
-
-    picked = lane_list(list1, (1, 4, 16), here * 128)
-    split_to(split_rows, slice(0, 128), payload[0])
-    ids = source_ids(0, s3 * 16 + s2 * 4 + s1, 128, 128)
-    for j in range(3):
-        gathered[...] = pick(split_rows, ids == picked[j : j + 1])
-        couple_picked(place_of(0), local.at[1], j > 0)
+    local[1] = far[0]
     descend_from(4, local.at[0], local.at[1], True)
     for j0 in range(4):
         descend_from(j0, local.at[1], leaf_local.at[j0], False)
@@ -646,7 +682,7 @@
 
 
 def downward_pass(
-    tops, et, payload, low_halo, high_halo, coef_top, prox_top, list1, list2, list3, basis, near_field
+    tops, et, far, coef_top, prox_top, basis, near_field
 ):
     vmem = pl.BlockSpec(memory_space=pltpu.VMEM)
     smem = pl.BlockSpec(memory_space=pltpu.SMEM)
@@ -656,10 +692,9 @@
     return pl.pallas_call(
         down_kernel,
         out_shape=jax.ShapeDtypeStruct((R, panels), f32),
-        in_specs=[smem, hbm] + [vmem] * 8 + [hbm] * 2,
+        in_specs=[smem, hbm] + [vmem] * 3 + [hbm] * 2,
         out_specs=vmem,
         scratch_shapes=[
-            pltpu.VMEM((3, WIDE, 256), bf16),
             pltpu.VMEM((3, ROWS, top_lanes), bf16),
             pltpu.VMEM((3, 3 * K, top_lanes), bf16),
             pltpu.VMEM((WIDE, 128), f32),
@@ -667,7 +702,6 @@
             pltpu.VMEM((2, ROWS, 128), f32),
             pltpu.VMEM((4, ROWS, 128), f32),
             pltpu.VMEM((panels // LEAF * R, 128), f32),
-            pltpu.VMEM((128, 128), f32),
             pltpu.VMEM((4 * K, 128), f32),
             pltpu.VMEM(et.shape, f32),
             pltpu.VMEM(basis.shape, f32),
@@ -680,8 +714,7 @@
         ),
         name="downward_pass",
     )(
-        tops, et, payload, low_halo, high_halo, coef_top, prox_top,
-        list1, list2, list3, basis, near_field,
+        tops, et, far, coef_top, prox_top, basis, near_field
     )
 
 
@@ -700,9 +733,11 @@
     high_halo = lax.ppermute(first, "gx", backward)
     coef_top = lax.psum(terms, "gx")
     near_field = near_potential(near.T, jitter, charge, low_leaves, high_leaves)
-    near_field, coef_top = lax.optimization_barrier((near_field, coef_top))
+    near_field, low_halo, high_halo = lax.optimization_barrier((near_field, low_halo, high_halo))
+    far = couplings(payload, low_halo, high_halo, list1.T, list2.T, list3.T)
+    far, coef_top = lax.optimization_barrier((far, coef_top))
     return downward_pass(
-        top_of, et, payload, low_halo, high_halo, coef_top, prox_top, list1.T, list2.T, list3.T, basis, near_field
+        top_of, et, far, coef_top, prox_top, basis, near_field
     )
 
 

time: 162 us -> 161 us (level)
    pallas_call x1, Pallas kernels: 27.9 us -> 19.1 us  [downward_pass(): pl.pallas_call(down_kernel, out_shape=jax.ShapeDtypeStruct((R, panels), f...]
    pallas_call x0 -> x1, Pallas kernels: none -> 8.76 us  [couplings(): pl.pallas_call(couple_kernel, out_shape=jax.ShapeDtypeStruct((3, ROWS, 12...]
  transfers between devices with their start and end apart: 5 -> 5, of which waited for: 0 -> 0; matrix products, arithmetic and copies ran while one was open for 0% -> 0% of each run, Pallas kernels for 64% -> 69%
where the time goes in v6:
time: 161 us; the launch traced here: 160 us
  Pallas kernels  130 us (81%)
  between operations  13.6 us (8%)
  starting transfers between devices  13.1 us (8%)
  local copies, waits for them, and re-layouts  3.92 us (2%)
    pallas_call x1, Pallas kernels, near_potential(): pl.pallas_call(near_kernel, out_shape=jax.ShapeDtypeStruct((R, panels), f...  79.3 us
    pallas_call x1, Pallas kernels, upward_pass(): pl.pallas_call(up_kernel, out_shape=[jax.ShapeDtypeStruct((7, K * K, 128)...  22.4 us
    pallas_call x1, Pallas kernels, downward_pass(): pl.pallas_call(down_kernel, out_shape=jax.ShapeDtypeStruct((R, panels), f...  19.1 us
    pallas_call x1, Pallas kernels, couplings(): pl.pallas_call(couple_kernel, out_shape=jax.ShapeDtypeStruct((3, ROWS, 12...  8.76 us
    ppermute x1, starting transfers between devices, body(): high_halo = lax.ppermute(first, 'gx', backward)  4.72 us
    ppermute x1, starting transfers between devices, leaf_halos(): lax.ppermute(first, 'gx', backward)  4.54 us
  transfers between devices with their start and end apart: 5, of which 0 were waited for; matrix products, arithmetic and copies ran while one was open for 0% of the time, Pallas kernels for 69%

profile of v6, /device:TPU:8, one launch (start us, length us, event | category | flops | bytes accessed | tf_op | source)
XLA Modules:
  0.0 160.2 jit_solution(17524883680470464281)
XLA Ops:
  6.5 0.0 all-reduce.2.cloned.1.call-start
  6.5 0.7 fusion.1
  7.3 0.9 fusion
  8.2 1.9 %collective-permute-start = (f32[19,1024]{1,0:T(8,128)S(1)}, f32[19,1024]{1,0:T(8,128)S(1)}, u32[]{:S(2)}, u32[]{:S(2)}) collective-permute-start(f32[19,1024]{1,0:T(8,128)S(1)} %pad_maximum_fusion), channel_id=1, source_target_pairs={{0,1},{1,2},{2,3},{3,4},{4,5},{5,6},{6,7},{7,8},{8,9},{9,10},{10,1... | collective-permute-start | bytes 233480 | tf_op jit(solution)/shard_map/ppermute | solution.py:26
  10.1 4.5 %collective-permute-start.1 = (f32[19,1024]{1,0:T(8,128)S(1)}, f32[19,1024]{1,0:T(8,128)S(1)}, u32[]{:S(2)}, u32[]{:S(2)}) collective-permute-start(f32[19,1024]{1,0:T(8,128)S(1)} %pad_maximum_fusion.1), channel_id=1, source_target_pairs={{1,0},{2,1},{3,2},{4,3},{5,4},{6,5},{7,6},{8,7},{9,8},{10,9},{11,1... | collective-permute-start | bytes 233480 | tf_op jit(solution)/shard_map/ppermute | solution.py:26
  14.7 0.0 copy-start.1
  14.7 0.0 copy-start.4
  14.7 0.0 copy-start.8
  14.7 22.4 %upward_pass.1 = (f32[7,1024,128]{2,1,0:T(8,128)}, f32[3,608,128]{2,1,0:T(8,128)}, f32[16,608]{1,0:T(8,128)}, f32[16,608]{1,0:T(8,128)}, f32[32,512]{1,0:T(8,128)}) custom-call(s32[128]{0:T(128)} %tops.3, f32[32,32768]{1,0:T(8,128)} %basis_hbm.3, f32[16,32768]{1,0:T(8,128)} %own_charge.1, f32[512,1024]{1,0:T(8,128)} %trans0_hbm.1, f32[128,1024]{1,0:T(8,128)} %trans1.1, ...), custom_call_target="tpu_custom_call" | custom-call | flops 102400000 | bytes 10240000 | tf_op jit(solution)/shard_map/upward_pass/pallas_call | solution.py:436
  37.1 0.0 all-reduce.2.cloned.1.call-update
  37.1 1.9 %collective-permute-start.2 = (f32[16,608]{1,0:T(8,128)}, f32[16,608]{1,0:T(8,128)S(1)}, u32[]{:S(2)}, u32[]{:S(2)}) collective-permute-start(f32[16,608]{1,0:T(8,128)} %get-tuple-element.17), channel_id=1, source_target_pairs={{0,1},{1,2},{2,3},{3,4},{4,5},{5,6},{6,7},{7,8},{8,9},{9,10},{10,1... | collective-permute-start | bytes 116744 | tf_op jit(solution)/shard_map/ppermute | solution.py:732
  39.1 4.7 %collective-permute-start.3 = (f32[16,608]{1,0:T(8,128)}, f32[16,608]{1,0:T(8,128)S(1)}, u32[]{:S(2)}, u32[]{:S(2)}) collective-permute-start(f32[16,608]{1,0:T(8,128)} %get-tuple-element.18), channel_id=1, source_target_pairs={{1,0},{2,1},{3,2},{4,3},{5,4},{6,5},{7,6},{8,7},{9,8},{10,9},{11,1... | collective-permute-start | bytes 116744 | tf_op jit(solution)/shard_map/ppermute | solution.py:733
  43.8 0.0 collective-permute-done.low_halo
  43.8 0.0 collective-permute-done.1.high_halo
  43.8 0.0 copy-done.1
  43.8 0.0 copy-done.4
  43.8 0.0 copy-done.8
  43.8 0.0 copy-start.3
  43.8 0.0 copy-start.5
  43.9 0.0 copy-start.6
  43.9 0.0 copy-start.7
  43.9 79.3 %near_potential.1.near_hbm = f32[16,32768]{1,0:T(8,128)S(1)} custom-call(s32[16,512]{1,0:T(8,128)S(1)} %bitcast.8, f32[3,32768]{1,0:T(4,128)S(1)} %copy-done.4, f32[16,32768]{1,0:T(8,128)S(1)} %copy-done.1, f32[19,1024]{1,0:T(8,128)S(1)} %collective-permute-done.low_halo, f32[19,1024]{1,0:T(8,128)S(1)} %collective-permute-done.1.high_halo), custom_call_target="tpu_custom_call" | custom-call | flops 6442450944 | bytes 5242880 | tf_op jit(solution)/shard_map/near_potential/pallas_call | solution.py:203
  123.2 0.0 copy-start.2
  123.2 1.4 copy-done.2
  124.6 0.0 collective-permute-done.2.low_halo
  124.6 0.0 collective-permute-done.3.high_halo
  124.6 0.0 copy-done.3
  124.6 0.0 copy-done.5
  124.6 0.0 copy-done.6
  124.6 0.0 copy-done.7
  124.6 8.8 %couplings.1.far = f32[3,512,128]{2,1,0:T(8,128)S(1)} custom-call(f32[3,608,128]{2,1,0:T(8,128)S(1)} %copy-done.3, f32[16,608]{1,0:T(8,128)S(1)} %collective-permute-done.2.low_halo, f32[16,608]{1,0:T(8,128)S(1)} %collective-permute-done.3.high_halo, s32[3,128]{1,0:T(4,128)S(1)} %bitcast.5, s32[3,32]{1,0:T(4,128)S(1)} %bitcast.6, s32[3,8]{1,0:T(4,128)S(1)} %bitcast.7), custom_call_target="tpu_custom_call" | custom-call | flops 20000000 | bytes 2000000 | tf_op jit(solution)/shard_map/couplings/pallas_call | solution.py:560
  133.4 0.0 copy-start
  133.4 0.9 copy-done
  134.3 0.0 all-reduce.2.cloned.1.call-done.coef_top
  134.3 19.1 %downward_pass.1 = f32[16,32768]{1,0:T(8,128)} custom-call(s32[128]{0:T(128)} %tops.3, f32[7,1024,128]{2,1,0:T(8,128)} %get-tuple-element.15.et_hbm, f32[3,512,128]{2,1,0:T(8,128)} %copy-done, f32[32,512]{1,0:T(8,128)} %all-reduce.2.cloned.1.call-done.coef_top, f32[32,96]{1,0:T(8,128)} %prox_top.1, f32[32,32768]{1,0:T(8,128)} %basis_hbm.3, f32[16,32768]{1,0:T(8,128)} %copy-done.2), custom_call_target="tpu_custom_call" | custom-call | flops 131072000 | bytes 13107200 | tf_op jit(solution)/shard_map/downward_pass/pallas_call | solution.py:692
  (2 shorter events, 0.0 us)
Async XLA Ops:
  6.5 127.7 %all-reduce.2.cloned.1.call-start = ((), (), s32[]{:S(2)}) async-start(), calls=%async_computation | async-start | bytes 131072 | tf_op jit(solution)/shard_map/psum | solution.py:734
  8.2 35.6 %collective-permute-start = (f32[19,1024]{1,0:T(8,128)S(1)}, f32[19,1024]{1,0:T(8,128)S(1)}, u32[]{:S(2)}, u32[]{:S(2)}) collective-permute-start(f32[19,1024]{1,0:T(8,128)S(1)} %pad_maximum_fusion), channel_id=1, source_target_pairs={{0,1},{1,2},{2,3},{3,4},{4,5},{5,6},{6,7},{7,8},{8,9},{9,10},{10,1... | collective-permute-start | bytes 233480 | tf_op jit(solution)/shard_map/ppermute | solution.py:26
  10.1 33.7 %collective-permute-start.1 = (f32[19,1024]{1,0:T(8,128)S(1)}, f32[19,1024]{1,0:T(8,128)S(1)}, u32[]{:S(2)}, u32[]{:S(2)}) collective-permute-start(f32[19,1024]{1,0:T(8,128)S(1)} %pad_maximum_fusion.1), channel_id=1, source_target_pairs={{1,0},{2,1},{3,2},{4,3},{5,4},{6,5},{7,6},{8,7},{9,8},{10,9},{11,1... | collective-permute-start | bytes 233480 | tf_op jit(solution)/shard_map/ppermute | solution.py:26
  14.7 29.1 %copy-start.1 = (f32[16,32768]{1,0:T(8,128)S(1)}, f32[16,32768]{1,0:T(8,128)}, u32[]{:S(2)}) copy-start(f32[16,32768]{1,0:T(8,128)} %own_charge.1) | copy-start | bytes 6291460
  14.7 29.1 %copy-start.4 = (f32[3,32768]{1,0:T(4,128)S(1)}, f32[3,32768]{1,0:T(4,128)}, u32[]{:S(2)}) copy-start(f32[3,32768]{1,0:T(4,128)} %own_jitter.1) | copy-start | bytes 1179652
  14.7 29.1 %copy-start.8 = (s32[512,16]{0,1:T(8,128)S(1)}, s32[512,16]{0,1:T(8,128)}, u32[]{:S(2)}) copy-start(s32[512,16]{0,1:T(8,128)} %param.19) | copy-start | bytes 98308
  37.1 87.5 %collective-permute-start.2 = (f32[16,608]{1,0:T(8,128)}, f32[16,608]{1,0:T(8,128)S(1)}, u32[]{:S(2)}, u32[]{:S(2)}) collective-permute-start(f32[16,608]{1,0:T(8,128)} %get-tuple-element.17), channel_id=1, source_target_pairs={{0,1},{1,2},{2,3},{3,4},{4,5},{5,6},{6,7},{7,8},{8,9},{9,10},{10,1... | collective-permute-start | bytes 116744 | tf_op jit(solution)/shard_map/ppermute | solution.py:732
  39.1 85.5 %collective-permute-start.3 = (f32[16,608]{1,0:T(8,128)}, f32[16,608]{1,0:T(8,128)S(1)}, u32[]{:S(2)}, u32[]{:S(2)}) collective-permute-start(f32[16,608]{1,0:T(8,128)} %get-tuple-element.18), channel_id=1, source_target_pairs={{1,0},{2,1},{3,2},{4,3},{5,4},{6,5},{7,6},{8,7},{9,8},{10,9},{11,1... | collective-permute-start | bytes 116744 | tf_op jit(solution)/shard_map/ppermute | solution.py:733
  43.8 80.8 %copy-start.3 = (f32[3,608,128]{2,1,0:T(8,128)S(1)}, f32[3,608,128]{2,1,0:T(8,128)}, u32[]{:S(2)}) copy-start(f32[3,608,128]{2,1,0:T(8,128)} %get-tuple-element.16.payload) | copy-start | bytes 2801668
  43.8 80.8 %copy-start.5 = (s32[128,3]{0,1:T(4,128)S(1)}, s32[128,3]{0,1:T(4,128)}, u32[]{:S(2)}) copy-start(s32[128,3]{0,1:T(4,128)} %param.28) | copy-start | bytes 4612
  43.9 80.7 %copy-start.6 = (s32[32,3]{0,1:T(4,128)S(1)}, s32[32,3]{0,1:T(4,128)}, u32[]{:S(2)}) copy-start(s32[32,3]{0,1:T(4,128)} %param.29) | copy-start | bytes 1156
  43.9 80.7 %copy-start.7 = (s32[8,3]{0,1:T(4,128)S(1)}, s32[8,3]{0,1:T(4,128)}, u32[]{:S(2)}) copy-start(s32[8,3]{0,1:T(4,128)} %param.30) | copy-start | bytes 292
  123.2 1.4 copy-start.2
  133.4 0.9 copy-start
Sparse Core Ops, SparseCore 0:
  37.2 87.3 all-reduce.1

commit v7 on v6

--- a/solution.py
+++ b/solution.py
@@ -94,7 +94,7 @@
 
     stage_halo(low_halo, 0)
     stage_halo(high_halo, halo_tiles + own_tiles)
-    lax.fori_loop(0, own_tiles, stage_own, 0, unroll=4)
+    lax.fori_loop(0, own_tiles, stage_own, 0, unroll=16)
 
     def back(slot):
         total = lax.dot_general(
@@ -187,8 +187,6 @@
             lax.fori_loop(0, GROUP // BATCH, step, 0)
         return carry
 
-    kernels[...] = jnp.zeros_like(kernels)
-    weights[...] = jnp.zeros_like(weights)
     fill(0, feats0, targets0, 0, 1)
     lax.fori_loop(0, group_count // 2, do_two_groups, 0)
     emit(own_tiles * 2 - BATCH)
@@ -343,7 +341,7 @@
             coef0[j0, place, :] = jnp.transpose(rows)[0:K]
         return carry
 
-    lax.fori_loop(0, R, leaf_coefs, 0, unroll=2)
+    lax.fori_loop(0, R, leaf_coefs, 0, unroll=4)
 
     def digits_first(q, rows):
         parts = [
@@ -481,7 +479,7 @@
         green_rows[pl.ds(pl.multiple_of(b * K, K), K), :] = inv_four_pi * lax.rsqrt(square + soft_square)
         return carry
 
-    lax.fori_loop(0, K, step, 0, unroll=4)
+    lax.fori_loop(0, K, step, 0, unroll=16)
     if shifts is None:
         matvec(lambda b: green_rows[b * K : (b + 1) * K, :], gathered, out_ref, add)
     else:

time: 161 us -> 157 us (0.975)
  Pallas kernels: 130 us -> 125 us
    pallas_call x1, Pallas kernels: 79.3 us -> 75.9 us  [near_potential(): pl.pallas_call(near_kernel, out_shape=jax.ShapeDtypeStruct((R, panels), f...]
  transfers between devices with their start and end apart: 5 -> 5, of which waited for: 0 -> 0; matrix products, arithmetic and copies ran while one was open for 0% -> 0% of each run, Pallas kernels for 69% -> 68%
where the time goes in v7:
time: 157 us; the launch traced here: 156 us
  Pallas kernels  125 us (80%)
  between operations  13.6 us (9%)
  starting transfers between devices  13.1 us (8%)
  local copies, waits for them, and re-layouts  3.92 us (2%)
    pallas_call x1, Pallas kernels, near_potential(): pl.pallas_call(near_kernel, out_shape=jax.ShapeDtypeStruct((R, panels), f...  75.9 us
    pallas_call x1, Pallas kernels, upward_pass(): pl.pallas_call(up_kernel, out_shape=[jax.ShapeDtypeStruct((7, K * K, 128)...  22.2 us
    pallas_call x1, Pallas kernels, downward_pass(): pl.pallas_call(down_kernel, out_shape=jax.ShapeDtypeStruct((R, panels), f...  18.9 us
    pallas_call x1, Pallas kernels, couplings(): pl.pallas_call(couple_kernel, out_shape=jax.ShapeDtypeStruct((3, ROWS, 12...  8.38 us
    ppermute x1, starting transfers between devices, body(): high_halo = lax.ppermute(first, 'gx', backward)  4.72 us
    ppermute x1, starting transfers between devices, leaf_halos(): lax.ppermute(first, 'gx', backward)  4.54 us
  transfers between devices with their start and end apart: 5, of which 0 were waited for; matrix products, arithmetic and copies ran while one was open for 0% of the time, Pallas kernels for 68%

profile of v7, /device:TPU:8, one launch (start us, length us, event | category | flops | bytes accessed | tf_op | source)
XLA Modules:
  0.0 156.2 jit_solution(9305075517446660677)
XLA Ops:
  6.5 0.0 all-reduce.2.cloned.1.call-start
  6.5 0.7 fusion.1
  7.3 0.9 fusion
  8.2 1.9 %collective-permute-start = (f32[19,1024]{1,0:T(8,128)S(1)}, f32[19,1024]{1,0:T(8,128)S(1)}, u32[]{:S(2)}, u32[]{:S(2)}) collective-permute-start(f32[19,1024]{1,0:T(8,128)S(1)} %pad_maximum_fusion), channel_id=1, source_target_pairs={{0,1},{1,2},{2,3},{3,4},{4,5},{5,6},{6,7},{7,8},{8,9},{9,10},{10,1... | collective-permute-start | bytes 233480 | tf_op jit(solution)/shard_map/ppermute | solution.py:26
  10.1 4.5 %collective-permute-start.1 = (f32[19,1024]{1,0:T(8,128)S(1)}, f32[19,1024]{1,0:T(8,128)S(1)}, u32[]{:S(2)}, u32[]{:S(2)}) collective-permute-start(f32[19,1024]{1,0:T(8,128)S(1)} %pad_maximum_fusion.1), channel_id=1, source_target_pairs={{1,0},{2,1},{3,2},{4,3},{5,4},{6,5},{7,6},{8,7},{9,8},{10,9},{11,1... | collective-permute-start | bytes 233480 | tf_op jit(solution)/shard_map/ppermute | solution.py:26
  14.7 0.0 copy-start.1
  14.7 0.0 copy-start.4
  14.7 0.0 copy-start.8
  14.7 22.2 %upward_pass.1 = (f32[7,1024,128]{2,1,0:T(8,128)}, f32[3,608,128]{2,1,0:T(8,128)}, f32[16,608]{1,0:T(8,128)}, f32[16,608]{1,0:T(8,128)}, f32[32,512]{1,0:T(8,128)}) custom-call(s32[128]{0:T(128)} %tops.3, f32[32,32768]{1,0:T(8,128)} %basis_hbm.3, f32[16,32768]{1,0:T(8,128)} %own_charge.1, f32[512,1024]{1,0:T(8,128)} %trans0_hbm.1, f32[128,1024]{1,0:T(8,128)} %trans1.1, ...), custom_call_target="tpu_custom_call" | custom-call | flops 102400000 | bytes 10240000 | tf_op jit(solution)/shard_map/upward_pass/pallas_call | solution.py:434
  36.9 0.0 all-reduce.2.cloned.1.call-update
  37.0 1.9 %collective-permute-start.2 = (f32[16,608]{1,0:T(8,128)}, f32[16,608]{1,0:T(8,128)S(1)}, u32[]{:S(2)}, u32[]{:S(2)}) collective-permute-start(f32[16,608]{1,0:T(8,128)} %get-tuple-element.17), channel_id=1, source_target_pairs={{0,1},{1,2},{2,3},{3,4},{4,5},{5,6},{6,7},{7,8},{8,9},{9,10},{10,1... | collective-permute-start | bytes 116744 | tf_op jit(solution)/shard_map/ppermute | solution.py:730
  38.9 4.7 %collective-permute-start.3 = (f32[16,608]{1,0:T(8,128)}, f32[16,608]{1,0:T(8,128)S(1)}, u32[]{:S(2)}, u32[]{:S(2)}) collective-permute-start(f32[16,608]{1,0:T(8,128)} %get-tuple-element.18), channel_id=1, source_target_pairs={{1,0},{2,1},{3,2},{4,3},{5,4},{6,5},{7,6},{8,7},{9,8},{10,9},{11,1... | collective-permute-start | bytes 116744 | tf_op jit(solution)/shard_map/ppermute | solution.py:731
  43.6 0.0 collective-permute-done.low_halo
  43.6 0.0 collective-permute-done.1.high_halo
  43.6 0.0 copy-done.1
  43.6 0.0 copy-done.4
  43.7 0.0 copy-done.8
  43.7 0.0 copy-start.3
  43.7 0.0 copy-start.5
  43.7 0.0 copy-start.6
  43.7 0.0 copy-start.7
  43.7 75.9 %near_potential.1.near_hbm = f32[16,32768]{1,0:T(8,128)S(1)} custom-call(s32[16,512]{1,0:T(8,128)S(1)} %bitcast.8, f32[3,32768]{1,0:T(4,128)S(1)} %copy-done.4, f32[16,32768]{1,0:T(8,128)S(1)} %copy-done.1, f32[19,1024]{1,0:T(8,128)S(1)} %collective-permute-done.low_halo, f32[19,1024]{1,0:T(8,128)S(1)} %collective-permute-done.1.high_halo), custom_call_target="tpu_custom_call" | custom-call | flops 6442450944 | bytes 5242880 | tf_op jit(solution)/shard_map/near_potential/pallas_call | solution.py:201
  119.7 0.0 copy-start.2
  119.7 1.4 copy-done.2
  121.0 0.0 collective-permute-done.2.low_halo
  121.0 0.0 collective-permute-done.3.high_halo
  121.0 0.0 copy-done.3
  121.0 0.0 copy-done.5
  121.0 0.0 copy-done.6
  121.1 0.0 copy-done.7
  121.1 8.4 %couplings.1.far = f32[3,512,128]{2,1,0:T(8,128)S(1)} custom-call(f32[3,608,128]{2,1,0:T(8,128)S(1)} %copy-done.3, f32[16,608]{1,0:T(8,128)S(1)} %collective-permute-done.2.low_halo, f32[16,608]{1,0:T(8,128)S(1)} %collective-permute-done.3.high_halo, s32[3,128]{1,0:T(4,128)S(1)} %bitcast.5, s32[3,32]{1,0:T(4,128)S(1)} %bitcast.6, s32[3,8]{1,0:T(4,128)S(1)} %bitcast.7), custom_call_target="tpu_custom_call" | custom-call | flops 20000000 | bytes 2000000 | tf_op jit(solution)/shard_map/couplings/pallas_call | solution.py:558
  129.4 0.0 copy-start
  129.5 0.9 copy-done
  130.3 0.0 all-reduce.2.cloned.1.call-done.coef_top
  130.3 18.9 %downward_pass.1 = f32[16,32768]{1,0:T(8,128)} custom-call(s32[128]{0:T(128)} %tops.3, f32[7,1024,128]{2,1,0:T(8,128)} %get-tuple-element.15.et_hbm, f32[3,512,128]{2,1,0:T(8,128)} %copy-done, f32[32,512]{1,0:T(8,128)} %all-reduce.2.cloned.1.call-done.coef_top, f32[32,96]{1,0:T(8,128)} %prox_top.1, f32[32,32768]{1,0:T(8,128)} %basis_hbm.3, f32[16,32768]{1,0:T(8,128)} %copy-done.2), custom_call_target="tpu_custom_call" | custom-call | flops 131072000 | bytes 13107200 | tf_op jit(solution)/shard_map/downward_pass/pallas_call | solution.py:690
  (2 shorter events, 0.0 us)
Async XLA Ops:
  6.5 123.8 %all-reduce.2.cloned.1.call-start = ((), (), s32[]{:S(2)}) async-start(), calls=%async_computation | async-start | bytes 131072 | tf_op jit(solution)/shard_map/psum | solution.py:732
  8.2 35.4 %collective-permute-start = (f32[19,1024]{1,0:T(8,128)S(1)}, f32[19,1024]{1,0:T(8,128)S(1)}, u32[]{:S(2)}, u32[]{:S(2)}) collective-permute-start(f32[19,1024]{1,0:T(8,128)S(1)} %pad_maximum_fusion), channel_id=1, source_target_pairs={{0,1},{1,2},{2,3},{3,4},{4,5},{5,6},{6,7},{7,8},{8,9},{9,10},{10,1... | collective-permute-start | bytes 233480 | tf_op jit(solution)/shard_map/ppermute | solution.py:26
  10.1 33.5 %collective-permute-start.1 = (f32[19,1024]{1,0:T(8,128)S(1)}, f32[19,1024]{1,0:T(8,128)S(1)}, u32[]{:S(2)}, u32[]{:S(2)}) collective-permute-start(f32[19,1024]{1,0:T(8,128)S(1)} %pad_maximum_fusion.1), channel_id=1, source_target_pairs={{1,0},{2,1},{3,2},{4,3},{5,4},{6,5},{7,6},{8,7},{9,8},{10,9},{11,1... | collective-permute-start | bytes 233480 | tf_op jit(solution)/shard_map/ppermute | solution.py:26
  14.7 29.0 %copy-start.1 = (f32[16,32768]{1,0:T(8,128)S(1)}, f32[16,32768]{1,0:T(8,128)}, u32[]{:S(2)}) copy-start(f32[16,32768]{1,0:T(8,128)} %own_charge.1) | copy-start | bytes 6291460
  14.7 29.0 %copy-start.4 = (f32[3,32768]{1,0:T(4,128)S(1)}, f32[3,32768]{1,0:T(4,128)}, u32[]{:S(2)}) copy-start(f32[3,32768]{1,0:T(4,128)} %own_jitter.1) | copy-start | bytes 1179652
  14.7 29.0 %copy-start.8 = (s32[512,16]{0,1:T(8,128)S(1)}, s32[512,16]{0,1:T(8,128)}, u32[]{:S(2)}) copy-start(s32[512,16]{0,1:T(8,128)} %param.19) | copy-start | bytes 98308
  37.0 84.1 %collective-permute-start.2 = (f32[16,608]{1,0:T(8,128)}, f32[16,608]{1,0:T(8,128)S(1)}, u32[]{:S(2)}, u32[]{:S(2)}) collective-permute-start(f32[16,608]{1,0:T(8,128)} %get-tuple-element.17), channel_id=1, source_target_pairs={{0,1},{1,2},{2,3},{3,4},{4,5},{5,6},{6,7},{7,8},{8,9},{9,10},{10,1... | collective-permute-start | bytes 116744 | tf_op jit(solution)/shard_map/ppermute | solution.py:730
  38.9 82.1 %collective-permute-start.3 = (f32[16,608]{1,0:T(8,128)}, f32[16,608]{1,0:T(8,128)S(1)}, u32[]{:S(2)}, u32[]{:S(2)}) collective-permute-start(f32[16,608]{1,0:T(8,128)} %get-tuple-element.18), channel_id=1, source_target_pairs={{1,0},{2,1},{3,2},{4,3},{5,4},{6,5},{7,6},{8,7},{9,8},{10,9},{11,1... | collective-permute-start | bytes 116744 | tf_op jit(solution)/shard_map/ppermute | solution.py:731
  43.7 77.4 %copy-start.3 = (f32[3,608,128]{2,1,0:T(8,128)S(1)}, f32[3,608,128]{2,1,0:T(8,128)}, u32[]{:S(2)}) copy-start(f32[3,608,128]{2,1,0:T(8,128)} %get-tuple-element.16.payload) | copy-start | bytes 2801668
  43.7 77.4 %copy-start.5 = (s32[128,3]{0,1:T(4,128)S(1)}, s32[128,3]{0,1:T(4,128)}, u32[]{:S(2)}) copy-start(s32[128,3]{0,1:T(4,128)} %param.28) | copy-start | bytes 4612
  43.7 77.4 %copy-start.6 = (s32[32,3]{0,1:T(4,128)S(1)}, s32[32,3]{0,1:T(4,128)}, u32[]{:S(2)}) copy-start(s32[32,3]{0,1:T(4,128)} %param.29) | copy-start | bytes 1156
  43.7 77.3 %copy-start.7 = (s32[8,3]{0,1:T(4,128)S(1)}, s32[8,3]{0,1:T(4,128)}, u32[]{:S(2)}) copy-start(s32[8,3]{0,1:T(4,128)} %param.30) | copy-start | bytes 292
  119.7 1.4 copy-start.2
  129.4 0.9 copy-start
Sparse Core Ops, SparseCore 0:
  37.1 87.3 all-reduce.1

commit v8 on v7

--- a/solution.py
+++ b/solution.py
@@ -296,7 +296,7 @@
 
 def up_kernel(
     tops, basis_hbm, charge_hbm, trans0_hbm, trans1, trans2, trans3, prox1, prox2, prox3,
-    et, payload, last_out, first_out, terms, leaf_rows, coef0, coef, flipped, columns, by_column, packed, basis, charge, trans0, sems,
+    et_hbm, payload, last_out, first_out, terms, leaf_rows, coef0, coef, flipped, columns, by_column, packed, basis, charge, trans0, et, sems,
 ):
     here = lax.axis_index("gx")
     quarter = lax.broadcasted_iota(jnp.int32, (R, 256), 1).astype(f32)
@@ -362,15 +362,17 @@
     flip(trans1, [(4, (1, 4, 0, 16))])
     flip(trans2, [(5, (0, 1, 0, 4))])
     flip(trans3, [(6, (0, 0, 0, 1))])
+    give = pltpu.make_async_copy(et, et_hbm, sems.at[2 * CHUNKS + 1])
+    give.start()
 
     def lift_from(entry, vector, out, add):
-        for b in range(K):
-            by_column[b * K : (b + 1) * K, :] = et[entry, pl.ds(b, K, stride=K), :]
         if entry < 5:
+            for b in range(K):
+                by_column[b * K : (b + 1) * K, :] = et[entry, pl.ds(b, K, stride=K), :]
             matvec(lambda b: by_column[b * K : (b + 1) * K, :], vector, out, add)
         else:
             shifts = (8, 16) if entry == 5 else ()
-            matvec_packed(lambda b: by_column[b * K : (b + 1) * K, :], vector, packed, out, add, shifts)
+            matvec_packed(lambda b: et[entry, pl.ds(b, K, stride=K), :], vector, packed, out, add, shifts)
 
     for j0 in range(4):
         lift_from(j0, coef0.at[j0], coef.at[0], j0 > 0)
@@ -426,6 +428,7 @@
     for c in range(8):
         total = total + jnp.where(top_ids == tops[here * 8 + c], flipped[c : c + 1, 0:ROWS], 0.0)
     terms[...] = total
+    give.wait()
 
 
 def upward_pass(tops, basis, charge, trans0, trans1, trans2, trans3, prox1, prox2, prox3, top_count):
@@ -441,7 +444,7 @@
             jax.ShapeDtypeStruct((top_count, ROWS), f32),
         ],
         in_specs=[pl.BlockSpec(memory_space=pltpu.SMEM)] + [pl.BlockSpec(memory_space=pltpu.HBM)] * 3 + [vmem] * 6,
-        out_specs=[vmem] * 5,
+        out_specs=[pl.BlockSpec(memory_space=pltpu.HBM)] + [vmem] * 4,
         scratch_shapes=[
             pltpu.VMEM((leaves * R, 128), f32),
             pltpu.VMEM((4, ROWS, 128), f32),
@@ -453,7 +456,8 @@
             pltpu.VMEM(basis.shape, f32),
             pltpu.VMEM(charge.shape, f32),
             pltpu.VMEM(trans0.shape, f32),
-            pltpu.SemaphoreType.DMA((2 * CHUNKS + 1,)),
+            pltpu.VMEM((7, K * K, 128), f32),
+            pltpu.SemaphoreType.DMA((2 * CHUNKS + 2,)),
         ],
         compiler_params=pltpu.CompilerParams(vmem_limit_bytes=54 * 2**20),
         cost_estimate=pl.CostEstimate(

time: 157 us -> 157 us (level)
  no operation moved by 1% of the time
where the time goes in v8:
time: 157 us; the launch traced here: 156 us
  Pallas kernels  126 us (80%)
  between operations  13.6 us (9%)
  starting transfers between devices  13.1 us (8%)
  local copies, waits for them, and re-layouts  3.92 us (2%)
    pallas_call x1, Pallas kernels, near_potential(): pl.pallas_call(near_kernel, out_shape=jax.ShapeDtypeStruct((R, panels), f...  75.9 us
    pallas_call x1, Pallas kernels, upward_pass(): pl.pallas_call(up_kernel, out_shape=[jax.ShapeDtypeStruct((7, K * K, 128)...  22.4 us
    pallas_call x1, Pallas kernels, downward_pass(): pl.pallas_call(down_kernel, out_shape=jax.ShapeDtypeStruct((R, panels), f...  18.9 us
    pallas_call x1, Pallas kernels, couplings(): pl.pallas_call(couple_kernel, out_shape=jax.ShapeDtypeStruct((3, ROWS, 12...  8.38 us
    ppermute x1, starting transfers between devices, body(): high_halo = lax.ppermute(first, 'gx', backward)  4.72 us
    ppermute x1, starting transfers between devices, leaf_halos(): lax.ppermute(first, 'gx', backward)  4.54 us
  transfers between devices with their start and end apart: 5, of which 0 were waited for; matrix products, arithmetic and copies ran while one was open for 0% of the time, Pallas kernels for 68%

profile of v8, /device:TPU:8, one launch (start us, length us, event | category | flops | bytes accessed | tf_op | source)
XLA Modules:
  0.0 156.3 jit_solution(10576987759791085143)
XLA Ops:
  6.5 0.0 all-reduce.2.cloned.1.call-start
  6.5 0.7 fusion.1
  7.3 0.9 fusion
  8.2 1.9 %collective-permute-start = (f32[19,1024]{1,0:T(8,128)S(1)}, f32[19,1024]{1,0:T(8,128)S(1)}, u32[]{:S(2)}, u32[]{:S(2)}) collective-permute-start(f32[19,1024]{1,0:T(8,128)S(1)} %pad_maximum_fusion), channel_id=1, source_target_pairs={{0,1},{1,2},{2,3},{3,4},{4,5},{5,6},{6,7},{7,8},{8,9},{9,10},{10,1... | collective-permute-start | bytes 233480 | tf_op jit(solution)/shard_map/ppermute | solution.py:26
  10.1 4.5 %collective-permute-start.1 = (f32[19,1024]{1,0:T(8,128)S(1)}, f32[19,1024]{1,0:T(8,128)S(1)}, u32[]{:S(2)}, u32[]{:S(2)}) collective-permute-start(f32[19,1024]{1,0:T(8,128)S(1)} %pad_maximum_fusion.1), channel_id=1, source_target_pairs={{1,0},{2,1},{3,2},{4,3},{5,4},{6,5},{7,6},{8,7},{9,8},{10,9},{11,1... | collective-permute-start | bytes 233480 | tf_op jit(solution)/shard_map/ppermute | solution.py:26
  14.7 0.0 copy-start.1
  14.7 0.0 copy-start.4
  14.7 0.0 copy-start.8
  14.7 22.4 %upward_pass.1 = (f32[7,1024,128]{2,1,0:T(8,128)}, f32[3,608,128]{2,1,0:T(8,128)}, f32[16,608]{1,0:T(8,128)}, f32[16,608]{1,0:T(8,128)}, f32[32,512]{1,0:T(8,128)}) custom-call(s32[128]{0:T(128)} %tops.3, f32[32,32768]{1,0:T(8,128)} %basis_hbm.3, f32[16,32768]{1,0:T(8,128)} %own_charge.1, f32[512,1024]{1,0:T(8,128)} %trans0_hbm.1, f32[128,1024]{1,0:T(8,128)} %trans1.1, ...), custom_call_target="tpu_custom_call" | custom-call | flops 102400000 | bytes 10240000 | tf_op jit(solution)/shard_map/upward_pass/pallas_call | solution.py:437
  37.2 0.0 all-reduce.2.cloned.1.call-update
  37.2 1.9 %collective-permute-start.2 = (f32[16,608]{1,0:T(8,128)}, f32[16,608]{1,0:T(8,128)S(1)}, u32[]{:S(2)}, u32[]{:S(2)}) collective-permute-start(f32[16,608]{1,0:T(8,128)} %get-tuple-element.17), channel_id=1, source_target_pairs={{0,1},{1,2},{2,3},{3,4},{4,5},{5,6},{6,7},{7,8},{8,9},{9,10},{10,1... | collective-permute-start | bytes 116744 | tf_op jit(solution)/shard_map/ppermute | solution.py:734
  39.1 4.7 %collective-permute-start.3 = (f32[16,608]{1,0:T(8,128)}, f32[16,608]{1,0:T(8,128)S(1)}, u32[]{:S(2)}, u32[]{:S(2)}) collective-permute-start(f32[16,608]{1,0:T(8,128)} %get-tuple-element.18), channel_id=1, source_target_pairs={{1,0},{2,1},{3,2},{4,3},{5,4},{6,5},{7,6},{8,7},{9,8},{10,9},{11,1... | collective-permute-start | bytes 116744 | tf_op jit(solution)/shard_map/ppermute | solution.py:735
  43.8 0.0 collective-permute-done.low_halo
  43.8 0.0 collective-permute-done.1.high_halo
  43.9 0.0 copy-done.1
  43.9 0.0 copy-done.4
  43.9 0.0 copy-done.8
  43.9 0.0 copy-start.3
  43.9 0.0 copy-start.5
  43.9 0.0 copy-start.6
  43.9 0.0 copy-start.7
  43.9 75.9 %near_potential.1.near_hbm = f32[16,32768]{1,0:T(8,128)S(1)} custom-call(s32[16,512]{1,0:T(8,128)S(1)} %bitcast.8, f32[3,32768]{1,0:T(4,128)S(1)} %copy-done.4, f32[16,32768]{1,0:T(8,128)S(1)} %copy-done.1, f32[19,1024]{1,0:T(8,128)S(1)} %collective-permute-done.low_halo, f32[19,1024]{1,0:T(8,128)S(1)} %collective-permute-done.1.high_halo), custom_call_target="tpu_custom_call" | custom-call | flops 6442450944 | bytes 5242880 | tf_op jit(solution)/shard_map/near_potential/pallas_call | solution.py:201
  119.8 0.0 copy-start.2
  119.8 1.4 copy-done.2
  121.2 0.0 collective-permute-done.2.low_halo
  121.2 0.0 collective-permute-done.3.high_halo
  121.2 0.0 copy-done.3
  121.2 0.0 copy-done.5
  121.2 0.0 copy-done.6
  121.2 0.0 copy-done.7
  121.2 8.4 %couplings.1.far = f32[3,512,128]{2,1,0:T(8,128)S(1)} custom-call(f32[3,608,128]{2,1,0:T(8,128)S(1)} %copy-done.3, f32[16,608]{1,0:T(8,128)S(1)} %collective-permute-done.2.low_halo, f32[16,608]{1,0:T(8,128)S(1)} %collective-permute-done.3.high_halo, s32[3,128]{1,0:T(4,128)S(1)} %bitcast.5, s32[3,32]{1,0:T(4,128)S(1)} %bitcast.6, s32[3,8]{1,0:T(4,128)S(1)} %bitcast.7), custom_call_target="tpu_custom_call" | custom-call | flops 20000000 | bytes 2000000 | tf_op jit(solution)/shard_map/couplings/pallas_call | solution.py:562
  129.6 0.0 copy-start
  129.6 0.9 copy-done
  130.5 0.0 all-reduce.2.cloned.1.call-done.coef_top
  130.5 18.9 %downward_pass.1 = f32[16,32768]{1,0:T(8,128)} custom-call(s32[128]{0:T(128)} %tops.3, f32[7,1024,128]{2,1,0:T(8,128)} %get-tuple-element.15.et_hbm, f32[3,512,128]{2,1,0:T(8,128)} %copy-done, f32[32,512]{1,0:T(8,128)} %all-reduce.2.cloned.1.call-done.coef_top, f32[32,96]{1,0:T(8,128)} %prox_top.1, f32[32,32768]{1,0:T(8,128)} %basis_hbm.3, f32[16,32768]{1,0:T(8,128)} %copy-done.2), custom_call_target="tpu_custom_call" | custom-call | flops 131072000 | bytes 13107200 | tf_op jit(solution)/shard_map/downward_pass/pallas_call | solution.py:694
  (2 shorter events, 0.0 us)
Async XLA Ops:
  6.5 124.0 %all-reduce.2.cloned.1.call-start = ((), (), s32[]{:S(2)}) async-start(), calls=%async_computation | async-start | bytes 131072 | tf_op jit(solution)/shard_map/psum | solution.py:736
  8.2 35.7 %collective-permute-start = (f32[19,1024]{1,0:T(8,128)S(1)}, f32[19,1024]{1,0:T(8,128)S(1)}, u32[]{:S(2)}, u32[]{:S(2)}) collective-permute-start(f32[19,1024]{1,0:T(8,128)S(1)} %pad_maximum_fusion), channel_id=1, source_target_pairs={{0,1},{1,2},{2,3},{3,4},{4,5},{5,6},{6,7},{7,8},{8,9},{9,10},{10,1... | collective-permute-start | bytes 233480 | tf_op jit(solution)/shard_map/ppermute | solution.py:26
  10.1 33.7 %collective-permute-start.1 = (f32[19,1024]{1,0:T(8,128)S(1)}, f32[19,1024]{1,0:T(8,128)S(1)}, u32[]{:S(2)}, u32[]{:S(2)}) collective-permute-start(f32[19,1024]{1,0:T(8,128)S(1)} %pad_maximum_fusion.1), channel_id=1, source_target_pairs={{1,0},{2,1},{3,2},{4,3},{5,4},{6,5},{7,6},{8,7},{9,8},{10,9},{11,1... | collective-permute-start | bytes 233480 | tf_op jit(solution)/shard_map/ppermute | solution.py:26
  14.7 29.2 %copy-start.1 = (f32[16,32768]{1,0:T(8,128)S(1)}, f32[16,32768]{1,0:T(8,128)}, u32[]{:S(2)}) copy-start(f32[16,32768]{1,0:T(8,128)} %own_charge.1) | copy-start | bytes 6291460
  14.7 29.2 %copy-start.4 = (f32[3,32768]{1,0:T(4,128)S(1)}, f32[3,32768]{1,0:T(4,128)}, u32[]{:S(2)}) copy-start(f32[3,32768]{1,0:T(4,128)} %own_jitter.1) | copy-start | bytes 1179652
  14.7 29.2 %copy-start.8 = (s32[512,16]{0,1:T(8,128)S(1)}, s32[512,16]{0,1:T(8,128)}, u32[]{:S(2)}) copy-start(s32[512,16]{0,1:T(8,128)} %param.19) | copy-start | bytes 98308
  37.2 84.0 %collective-permute-start.2 = (f32[16,608]{1,0:T(8,128)}, f32[16,608]{1,0:T(8,128)S(1)}, u32[]{:S(2)}, u32[]{:S(2)}) collective-permute-start(f32[16,608]{1,0:T(8,128)} %get-tuple-element.17), channel_id=1, source_target_pairs={{0,1},{1,2},{2,3},{3,4},{4,5},{5,6},{6,7},{7,8},{8,9},{9,10},{10,1... | collective-permute-start | bytes 116744 | tf_op jit(solution)/shard_map/ppermute | solution.py:734
  39.1 82.1 %collective-permute-start.3 = (f32[16,608]{1,0:T(8,128)}, f32[16,608]{1,0:T(8,128)S(1)}, u32[]{:S(2)}, u32[]{:S(2)}) collective-permute-start(f32[16,608]{1,0:T(8,128)} %get-tuple-element.18), channel_id=1, source_target_pairs={{1,0},{2,1},{3,2},{4,3},{5,4},{6,5},{7,6},{8,7},{9,8},{10,9},{11,1... | collective-permute-start | bytes 116744 | tf_op jit(solution)/shard_map/ppermute | solution.py:735
  43.9 77.3 %copy-start.3 = (f32[3,608,128]{2,1,0:T(8,128)S(1)}, f32[3,608,128]{2,1,0:T(8,128)}, u32[]{:S(2)}) copy-start(f32[3,608,128]{2,1,0:T(8,128)} %get-tuple-element.16.payload) | copy-start | bytes 2801668
  43.9 77.3 %copy-start.5 = (s32[128,3]{0,1:T(4,128)S(1)}, s32[128,3]{0,1:T(4,128)}, u32[]{:S(2)}) copy-start(s32[128,3]{0,1:T(4,128)} %param.28) | copy-start | bytes 4612
  43.9 77.3 %copy-start.6 = (s32[32,3]{0,1:T(4,128)S(1)}, s32[32,3]{0,1:T(4,128)}, u32[]{:S(2)}) copy-start(s32[32,3]{0,1:T(4,128)} %param.29) | copy-start | bytes 1156
  43.9 77.3 %copy-start.7 = (s32[8,3]{0,1:T(4,128)S(1)}, s32[8,3]{0,1:T(4,128)}, u32[]{:S(2)}) copy-start(s32[8,3]{0,1:T(4,128)} %param.30) | copy-start | bytes 292
  119.8 1.4 copy-start.2
  129.6 0.9 copy-start
Sparse Core Ops, SparseCore 0:
  37.3 87.3 all-reduce.1
